TPU v7x, 512 devices: a whole 4x4x16 slice. The times are simulated.
512 devices in a mesh: segment: 8 (over y, core), expert: 64 (over x, z).
Axes of the slice: x: 4, y: 4, z: 16, core: 2. Of those that a mesh axis runs over, the one named last changes fastest.
Arguments:
- hidden: bfloat16 [8, 2048, 2048], P('segment', 'expert'), may hold values from -6 to 6
- memory: bfloat16 [8, 2048, 2048], P('segment', 'expert'), may hold values from -6 to 6
- lengths: int32 [8, 64], P('segment', 'expert'), may hold values from 1 to 32, as said below
- memory_lengths: int32 [8, 64], P('segment', 'expert'), may hold values from 1 to 32, as said below
- routes: int32 [8, 2048, 2], P('segment', 'expert'), may hold values from 0 to 3, all different within a row; in each aligned block of 32 rows (0 to 31, 32 to 63, ..., all dimensions but the last counted through in order) at most 20 rows name the same one
- norm_gain: float32 [8, 3, 2048], P('segment'), may hold values from 0.5 to 1.5, as said below
- router: bfloat16 [8, 2048, 4], P('segment'), may hold values from -0.26516504 to 0.26516504, as said below
- w_in: bfloat16 [8, 2048, 16384], P('segment', None, 'expert'), may hold values from -0.13258252 to 0.13258252, as said below
- w_out: bfloat16 [8, 16384, 2048], P('segment', 'expert'), may hold values from -0.125 to 0.125, as said below
- shortlist: bfloat16 [8, 2048, 512], P('segment'), may hold values from -0.375 to 0.375
- student: float32 [8, 2048, 512], P('segment', 'expert'), may hold values from -15 to 15
- targets: int32 [8, 2048], P('segment', 'expert'), may hold values from 0 to 511
Outputs:
- layer_out: bfloat16 [8, 2048, 2048], P('segment', 'expert')
- loss: float32 [], replicated
Inputs may be any that keep to these rules, and one draw needn't show every extreme that they name: `lengths`: every sequence has at least one position; the first sequence of each section has 32. `memory_lengths`: every sequence has at least one position; the first sequence of each section has 32. `routes`: A token's two experts differ. In the 32 rows of one device no expert is named more than 20 times, a bound that some block reaches. `norm_gain`: equal in all encoder sections, and equal in all decoder sections. `router`: equal in all encoder sections, and equal in all decoder sections. `w_in`: equal in all encoder sections, and equal in all decoder sections. `w_out`: equal in all encoder sections, and equal in all decoder sections.
All inputs are finite; a program needn't handle non-finite values.
Results may differ from a plain program's by a relative error of at most 0.0049.
Values may be sent and summed in bfloat16 or wider, within the bound.
No kernel may reach another device: no remote copies, remote signals or barrier semaphores. Data moves between devices by JAX's collectives and lax.ppermute only.
A program may use at most 64 MiB of HBM per device.

v0:
```python
import math

import jax
import jax.numpy as jnp
from jax import lax
from jax.sharding import PartitionSpec as P

HEADS = 16
HEAD_DIM = 128
LEN = 32


epsilon = 1e-05


def passed_along(block, axis, distance):
    devices = range(lax.axis_size(axis))
    route = [(i - distance, i) for i in devices if i - distance in devices]
    return lax.ppermute(block, axis, route)


def layer_norm(values, gain_row):
    centred = values - jnp.mean(values, axis=-1, keepdims=True)
    spread = jnp.mean(centred * centred, axis=-1, keepdims=True)
    return centred * lax.rsqrt(spread + epsilon) * gain_row


def expert_rows(received, first_weight, second_weight):
    sources = received.shape[0]
    slot_count = received.shape[1]
    model_width = received.shape[2]
    flat_rows = received.reshape(sources * slot_count, model_width)
    activated = jnp.maximum(
        jnp.dot(flat_rows, first_weight, preferred_element_type=jnp.float32), 0.0
    ).astype(jnp.bfloat16)
    partial_out = jnp.dot(activated, second_weight, preferred_element_type=jnp.float32).astype(
        jnp.bfloat16
    )
    return partial_out.reshape(sources, slot_count, model_width)


def local(
    hidden,
    memory,
    lengths,
    memory_lengths,
    routes,
    norm_gain,
    router,
    w_in,
    w_out,
    shortlist,
    student,
    targets,
):
    segment_index = lax.axis_index("segment")
    half_segments = lax.axis_size("segment") // 2
    expert_count = lax.axis_size("expert")
    experts = router.shape[2]
    group_size = expert_count // experts
    tok_rows = hidden.shape[1]
    model_width = hidden.shape[2]
    capacity = 5 * tok_rows // 8
    decoder = segment_index >= half_segments
    positions = jnp.arange(tok_rows) % LEN
    seq_index = jnp.arange(tok_rows) // LEN
    is_valid = positions < lengths[0][seq_index]
    key_mask = (positions < memory_lengths[0][seq_index]).astype(jnp.bfloat16)
    arrived, arrived_mask = passed_along((memory[0], key_mask), "segment", half_segments)
    states = hidden[0].astype(jnp.float32)
    gain_rows = norm_gain[0]
    seq_count = tok_rows // LEN
    score_scale = 1.0 / math.sqrt(HEAD_DIM)
    queries = (
        layer_norm(states, gain_rows[0])
        .astype(jnp.bfloat16)
        .reshape(seq_count, LEN, HEADS, HEAD_DIM)
    )
    key_rows = arrived.reshape(seq_count, LEN, HEADS, HEAD_DIM)
    scores = (
        jnp.einsum("bqhd,bkhd->bhqk", queries, key_rows, preferred_element_type=jnp.float32)
        * score_scale
    )
    allowed = arrived_mask.reshape(seq_count, 1, 1, LEN) > 0.5
    scores = jnp.where(allowed, scores, -1e30)
    weights = jax.nn.softmax(scores, axis=-1).astype(jnp.bfloat16)
    attended = jnp.einsum(
        "bhqk,bkhd->bqhd", weights, key_rows, preferred_element_type=jnp.float32
    ).reshape(tok_rows, model_width)
    mid_states = states + jnp.where(decoder, attended, 0.0)
    normed = layer_norm(mid_states, gain_rows[1]).astype(jnp.bfloat16)
    router_probs = jax.nn.softmax(
        jnp.dot(normed, router[0], preferred_element_type=jnp.float32), axis=-1
    )
    expert_ids = jnp.arange(experts)
    first_hot = (routes[0][:, 0:1] == expert_ids).astype(jnp.float32)
    second = (routes[0][:, 1:2] == expert_ids).astype(jnp.float32)
    prob_first = jnp.sum(router_probs * first_hot, axis=-1, keepdims=True)
    prob_second = jnp.sum(router_probs * second, axis=-1, keepdims=True)
    prob_total = prob_first + prob_second
    gate_rows = (prob_first * first_hot + prob_second * second) / prob_total
    chosen = (first_hot + second) * is_valid[:, None].astype(jnp.float32)
    slot_rank = jnp.cumsum(chosen, axis=0) - 1.0
    slot_ids = jnp.arange(capacity).astype(jnp.float32)
    placing = chosen.T[:, None, :] * (slot_rank.T[:, None, :] == slot_ids[None, :, None]).astype(
        jnp.float32
    )
    buffer = jnp.einsum(
        "ect,td->ecd", placing.astype(jnp.bfloat16), normed, preferred_element_type=jnp.float32
    ).astype(jnp.bfloat16)
    outgoing = jnp.broadcast_to(
        buffer[:, None], (experts, group_size, capacity, model_width)
    ).reshape(expert_count, capacity, model_width)
    partial_out = expert_rows(
        lax.all_to_all(outgoing, "expert", split_axis=0, concat_axis=0, tiled=True),
        w_in[0],
        w_out[0],
    )
    returned = lax.all_to_all(partial_out, "expert", split_axis=0, concat_axis=0, tiled=True)
    summed = (
        returned.reshape(experts, group_size, capacity, model_width).astype(jnp.float32).sum(axis=1)
    )
    weighting = placing * gate_rows.T[:, None, :]
    moe_out = jnp.einsum("ect,ecd->td", weighting, summed, precision=lax.Precision.HIGHEST)
    layer_out = (mid_states + moe_out).astype(jnp.bfloat16)
    final_normed = layer_norm(layer_out.astype(jnp.float32), gain_rows[2]).astype(jnp.bfloat16)
    teacher = jax.nn.log_softmax(
        jnp.dot(final_normed, shortlist[0], preferred_element_type=jnp.float32), axis=-1
    )
    learner = jax.nn.log_softmax(student[0], axis=-1)
    picked = (targets[0][:, None] == jnp.arange(student.shape[2])).astype(jnp.float32)
    token_loss = jnp.sum(jnp.exp(teacher) * (teacher - learner), axis=-1) - jnp.sum(
        picked * learner, axis=-1
    )
    counted = jnp.where(decoder, is_valid.astype(jnp.float32), 0.0)
    loss_sum, loss_count = lax.psum(
        (jnp.sum(token_loss * counted), jnp.sum(counted)), ("segment", "expert")
    )
    return (layer_out[None], loss_sum / loss_count)


def solution(mesh):
    placed = (
        P("segment", "expert", None),
        P("segment", "expert", None),
        P("segment", "expert"),
        P("segment", "expert"),
        P("segment", "expert", None),
        P("segment", None, None),
        P("segment", None, None),
        P("segment", None, "expert"),
        P("segment", "expert", None),
        P("segment", None, None),
        P("segment", "expert", None),
        P("segment", "expert"),
    )
    return jax.shard_map(
        local,
        mesh=mesh,
        in_specs=placed,
        out_specs=(P("segment", "expert", None), P()),
        check_vma=False,
    )
```

profile of v0, /device:TPU:1, one launch (start us, length us, event | category | flops | bytes accessed | tf_op | source)
XLA Modules:
  0.0 739.3 jit_solution(8216992478677844114)
XLA Ops:
  0.7 5.8 collective-permute-start.1
  7.1 1.3 collective-permute-start
  8.4 1.0 convert_reduce_fusion.1
  9.4 0.9 convert_bitcast_fusion
  10.4 0.7 fusion.73
  11.1 1.1 fusion.21
  12.3 0.8 slice_bitcast_fusion.1
  13.8 0.3 fusion.74
  14.7 1.1 fusion.72
  15.8 1.1 multiply_reduce_fusion
  17.0 0.3 fusion.75
  17.5 0.3 convolution_convert_fusion.1
  17.9 0.8 broadcast_in_dim.26
  18.6 289.8 %all_to_all.10 = bf16[64,20,2048]{2,1,0:T(8,128)(2,1)} all-to-all(bf16[64,20,2048]{2,1,0:T(8,128)(2,1)S(1)} %bitcast.126), channel_id=1, replica_groups=mesh['segment'=8,'expert'=64] {'expert'}, dimensions={0} | all-to-all | bytes 10485760 | tf_op jit(solution)/shard_map/all_to_all | solution.py:115
  308.4 9.0 %reshape.327 = bf16[1280,2048]{1,0:T(8,128)(2,1)} reshape(bf16[64,20,2048]{2,1,0:T(8,128)(2,1)} %all_to_all.10) | data formatting | bytes 10485760 | tf_op jit(solution)/shard_map/reshape | solution.py:32
  317.4 10.8 %convolution_convert_fusion = bf16[1280,2048]{1,0:T(8,128)(2,1)} fusion(bf16[1280,2048]{1,0:T(8,128)(2,1)} %reshape.327, bf16[1,256,2048]{2,1,0:T(8,128)(2,1)} %param.21, bf16[1,2048,256]{2,1,0:T(8,128)(2,1)} %param.20), kind=kOutput, calls=%fused_computation.2 | convolution fusion | flops 2687631360 | bytes 12582912 | tf_op jit(solution)/shard_map/dot_general | solution.py:36
  328.3 8.9 %reshape.328 = bf16[64,20,2048]{2,1,0:T(8,128)(2,1)} reshape(bf16[1280,2048]{1,0:T(8,128)(2,1)} %convolution_convert_fusion) | data formatting | bytes 10485760 | tf_op jit(solution)/shard_map/reshape | solution.py:39
  337.2 14.2 %all-to-all-start.1 = ((bf16[64,20,2048]{2,1,0:T(8,128)(2,1)}), bf16[64,20,2048]{2,1,0:T(8,128)(2,1)}, u32[]{:S(2)}, u32[]{:S(2)}) async-start(bf16[64,20,2048]{2,1,0:T(8,128)(2,1)} %reshape.328), calls=%async_computation.1 | async-start | bytes 12582912 | tf_op jit(solution)/shard_map/all_to_all | solution.py:119
  351.7 273.1 %all-to-all-done.1 = bf16[64,20,2048]{2,1,0:T(8,128)(2,1)} async-done(((bf16[64,20,2048]{2,1,0:T(8,128)(2,1)}), bf16[64,20,2048]{2,1,0:T(8,128)(2,1)}, u32[]{:S(2)}, u32[]{:S(2)}) %all-to-all-start.1) | async-done | bytes 5242912 | tf_op jit(solution)/shard_map/all_to_all | solution.py:119
  624.8 4.2 convert_reduce_fusion
  628.9 0.7 convert_reduce_fusion.2
  629.9 0.6 fusion.76
  631.0 0.7 multiply_reduce_fusion.2
  631.6 105.2 %all-reduce = (f32[]{:T(128)}, f32[]{:T(128)}) all-reduce(f32[]{:T(128)} %get-tuple-element.25, f32[]{:T(128)} %get-tuple-element.26), channel_id=1, replica_groups=mesh['segment'=8,'expert'=64] {'segment','expert'}, use_global_device_ids=true, to_apply=%region_19.21 | all-reduce | flops 2 | bytes 16 | tf_op jit(solution)/shard_map/psum | solution.py:136
  (43 shorter events, 1.9 us)
Async XLA Ops:
  0.6 629.3 %copy-start = (bf16[1,2048,512]{2,1,0:T(8,128)(2,1)S(1)}, bf16[1,2048,512]{2,1,0:T(8,128)(2,1)}, u32[]{:S(2)}) copy-start(bf16[1,2048,512]{2,1,0:T(8,128)(2,1)} %param.22) | copy-start | bytes 6291460
  0.6 16.3 %copy-start.1 = (bf16[1,32,2048]{2,1,0:T(8,128)(2,1)S(1)}, bf16[1,32,2048]{2,1,0:T(8,128)(2,1)}, u32[]{:S(2)}) copy-start(bf16[1,32,2048]{2,1,0:T(8,128)(2,1)} %param.13) | copy-start | bytes 393220
  0.7 16.3 %copy-start.5 = (bf16[1,2048,4]{1,2,0:T(4,128)(2,1)S(1)}, bf16[1,2048,4]{1,2,0:T(4,128)(2,1)}, u32[]{:S(2)}) copy-start(bf16[1,2048,4]{1,2,0:T(4,128)(2,1)} %param.19) | copy-start | bytes 49156
  0.7 13.1 %collective-permute-start.1 = (bf16[32,2048]{1,0:T(8,128)(2,1)}, bf16[32,2048]{1,0:T(8,128)(2,1)S(1)}, u32[]{:S(2)}, u32[]{:S(2)}) collective-permute-start(bf16[32,2048]{1,0:T(8,128)(2,1)} %bitcast.140), channel_id=1, source_target_pairs={{0,256},{64,320},{128,384},{192,448},{1,257},{65,321},{129,385},{1... | collective-permute-start | bytes 393224 | tf_op jit(solution)/shard_map/ppermute | solution.py:19
  7.1 6.6 collective-permute-start
  337.2 14.2 %copy-start.3 = (f32[1,32,512]{2,1,0:T(8,128)S(1)}, f32[1,32,512]{2,1,0:T(8,128)}, u32[]{:S(2)}) copy-start(f32[1,32,512]{2,1,0:T(8,128)} %param.23) | copy-start | bytes 196612
  337.2 287.6 %all-to-all-start.1 = ((bf16[64,20,2048]{2,1,0:T(8,128)(2,1)}), bf16[64,20,2048]{2,1,0:T(8,128)(2,1)}, u32[]{:S(2)}, u32[]{:S(2)}) async-start(bf16[64,20,2048]{2,1,0:T(8,128)(2,1)} %reshape.328), calls=%async_computation.1 | async-start | bytes 12582912 | tf_op jit(solution)/shard_map/all_to_all | solution.py:119
  351.7 279.0 %copy-start.4 = (s32[1,32]{1,0:T(1,128)S(1)}, s32[1,32]{1,0:T(1,128)}, u32[]{:S(2)}) copy-start(s32[1,32]{1,0:T(1,128)} %param.24) | copy-start | bytes 388
  629.7 108.5 %copy-start.2 = (bf16[32,2048]{1,0:T(8,128)(2,1)}, bf16[32,2048]{1,0:T(8,128)(2,1)S(1)}, u32[]{:S(2)}) copy-start(bf16[32,2048]{1,0:T(8,128)(2,1)S(1)} %get-tuple-element.22) | copy-start | bytes 393220
where the time goes:
time: 740 us; the launch traced here: 739 us
  blocking collectives  395 us (53%)
  waiting for transfers between devices  273 us (37%)
  starting transfers between devices  21.3 us (3%)
  local copies, waits for them, and re-layouts  20.8 us (3%)
  matrix products  13.3 us (2%)
  other arithmetic  11.2 us (2%)
    all_to_all x1, blocking collectives, local(): lax.all_to_all(outgoing, 'expert', split_axis=0, concat_axis=0, tiled=True)  290 us
    all_to_all x1, waiting for transfers between devices, local(): lax.all_to_all(partial_out, 'expert', split_axis=0, concat_axis=0, tiled=...  273 us
    psum x1, blocking collectives, local(): lax.psum((jnp.sum(token_loss * counted), jnp.sum(counted)), ('segment', '...  105 us
  transfers between devices with their start and end apart: 3, of which 1 were waited for; matrix products, arithmetic and copies ran while one was open for 1% of the time, Pallas kernels for 0%

commit v1 on v0

v1 whole, which is shorter than its diff:
```python
import math

import jax
import jax.numpy as jnp
from jax import lax
from jax.sharding import Mesh, PartitionSpec as P

HEADS = 16
HEAD_DIM = 128
LEN = 32


epsilon = 1e-05


def passed_along(block, axis, distance):
    devices = range(lax.axis_size(axis))
    route = [(i - distance, i) for i in devices if i - distance in devices]
    return lax.ppermute(block, axis, route)


def layer_norm(values, gain_row):
    centred = values - jnp.mean(values, axis=-1, keepdims=True)
    spread = jnp.mean(centred * centred, axis=-1, keepdims=True)
    return centred * lax.rsqrt(spread + epsilon) * gain_row


def expert_rows(rows, first_weight, second_weight):
    activated = jnp.maximum(
        jnp.dot(rows, first_weight, preferred_element_type=jnp.float32), 0.0
    ).astype(jnp.bfloat16)
    return jnp.dot(activated, second_weight, preferred_element_type=jnp.float32).astype(
        jnp.bfloat16
    )


def local(
    hidden,
    memory,
    lengths,
    memory_lengths,
    routes,
    norm_gain,
    router,
    w_in,
    w_out,
    shortlist,
    student,
    targets,
):
    chips = lax.axis_size("y")
    experts = router.shape[2]
    tok_rows = hidden.shape[1]
    model_width = hidden.shape[2]
    capacity = 5 * tok_rows // 8
    decoder = lax.axis_index("y") >= chips // 2
    positions = jnp.arange(tok_rows) % LEN
    seq_index = jnp.arange(tok_rows) // LEN
    is_valid = positions < lengths[0][seq_index]
    key_mask = (positions < memory_lengths[0][seq_index]).astype(jnp.bfloat16)
    arrived, arrived_mask = passed_along((memory[0], key_mask), "y", chips // 2)
    states = hidden[0].astype(jnp.float32)
    gain_rows = norm_gain[0]
    seq_count = tok_rows // LEN
    score_scale = 1.0 / math.sqrt(HEAD_DIM)
    queries = (
        layer_norm(states, gain_rows[0])
        .astype(jnp.bfloat16)
        .reshape(seq_count, LEN, HEADS, HEAD_DIM)
    )
    key_rows = arrived.reshape(seq_count, LEN, HEADS, HEAD_DIM)
    scores = (
        jnp.einsum("bqhd,bkhd->bhqk", queries, key_rows, preferred_element_type=jnp.float32)
        * score_scale
    )
    allowed = arrived_mask.reshape(seq_count, 1, 1, LEN) > 0.5
    scores = jnp.where(allowed, scores, -1e30)
    weights = jax.nn.softmax(scores, axis=-1).astype(jnp.bfloat16)
    attended = jnp.einsum(
        "bhqk,bkhd->bqhd", weights, key_rows, preferred_element_type=jnp.float32
    ).reshape(tok_rows, model_width)
    mid_states = states + jnp.where(decoder, attended, 0.0)
    normed = layer_norm(mid_states, gain_rows[1]).astype(jnp.bfloat16)
    router_probs = jax.nn.softmax(
        jnp.dot(normed, router[0], preferred_element_type=jnp.float32), axis=-1
    )
    expert_ids = jnp.arange(experts)
    first_hot = (routes[0][:, 0:1] == expert_ids).astype(jnp.float32)
    second = (routes[0][:, 1:2] == expert_ids).astype(jnp.float32)
    prob_first = jnp.sum(router_probs * first_hot, axis=-1, keepdims=True)
    prob_second = jnp.sum(router_probs * second, axis=-1, keepdims=True)
    prob_total = prob_first + prob_second
    gate_rows = (prob_first * first_hot + prob_second * second) / prob_total
    chosen = (first_hot + second) * is_valid[:, None].astype(jnp.float32)
    upto = (jnp.arange(tok_rows)[:, None] >= jnp.arange(tok_rows)[None, :]).astype(jnp.float32)
    slot_rank = jnp.dot(upto, chosen, preferred_element_type=jnp.float32) - 1.0
    slot_ids = jnp.arange(capacity).astype(jnp.float32)
    placing = chosen.T[:, None, :] * (slot_rank.T[:, None, :] == slot_ids[None, :, None]).astype(
        jnp.float32
    )
    buffer = jnp.einsum(
        "ect,td->ecd", placing.astype(jnp.bfloat16), normed, preferred_element_type=jnp.float32
    ).astype(jnp.bfloat16)
    at_expert = lax.all_to_all(buffer, "x", split_axis=0, concat_axis=0, tiled=True)
    rows = lax.all_gather(
        at_expert.reshape(experts * capacity, model_width), "z", axis=0, tiled=True
    )
    partial_out = expert_rows(rows, w_in[0], w_out[0])
    expert_sum = lax.psum_scatter(partial_out, "z", scatter_dimension=0, tiled=True)
    summed = lax.all_to_all(
        expert_sum.reshape(experts, capacity, model_width), "x", split_axis=0, concat_axis=0, tiled=True
    ).astype(jnp.float32)
    weighting = placing * gate_rows.T[:, None, :]
    moe_out = jnp.einsum("ect,ecd->td", weighting, summed, precision=lax.Precision.HIGHEST)
    layer_out = (mid_states + moe_out).astype(jnp.bfloat16)
    final_normed = layer_norm(layer_out.astype(jnp.float32), gain_rows[2]).astype(jnp.bfloat16)
    teacher = jax.nn.log_softmax(
        jnp.dot(final_normed, shortlist[0], preferred_element_type=jnp.float32), axis=-1
    )
    learner = jax.nn.log_softmax(student[0], axis=-1)
    picked = (targets[0][:, None] == jnp.arange(student.shape[2])).astype(jnp.float32)
    token_loss = jnp.sum(jnp.exp(teacher) * (teacher - learner), axis=-1) - jnp.sum(
        picked * learner, axis=-1
    )
    counted = jnp.where(decoder, is_valid.astype(jnp.float32), 0.0)
    totals = jnp.stack([jnp.sum(token_loss * counted), jnp.sum(counted)])
    for axis in ("z", "x", "y", "core"):
        totals = lax.psum(totals, axis)
    return (layer_out[None], totals[0] / totals[1])


def solution(mesh):
    segments, expert_devices = mesh.devices.shape
    experts = 4
    fine = Mesh(
        mesh.devices.reshape(segments // 2, 2, experts, expert_devices // experts),
        ("y", "core", "x", "z"),
    )
    seg, exp = ("y", "core"), ("x", "z")
    placed = (
        P(seg, exp, None),
        P(seg, exp, None),
        P(seg, exp),
        P(seg, exp),
        P(seg, exp, None),
        P(seg, None, None),
        P(seg, None, None),
        P(seg, None, exp),
        P(seg, exp, None),
        P(seg, None, None),
        P(seg, exp, None),
        P(seg, exp),
    )
    return jax.shard_map(
        local,
        mesh=fine,
        in_specs=placed,
        out_specs=(P(seg, exp, None), P()),
        check_vma=False,
    )
```

time: 740 us -> 287 us (0.39)
  blocking collectives: 395 us -> 71.2 us
  waiting for transfers between devices: 273 us -> 159 us
  local copies, waits for them, and re-layouts: 20.8 us -> 5.08 us
  between operations: 4.65 us -> 18.1 us
  starting transfers between devices: 21.3 us -> 11.2 us
    all_to_all x1, blocking collectives: 290 us -> 10.4 us  [local(): lax.all_to_all(buffer, 'x', split_axis=0, concat_axis=0, tiled=True)]
    all_to_all x1, waiting for transfers between devices: 273 us -> 5.91 us  [local(): lax.all_to_all(expert_sum.reshape(experts, capacity, model_width), 'x', s...]
    all_gather x0 -> x1, waiting for transfers between devices: none -> 76.6 us  [local(): lax.all_gather(at_expert.reshape(experts * capacity, model_width), 'z', a...]
    reduce_scatter x0 -> x1, waiting for transfers between devices: none -> 76.6 us  [local(): lax.psum_scatter(partial_out, 'z', scatter_dimension=0, tiled=True)]
    psum x1 -> x4, blocking collectives: 105 us -> 60.9 us  [local(): totals = lax.psum(totals, axis)]
    reshape x2, local copies, waits for them, and re-layouts: 17.9 us -> 2.57 us  [the longest x1 1.78 us: local(): expert_sum.reshape(experts, capacity, model_width)]
    all_to_all x1, starting transfers between devices: 14.2 us -> 4.04 us  [local(): lax.all_to_all(expert_sum.reshape(experts, capacity, model_width), 'x', s...]
  transfers between devices with their start and end apart: 3 -> 5, of which waited for: 1 -> 3; matrix products, arithmetic and copies ran while one was open for 1% -> 2% of each run, Pallas kernels for 0% -> 0%
where the time goes in v1:
time: 287 us; the launch traced here: 286 us
  waiting for transfers between devices  159 us (55%)
  blocking collectives  71.2 us (25%)
  between operations  18.1 us (6%)
  matrix products  13.2 us (5%)
  starting transfers between devices  11.2 us (4%)
  other arithmetic  8.34 us (3%)
  local copies, waits for them, and re-layouts  5.08 us (2%)
    all_gather x1, waiting for transfers between devices, local(): lax.all_gather(at_expert.reshape(experts * capacity, model_width), 'z', a...  76.6 us
    reduce_scatter x1, waiting for transfers between devices, local(): lax.psum_scatter(partial_out, 'z', scatter_dimension=0, tiled=True)  76.6 us
    psum x4, blocking collectives, local(): totals = lax.psum(totals, axis)  60.9 us
    dot_general x1, matrix products, expert_rows(): jnp.dot(activated, second_weight, preferred_element_type=jnp.float32)  10.8 us
    all_to_all x1, blocking collectives, local(): lax.all_to_all(buffer, 'x', split_axis=0, concat_axis=0, tiled=True)  10.4 us
    ppermute x2, starting transfers between devices, passed_along(): return lax.ppermute(block, axis, route)  7.08 us
    all_to_all x1, waiting for transfers between devices, local(): lax.all_to_all(expert_sum.reshape(experts, capacity, model_width), 'x', s...  5.91 us
  transfers between devices with their start and end apart: 5, of which 3 were waited for; matrix products, arithmetic and copies ran while one was open for 2% of the time, Pallas kernels for 0%

profile of v1, /device:TPU:1, one launch (start us, length us, event | category | flops | bytes accessed | tf_op | source)
XLA Modules:
  0.0 286.2 jit_solution(16205639869102974398)
XLA Ops:
  7.2 5.8 %collective-permute-start.1 = (bf16[32,2048]{1,0:T(8,128)(2,1)}, bf16[32,2048]{1,0:T(8,128)(2,1)S(1)}, u32[]{:S(2)}, u32[]{:S(2)}) collective-permute-start(bf16[32,2048]{1,0:T(8,128)(2,1)} %bitcast.136), channel_id=1, source_target_pairs={{0,256},{128,384},{1,257},{129,385},{2,258},{130,386},{3,259},{131... | collective-permute-start | bytes 393224 | tf_op jit(solution)/shard_map/ppermute | solution.py:19
  13.7 1.3 collective-permute-start
  15.0 1.0 convert_reduce_fusion
  16.0 0.9 convert_bitcast_fusion
  17.0 0.7 fusion.80
  17.7 1.1 fusion.21
  18.9 0.8 slice_bitcast_fusion.1
  21.4 1.1 fusion.79
  22.5 1.1 multiply_reduce_fusion
  24.3 10.4 %all_to_all.10 = bf16[4,20,2048]{2,1,0:T(8,128)(2,1)S(1)} all-to-all(bf16[4,20,2048]{2,1,0:T(8,128)(2,1)S(1)} %convolution_convert_fusion.1), channel_id=1, replica_groups=mesh['y'=4,'core'=2,'x'=4,'z'=16] {'x'}, dimensions={0} | all-to-all | bytes 655360 | tf_op jit(solution)/shard_map/all_to_all | solution.py:104
  34.7 0.8 reshape.320
  35.6 76.6 %all-gather.2.cloned.1.call-done = bf16[1280,2048]{1,0:T(8,128)(2,1)} async-done(((bf16[80,2048]{1,0:T(8,128)(2,1)}), bf16[1280,2048]{1,0:T(8,128)(2,1)}) %all-gather.2.cloned.1.call-update) | async-done | bytes 5242896 | tf_op jit(solution)/shard_map/all_gather | solution.py:105
  112.2 10.8 %convolution_convert_fusion = bf16[1280,2048]{1,0:T(8,128)(2,1)} fusion(bf16[1280,2048]{1,0:T(8,128)(2,1)} %all-gather.2.cloned.1.call-done, bf16[1,256,2048]{2,1,0:T(8,128)(2,1)} %param.21, bf16[1,2048,256]{2,1,0:T(8,128)(2,1)} %param.20), kind=kOutput, calls=%fused_computation.1 | convolution fusion | flops 2687631360 | bytes 12582912 | tf_op jit(solution)/shard_map/dot_general | solution.py:32
  123.0 76.6 %reduce-scatter.2.cloned.1.call-done = bf16[80,2048]{1,0:T(8,128)(2,1)} async-done(((bf16[1280,2048]{1,0:T(8,128)(2,1)}), bf16[80,2048]{1,0:T(8,128)(2,1)}) %reduce-scatter.2.cloned.1.call-update) | async-done | bytes 327696 | tf_op jit(solution)/shard_map/reduce_scatter | solution.py:109
  199.5 1.8 reshape.321
  201.3 4.0 %all-to-all-start.1 = ((bf16[4,20,2048]{2,1,0:T(8,128)(2,1)}), bf16[4,20,2048]{2,1,0:T(8,128)(2,1)S(1)}, u32[]{:S(2)}, u32[]{:S(2)}) async-start(bf16[4,20,2048]{2,1,0:T(8,128)(2,1)} %reshape.321), calls=%async_computation.2 | async-start | bytes 786432 | tf_op jit(solution)/shard_map/all_to_all | solution.py:110
  205.7 5.9 %all-to-all-done.1 = bf16[4,20,2048]{2,1,0:T(8,128)(2,1)S(1)} async-done(((bf16[4,20,2048]{2,1,0:T(8,128)(2,1)}), bf16[4,20,2048]{2,1,0:T(8,128)(2,1)S(1)}, u32[]{:S(2)}, u32[]{:S(2)}) %all-to-all-start.1) | async-done | bytes 327712 | tf_op jit(solution)/shard_map/all_to_all | solution.py:110
  212.4 0.6 fusion.84
  213.4 0.7 multiply_reduce_fusion.2
  214.1 1.3 pad_maximum_fusion
  215.4 21.9 %psum.28 = f32[2]{0:T(128)S(1)} all-reduce(f32[2]{0:T(128)S(1)} %pad_maximum_fusion), channel_id=1, replica_groups=mesh['y'=4,'core'=2,'x'=4,'z'=16] {'z'}, use_global_device_ids=true, to_apply=%region_19.21 | all-reduce | flops 2 | bytes 16 | tf_op jit(solution)/shard_map/psum | solution.py:128
  237.3 6.6 %psum.29 = f32[2]{0:T(128)S(1)} all-reduce(f32[2]{0:T(128)S(1)} %psum.28), channel_id=1, replica_groups=mesh['y'=4,'core'=2,'x'=4,'z'=16] {'x'}, use_global_device_ids=true, to_apply=%region_20.22 | all-reduce | flops 2 | bytes 16 | tf_op jit(solution)/shard_map/psum | solution.py:128
  243.9 8.3 %psum.30 = f32[2]{0:T(128)S(1)} all-reduce(f32[2]{0:T(128)S(1)} %psum.29), channel_id=1, replica_groups=mesh['y'=4,'core'=2,'x'=4,'z'=16] {'y'}, use_global_device_ids=true, to_apply=%region_21.23 | all-reduce | flops 2 | bytes 16 | tf_op jit(solution)/shard_map/psum | solution.py:128
  252.2 24.1 %psum.31 = f32[2]{0:T(128)S(1)} all-reduce(f32[2]{0:T(128)S(1)} %psum.30), channel_id=1, replica_groups=mesh['y'=4,'core'=2,'x'=4,'z'=16] {'core'}, use_global_device_ids=true, to_apply=%region_22.24 | all-reduce | flops 2 | bytes 16 | tf_op jit(solution)/shard_map/psum | solution.py:128
  (49 shorter events, 4.0 us)
Async XLA Ops:
  7.2 205.2 %copy-start = (bf16[1,2048,512]{2,1,0:T(8,128)(2,1)S(1)}, bf16[1,2048,512]{2,1,0:T(8,128)(2,1)}, u32[]{:S(2)}) copy-start(bf16[1,2048,512]{2,1,0:T(8,128)(2,1)} %param.22) | copy-start | bytes 6291460
  7.2 16.5 %copy-start.1 = (bf16[1,32,2048]{2,1,0:T(8,128)(2,1)S(1)}, bf16[1,32,2048]{2,1,0:T(8,128)(2,1)}, u32[]{:S(2)}) copy-start(bf16[1,32,2048]{2,1,0:T(8,128)(2,1)} %param.13) | copy-start | bytes 393220
  7.2 16.4 %copy-start.5 = (bf16[1,2048,4]{1,2,0:T(4,128)(2,1)S(1)}, bf16[1,2048,4]{1,2,0:T(4,128)(2,1)}, u32[]{:S(2)}) copy-start(bf16[1,2048,4]{1,2,0:T(4,128)(2,1)} %param.19) | copy-start | bytes 49156
  7.2 105.0 %all-gather.2.cloned.1.call-start = ((), (), s32[]{:S(2)}) async-start(), calls=%async_computation.3 | async-start | bytes 5570560 | tf_op jit(solution)/shard_map/all_gather | solution.py:105
  7.2 13.2 %collective-permute-start.1 = (bf16[32,2048]{1,0:T(8,128)(2,1)}, bf16[32,2048]{1,0:T(8,128)(2,1)S(1)}, u32[]{:S(2)}, u32[]{:S(2)}) collective-permute-start(bf16[32,2048]{1,0:T(8,128)(2,1)} %bitcast.136), channel_id=1, source_target_pairs={{0,256},{128,384},{1,257},{129,385},{2,258},{130,386},{3,259},{131... | collective-permute-start | bytes 393224 | tf_op jit(solution)/shard_map/ppermute | solution.py:19
  13.7 6.8 %collective-permute-start = (bf16[32]{0:T(256)(128)(2,1)S(1)}, bf16[32]{0:T(256)(128)(2,1)S(1)}, u32[]{:S(2)}, u32[]{:S(2)}) collective-permute-start(bf16[32]{0:T(256)(128)(2,1)S(1)} %compare_convert_fusion.1), channel_id=1, source_target_pairs={{0,256},{128,384},{1,257},{129,385},{2,258},{130,386},{3,259},{131... | collective-permute-start | bytes 200 | tf_op jit(solution)/shard_map/ppermute | solution.py:19
  35.5 164.0 %reduce-scatter.2.cloned.1.call-start = ((), (), s32[]{:S(2)}) async-start(), calls=%async_computation.4 | async-start | bytes 5570560 | tf_op jit(solution)/shard_map/reduce_scatter | solution.py:109
  123.0 82.4 %copy-start.3 = (f32[1,32,512]{2,1,0:T(8,128)S(1)}, f32[1,32,512]{2,1,0:T(8,128)}, u32[]{:S(2)}) copy-start(f32[1,32,512]{2,1,0:T(8,128)} %param.23) | copy-start | bytes 196612
  123.0 90.3 %copy-start.4 = (s32[1,32]{1,0:T(1,128)S(1)}, s32[1,32]{1,0:T(1,128)}, u32[]{:S(2)}) copy-start(s32[1,32]{1,0:T(1,128)} %param.24) | copy-start | bytes 388
  201.3 10.3 %all-to-all-start.1 = ((bf16[4,20,2048]{2,1,0:T(8,128)(2,1)}), bf16[4,20,2048]{2,1,0:T(8,128)(2,1)S(1)}, u32[]{:S(2)}, u32[]{:S(2)}) async-start(bf16[4,20,2048]{2,1,0:T(8,128)(2,1)} %reshape.321), calls=%async_computation.2 | async-start | bytes 786432 | tf_op jit(solution)/shard_map/all_to_all | solution.py:110
  212.1 66.1 %copy-start.2 = (bf16[32,2048]{1,0:T(8,128)(2,1)}, bf16[32,2048]{1,0:T(8,128)(2,1)S(1)}, u32[]{:S(2)}) copy-start(bf16[32,2048]{1,0:T(8,128)(2,1)S(1)} %get-tuple-element.21) | copy-start | bytes 393220
Sparse Core Ops, SparseCore 0:
  35.6 76.4 all-gather.1
  123.1 76.3 reduce-scatter.1

commit v2 on v1

--- a/solution.py
+++ b/solution.py
@@ -1,16 +1,21 @@
+import functools
 import math
 
 import jax
 import jax.numpy as jnp
 from jax import lax
+from jax.experimental import pallas as pl
+from jax.experimental.pallas import tpu as pltpu
 from jax.sharding import Mesh, PartitionSpec as P
 
 HEADS = 16
 HEAD_DIM = 128
 LEN = 32
+ZL = 4
 
 
 epsilon = 1e-05
+f32, bf16 = jnp.float32, jnp.bfloat16
 
 
 def passed_along(block, axis, distance):
@@ -19,19 +24,128 @@
     return lax.ppermute(block, axis, route)
 
 
+def turned(block, axis, distance):
+    count = math.prod(lax.axis_size(a) for a in ([axis] if isinstance(axis, str) else axis))
+    return lax.ppermute(block, axis, [(i, (i + distance) % count) for i in range(count)])
+
+
 def layer_norm(values, gain_row):
     centred = values - jnp.mean(values, axis=-1, keepdims=True)
     spread = jnp.mean(centred * centred, axis=-1, keepdims=True)
     return centred * lax.rsqrt(spread + epsilon) * gain_row
 
 
-def expert_rows(rows, first_weight, second_weight):
-    activated = jnp.maximum(
-        jnp.dot(rows, first_weight, preferred_element_type=jnp.float32), 0.0
-    ).astype(jnp.bfloat16)
-    return jnp.dot(activated, second_weight, preferred_element_type=jnp.float32).astype(
-        jnp.bfloat16
-    )
+def kernel_call(body, out_shape, in_specs, cost, limit=40 << 20):
+    whole = pl.BlockSpec(memory_space=pltpu.VMEM)
+    scalar = pl.BlockSpec(memory_space=pltpu.SMEM)
+    return pl.pallas_call(
+        body,
+        out_shape=out_shape,
+        in_specs=[scalar if k == "s" else whole for k in in_specs],
+        out_specs=jax.tree.map(lambda _: whole, out_shape),
+        cost_estimate=pl.CostEstimate(flops=cost[0], bytes_accessed=cost[1], transcendentals=0),
+        compiler_params=pltpu.CompilerParams(vmem_limit_bytes=limit),
+    )
+
+
+def share_body(core, w_in, w_out, out):
+    width, hidden = w_in.shape
+    half, deep = hidden // 2, width // 2
+
+    @pl.when(core[0] == 0)
+    def _():
+        for h in range(2):
+            for d in range(2):
+                out[h, :, d * half : (d + 1) * half] = w_in[
+                    d * deep : (d + 1) * deep, h * half : (h + 1) * half
+                ]
+
+    @pl.when(core[0] != 0)
+    def _():
+        for h in range(2):
+            for p in range(width // hidden):
+                out[h, p * half : (p + 1) * half, :] = w_out[
+                    h * half : (h + 1) * half, p * hidden : (p + 1) * hidden
+                ]
+
+
+def mlp_body(core, rows, w_in, w_out, up0, dn0, fu0, fd0, up1, dn1, fu1, fd1, out, acc):
+    width, hidden = w_in.shape
+    half, deep = hidden // 2, width // 2
+
+    def hidden_of(product):
+        return jnp.maximum(product, 0.0).astype(bf16)
+
+    first = hidden_of(jnp.dot(rows[...], w_in[...], preferred_element_type=f32))
+    acc[...] = jnp.dot(first, w_out[...], preferred_element_type=f32)
+
+    def pair(in_a, in_b, out_a, out_b):
+        low = jnp.concatenate([in_a[:, :half], in_b[:, :half]], axis=1)
+        high = jnp.concatenate([in_a[:, half:], in_b[:, half:]], axis=1)
+        act = hidden_of(
+            jnp.dot(rows[:, :deep], low, preferred_element_type=f32)
+            + jnp.dot(rows[:, deep:], high, preferred_element_type=f32)
+        )
+        for p in range(width // hidden):
+            at = slice(p * half, (p + 1) * half)
+            panel = jnp.concatenate([out_a[at, :], out_b[at, :]], axis=0)
+            cols = slice(p * hidden, (p + 1) * hidden)
+            acc[:, cols] += jnp.dot(act, panel, preferred_element_type=f32)
+
+    def rest(a, b):
+        for k in range(2):
+            pair(a[k].at[0], a[k].at[1], b[k].at[0], b[k].at[1])
+        pair(a[2], a[3], b[2], b[3])
+
+    mine, other = (up0, dn0, fu0, fd0), (up1, dn1, fu1, fd1)
+
+    @pl.when(core[0] == 0)
+    def _():
+        rest(mine, other)
+
+    @pl.when(core[0] != 0)
+    def _():
+        rest(other, mine)
+
+    out[...] = acc[...].astype(bf16)
+
+
+def pack_body(slots, own, b1, b2, b3, rows, high, low):
+    width = rows.shape[1]
+    lanes = rows.shape[0]
+    tokens = jnp.concatenate([own[...], b1[...], b2[...], b3[...]], axis=0)
+    count = tokens.shape[0]
+    aux = tokens[:, width:]
+    lane = lax.broadcasted_iota(jnp.int32, (128, lanes), 1)
+    part = lax.broadcasted_iota(jnp.int32, (128, lanes), 0)
+    of_expert = lane // slots
+    pick_high = (part == of_expert).astype(f32).astype(bf16)
+    pick_low = (part == of_expert + 8).astype(f32).astype(bf16)
+    gate_high = jnp.dot(aux, pick_high, preferred_element_type=f32)
+    gate_low = jnp.dot(aux, pick_low, preferred_element_type=f32)
+    chosen = gate_high > 0.0
+    upto = (
+        lax.broadcasted_iota(jnp.int32, (count, count), 0)
+        >= lax.broadcasted_iota(jnp.int32, (count, count), 1)
+    ).astype(f32).astype(bf16)
+    rank = jnp.dot(upto, chosen.astype(f32).astype(bf16), preferred_element_type=f32)
+    slot = (lax.broadcasted_iota(jnp.int32, (count, lanes), 1) % slots + 1).astype(f32)
+    here = jnp.where(chosen & (rank == slot), 1.0, 0.0)
+    rows[...] = lax.dot_general(
+        here.astype(bf16), tokens[:, :width], (((0,), (0,)), ((), ())), preferred_element_type=f32
+    ).astype(bf16)
+    high[...] = (here * gate_high).astype(bf16)
+    low[...] = (here * gate_low).astype(bf16)
+
+
+def combine_body(rows, high, low, own, o1, o2, o3):
+    value = jnp.dot(high[...], rows[...], preferred_element_type=f32) + jnp.dot(
+        low[...], rows[...], preferred_element_type=f32
+    )
+    n = own.shape[0]
+    own[...] = value[:n]
+    for k, o in enumerate((o1, o2, o3)):
+        o[...] = value[(k + 1) * n : (k + 2) * n].astype(bf16)
 
 
 def local(
@@ -59,6 +173,19 @@
     is_valid = positions < lengths[0][seq_index]
     key_mask = (positions < memory_lengths[0][seq_index]).astype(jnp.bfloat16)
     arrived, arrived_mask = passed_along((memory[0], key_mask), "y", chips // 2)
+    core = lax.axis_index("core").astype(jnp.int32)[None]
+    model_hidden = w_in.shape[2]
+    shared = kernel_call(
+        share_body,
+        jax.ShapeDtypeStruct((2, model_width // 2, model_hidden), bf16),
+        "svv",
+        (0, 3 << 20),
+    )(core, w_in[0], w_out[0])
+    line = ("z4", "zl")
+    up, down = turned(shared, line, -1), turned(shared, line, 1)
+    far_up, far_down = turned(up[0], line, -1), turned(down[1], line, 1)
+    mine = (up, down, far_up, far_down)
+    other = [turned(piece, "core", 1) for piece in mine]
     states = hidden[0].astype(jnp.float32)
     gain_rows = norm_gain[0]
     seq_count = tok_rows // LEN
@@ -91,27 +218,50 @@
     prob_second = jnp.sum(router_probs * second, axis=-1, keepdims=True)
     prob_total = prob_first + prob_second
     gate_rows = (prob_first * first_hot + prob_second * second) / prob_total
-    chosen = (first_hot + second) * is_valid[:, None].astype(jnp.float32)
-    upto = (jnp.arange(tok_rows)[:, None] >= jnp.arange(tok_rows)[None, :]).astype(jnp.float32)
-    slot_rank = jnp.dot(upto, chosen, preferred_element_type=jnp.float32) - 1.0
-    slot_ids = jnp.arange(capacity).astype(jnp.float32)
-    placing = chosen.T[:, None, :] * (slot_rank.T[:, None, :] == slot_ids[None, :, None]).astype(
-        jnp.float32
-    )
-    buffer = jnp.einsum(
-        "ect,td->ecd", placing.astype(jnp.bfloat16), normed, preferred_element_type=jnp.float32
-    ).astype(jnp.bfloat16)
-    at_expert = lax.all_to_all(buffer, "x", split_axis=0, concat_axis=0, tiled=True)
-    rows = lax.all_gather(
-        at_expert.reshape(experts * capacity, model_width), "z", axis=0, tiled=True
-    )
-    partial_out = expert_rows(rows, w_in[0], w_out[0])
-    expert_sum = lax.psum_scatter(partial_out, "z", scatter_dimension=0, tiled=True)
-    summed = lax.all_to_all(
-        expert_sum.reshape(experts, capacity, model_width), "x", split_axis=0, concat_axis=0, tiled=True
-    ).astype(jnp.float32)
-    weighting = placing * gate_rows.T[:, None, :]
-    moe_out = jnp.einsum("ect,ecd->td", weighting, summed, precision=lax.Precision.HIGHEST)
+    combine = gate_rows * (first_hot + second) * is_valid[:, None].astype(f32)
+    combine_high = combine.astype(bf16)
+    combine_low = (combine - lax.reduce_precision(combine, 8, 7)).astype(bf16)
+    pad = jnp.zeros((tok_rows, 8 - experts), bf16)
+    block = jnp.concatenate(
+        [normed, combine_high, pad, combine_low, pad, jnp.zeros((tok_rows, 112), bf16)], axis=1
+    )
+    visitors = [turned(block, "z4", k) for k in (1, 2, 3)]
+    slots = 4 * capacity
+    lanes = experts * slots
+    packed, gates_high, gates_low = kernel_call(
+        functools.partial(pack_body, slots),
+        (
+            jax.ShapeDtypeStruct((lanes, model_width), bf16),
+            jax.ShapeDtypeStruct((4 * tok_rows, lanes), bf16),
+            jax.ShapeDtypeStruct((4 * tok_rows, lanes), bf16),
+        ),
+        "vvvv",
+        (2 * lanes * 4 * tok_rows * model_width, 2 << 20),
+    )(block, *visitors)
+    rows = lax.all_to_all(packed, "x", split_axis=0, concat_axis=0, tiled=True)
+    whole = pl.BlockSpec(memory_space=pltpu.VMEM)
+    partial_out = pl.pallas_call(
+        mlp_body,
+        out_shape=jax.ShapeDtypeStruct((lanes, model_width), bf16),
+        in_specs=[pl.BlockSpec(memory_space=pltpu.SMEM)] + [whole] * 11,
+        out_specs=whole,
+        scratch_shapes=[pltpu.VMEM((lanes, model_width), f32)],
+        cost_estimate=pl.CostEstimate(
+            flops=4 * lanes * model_width * 1024, bytes_accessed=11 << 20, transcendentals=0
+        ),
+        compiler_params=pltpu.CompilerParams(vmem_limit_bytes=40 << 20),
+    )(core, rows, w_in[0], w_out[0], *mine, *other)
+    returned = lax.all_to_all(partial_out, "x", split_axis=0, concat_axis=0, tiled=True)
+    own_part, *parts = kernel_call(
+        combine_body,
+        (jax.ShapeDtypeStruct((tok_rows, model_width), f32),)
+        + (jax.ShapeDtypeStruct((tok_rows, model_width), bf16),) * 3,
+        "vvv",
+        (4 * lanes * 4 * tok_rows * model_width, 2 << 20),
+    )(returned, gates_high, gates_low)
+    moe_out = own_part
+    for k, part in zip((1, 2, 3), parts):
+        moe_out = moe_out + turned(part, "z4", -k).astype(f32)
     layer_out = (mid_states + moe_out).astype(jnp.bfloat16)
     final_normed = layer_norm(layer_out.astype(jnp.float32), gain_rows[2]).astype(jnp.bfloat16)
     teacher = jax.nn.log_softmax(
@@ -124,8 +274,10 @@
     )
     counted = jnp.where(decoder, is_valid.astype(jnp.float32), 0.0)
     totals = jnp.stack([jnp.sum(token_loss * counted), jnp.sum(counted)])
-    for axis in ("z", "x", "y", "core"):
-        totals = lax.psum(totals, axis)
+    for axes in (("x", "zl"), ("y", "core", "z4")):
+        count = math.prod(lax.axis_size(a) for a in axes)
+        spread_out = jnp.broadcast_to(jnp.pad(totals, (0, 126))[None], (count, 128))
+        totals = lax.all_to_all(spread_out, axes, split_axis=0, concat_axis=0, tiled=True).sum(0)[:2]
     return (layer_out[None], totals[0] / totals[1])
 
 
@@ -133,10 +285,10 @@
     segments, expert_devices = mesh.devices.shape
     experts = 4
     fine = Mesh(
-        mesh.devices.reshape(segments // 2, 2, experts, expert_devices // experts),
-        ("y", "core", "x", "z"),
-    )
-    seg, exp = ("y", "core"), ("x", "z")
+        mesh.devices.reshape(segments // 2, 2, experts, expert_devices // experts // ZL, ZL),
+        ("y", "core", "x", "z4", "zl"),
+    )
+    seg, exp = ("y", "core"), ("x", "z4", "zl")
     placed = (
         P(seg, exp, None),
         P(seg, exp, None),

time: 287 us -> 217 us (0.76)
  waiting for transfers between devices: 159 us -> 29.3 us
  starting transfers between devices: 11.2 us -> 76.9 us
  between operations: 18.1 us -> 4.93 us
  local copies, waits for them, and re-layouts: 5.08 us -> 17.6 us
  blocking collectives: 71.2 us -> 60.5 us
  Pallas kernels: 0 us -> 8.96 us
  matrix products: 13.2 us -> 6.15 us
    all_gather x1 -> x0, waiting for transfers between devices: 76.6 us -> none  [local(): lax.all_gather(at_expert.reshape(experts * capacity, model_width), 'z', a...]
    reduce_scatter x1 -> x0, waiting for transfers between devices: 76.6 us -> none  [local(): lax.psum_scatter(partial_out, 'z', scatter_dimension=0, tiled=True)]
    ppermute x0 -> x14, starting transfers between devices: none -> 65.6 us  [turned(): lax.ppermute(block, axis, [(i, (i + distance) % count) for i in range(cou...]
    psum x4 -> x0, blocking collectives: 60.9 us -> none  [local(): totals = lax.psum(totals, axis)]
    all_to_all x1 -> x3, blocking collectives: 10.4 us -> 60.5 us  [the longest x2 41.1 us: local(): lax.all_to_all(spread_out, axes, split_axis=0, concat_axis=0, tiled=True)]
    ppermute x0 -> x14, waiting for transfers between devices: none -> 21.7 us  [turned(): lax.ppermute(block, axis, [(i, (i + distance) % count) for i in range(cou...]
    dot_general x4 -> x1, matrix products: 11.8 us -> 1.19 us  [local(): jnp.einsum('bqhd,bkhd->bhqk', queries, key_rows, preferred_element_type=j...]
    pallas_call x0 -> x4, Pallas kernels: none -> 8.96 us  [the longest x1 7.34 us: local(): pl.pallas_call(mlp_body, out_shape=jax.ShapeDtypeStruct((lanes, model_wid...]
  transfers between devices with their start and end apart: 5 -> 17, of which waited for: 3 -> 5; matrix products, arithmetic and copies ran while one was open for 2% -> 11% of each run, Pallas kernels for 0% -> 0%
where the time goes in v2:
time: 217 us; the launch traced here: 215 us
  starting transfers between devices  76.9 us (35%)
  blocking collectives  60.5 us (28%)
  waiting for transfers between devices  29.3 us (14%)
  local copies, waits for them, and re-layouts  17.6 us (8%)
  other arithmetic  11.1 us (5%)
  Pallas kernels  8.96 us (4%)
  matrix products  6.15 us (3%)
  between operations  4.93 us (2%)
    ppermute x14, starting transfers between devices, turned(): lax.ppermute(block, axis, [(i, (i + distance) % count) for i in range(cou...  65.6 us
    all_to_all x2, blocking collectives, local(): lax.all_to_all(spread_out, axes, split_axis=0, concat_axis=0, tiled=True)  41.1 us
    ppermute x14, waiting for transfers between devices, turned(): lax.ppermute(block, axis, [(i, (i + distance) % count) for i in range(cou...  21.7 us
    all_to_all x1, blocking collectives, local(): lax.all_to_all(partial_out, 'x', split_axis=0, concat_axis=0, tiled=True)  19.4 us
    unnamed x49, local copies, waits for them, and re-layouts  7.85 us
    all_to_all x1, waiting for transfers between devices, local(): rows = lax.all_to_all(packed, 'x', split_axis=0, concat_axis=0, tiled=True)  7.59 us
    ppermute x2, starting transfers between devices, passed_along(): return lax.ppermute(block, axis, route)  7.35 us
    pallas_call x1, Pallas kernels, local(): pl.pallas_call(mlp_body, out_shape=jax.ShapeDtypeStruct((lanes, model_wid...  7.34 us
  transfers between devices with their start and end apart: 17, of which 5 were waited for; matrix products, arithmetic and copies ran while one was open for 11% of the time, Pallas kernels for 0%

profile of v2, /device:TPU:1, one launch (start us, length us, event | category | flops | bytes accessed | tf_op | source)
XLA Modules:
  0.0 215.5 jit_solution(4199511627906232158)
XLA Ops:
  3.3 12.0 %collective-permute-start.5 = (bf16[2,1024,256]{2,1,0:T(8,128)(2,1)S(1)}, bf16[2,1024,256]{2,1,0:T(8,128)(2,1)}, u32[]{:S(2)}, u32[]{:S(2)}) collective-permute-start(bf16[2,1024,256]{2,1,0:T(8,128)(2,1)S(1)} %shard_map.132), channel_id=1, source_target_pairs={{0,15},{1,0},{2,1},{3,2},{4,3},{5,4},{6,5},{7,6},{8,7},{9,8},{10,9... | collective-permute-start | bytes 3145736 | tf_op jit(solution)/shard_map/ppermute | solution.py:29
  15.3 1.9 collective-permute-start.6
  17.2 5.5 %collective-permute-start.1 = (bf16[32,2048]{1,0:T(8,128)(2,1)}, bf16[32,2048]{1,0:T(8,128)(2,1)}, u32[]{:S(2)}, u32[]{:S(2)}) collective-permute-start(bf16[32,2048]{1,0:T(8,128)(2,1)} %bitcast.3), channel_id=1, source_target_pairs={{0,256},{128,384},{1,257},{129,385},{2,258},{130,386},{3,259},{131... | collective-permute-start | bytes 393224 | tf_op jit(solution)/shard_map/ppermute | solution.py:24
  32.9 2.0 convolution_select_fusion
  36.5 2.3 %fusion.60 = (f32[32]{0:T(128)}, f32[32,4]{0,1:T(4,128)}) fusion(bf16[1,2048,4]{1,2,0:T(4,128)(2,1)} %param.19, bf16[1,32,2048]{2,1,0:T(8,128)(2,1)S(1)} %copy-done.10, f32[2048]{0:T(1024)S(1)} %bitcast.139, f32[32]{0:T(128)S(1)} %add_rsqrt_fusion.1, f32[32]{0:T(128)S(1)} %broadcast_multiply_fusion.1, f32[16,32,128]{2,1,0:T(8,128)} %convolution_select_fusion), kind=kOutput, calls=%fused_computation.99 | convolution fusion | flops 917600 | bytes 418688 | tf_op jit(solution)/shard_map/dot_general | solution.py:212
  47.6 10.3 %collective-permute-start.3 = (bf16[32,2176]{1,0:T(8,128)(2,1)S(1)}, bf16[32,2176]{1,0:T(8,128)(2,1)S(1)}, u32[]{:S(2)}, u32[]{:S(2)}) collective-permute-start(bf16[32,2176]{1,0:T(8,128)(2,1)S(1)} %concatenate.3.own), channel_id=1, source_target_pairs={{0,8},{4,12},{8,0},{12,4},{1,9},{5,13},{9,1},{13,5},{2,10},{6,14},... | collective-permute-start | bytes 417800 | tf_op jit(solution)/shard_map/ppermute | solution.py:29
  57.9 4.7 %collective-permute-start.4 = (bf16[32,2176]{1,0:T(8,128)(2,1)S(1)}, bf16[32,2176]{1,0:T(8,128)(2,1)S(1)}, u32[]{:S(2)}, u32[]{:S(2)}) collective-permute-start(bf16[32,2176]{1,0:T(8,128)(2,1)S(1)} %concatenate.3.own), channel_id=1, source_target_pairs={{0,12},{4,0},{8,4},{12,8},{1,13},{5,1},{9,5},{13,9},{2,14},{6,2},{... | collective-permute-start | bytes 417800 | tf_op jit(solution)/shard_map/ppermute | solution.py:29
  64.5 3.1 %collective-permute-start.7 = (bf16[1024,256]{1,0:T(8,128)(2,1)}, bf16[1024,256]{1,0:T(8,128)(2,1)}, u32[]{:S(2)}, u32[]{:S(2)}) collective-permute-start(bf16[1024,256]{1,0:T(8,128)(2,1)} %slice_bitcast_fusion.1), channel_id=1, source_target_pairs={{0,15},{1,0},{2,1},{3,2},{4,3},{5,4},{6,5},{7,6},{8,7},{9,8},{10,9... | collective-permute-start | bytes 1572872 | tf_op jit(solution)/shard_map/ppermute | solution.py:29
  69.5 2.1 collective-permute-start.8
  71.7 4.9 %collective-permute-start.10 = (bf16[2,1024,256]{2,1,0:T(8,128)(2,1)}, bf16[2,1024,256]{2,1,0:T(8,128)(2,1)}, u32[]{:S(2)}, u32[]{:S(2)}) collective-permute-start(bf16[2,1024,256]{2,1,0:T(8,128)(2,1)} %collective-permute-done.6.dn0), channel_id=1, source_target_pairs={{0,64},{64,0},{1,65},{65,1},{2,66},{66,2},{3,67},{67,3},{4,68},{68... | collective-permute-start | bytes 3145736 | tf_op jit(solution)/shard_map/ppermute | solution.py:29
  78.1 3.8 %collective-permute-start.9 = (bf16[2,1024,256]{2,1,0:T(8,128)(2,1)}, bf16[2,1024,256]{2,1,0:T(8,128)(2,1)}, u32[]{:S(2)}, u32[]{:S(2)}) collective-permute-start(bf16[2,1024,256]{2,1,0:T(8,128)(2,1)} %collective-permute-done.5.up0), channel_id=1, source_target_pairs={{0,64},{64,0},{1,65},{65,1},{2,66},{66,2},{3,67},{67,3},{4,68},{68... | collective-permute-start | bytes 3145736 | tf_op jit(solution)/shard_map/ppermute | solution.py:29
  84.4 4.0 %all-to-all-start = ((bf16[4,80,2048]{2,1,0:T(8,128)(2,1)}), bf16[4,80,2048]{2,1,0:T(8,128)(2,1)S(1)}, u32[]{:S(2)}, u32[]{:S(2)}) async-start(bf16[4,80,2048]{2,1,0:T(8,128)(2,1)} %bitcast.129), calls=%async_computation | async-start | bytes 2621440 | tf_op jit(solution)/shard_map/all_to_all | solution.py:241
  88.4 5.2 %collective-permute-done.7.fu0 = bf16[1024,256]{1,0:T(8,128)(2,1)} collective-permute-done((bf16[1024,256]{1,0:T(8,128)(2,1)}, bf16[1024,256]{1,0:T(8,128)(2,1)}, u32[]{:S(2)}, u32[]{:S(2)}) %collective-permute-start.7) | collective-permute-done | bytes 524320 | tf_op jit(solution)/shard_map/ppermute | solution.py:29
  93.6 3.0 %collective-permute-start.11 = (bf16[1024,256]{1,0:T(8,128)(2,1)}, bf16[1024,256]{1,0:T(8,128)(2,1)}, u32[]{:S(2)}, u32[]{:S(2)}) collective-permute-start(bf16[1024,256]{1,0:T(8,128)(2,1)} %collective-permute-done.7.fu0), channel_id=1, source_target_pairs={{0,64},{64,0},{1,65},{65,1},{2,66},{66,2},{3,67},{67,3},{4,68},{68... | collective-permute-start | bytes 1572872 | tf_op jit(solution)/shard_map/ppermute | solution.py:29
  96.7 1.9 collective-permute-start.12
  98.6 7.6 %all-to-all-done = bf16[4,80,2048]{2,1,0:T(8,128)(2,1)S(1)} async-done(((bf16[4,80,2048]{2,1,0:T(8,128)(2,1)}), bf16[4,80,2048]{2,1,0:T(8,128)(2,1)S(1)}, u32[]{:S(2)}, u32[]{:S(2)}) %all-to-all-start) | async-done | bytes 1310752 | tf_op jit(solution)/shard_map/all_to_all | solution.py:241
  108.7 7.3 %shard_map.133 = bf16[320,2048]{1,0:T(8,128)(2,1)S(1)} custom-call(s32[1]{0:T(128)} %bitcast.7.core, bf16[320,2048]{1,0:T(8,128)(2,1)S(1)} %bitcast.123, bf16[2048,256]{1,0:T(8,128)(2,1)S(1)} %bitcast.126, bf16[256,2048]{1,0:T(8,128)(2,1)S(1)} %bitcast.128, bf16[2,1024,256]{2,1,0:T(8,128)(2,1)} %collective-permute-done.5.up0, ...), custom_call_target="tpu_custom_call" | custom-call | flops 2684354560 | bytes 11534336 | tf_op jit(solution)/shard_map/pallas_call | solution.py:243
  116.1 19.4 %all_to_all.34 = bf16[4,80,2048]{2,1,0:T(8,128)(2,1)S(1)} all-to-all(bf16[4,80,2048]{2,1,0:T(8,128)(2,1)S(1)} %bitcast.124), channel_id=1, replica_groups=mesh['y'=4,'core'=2,'x'=4,'z4'=4,'zl'=4] {'x'}, dimensions={0} | all-to-all | bytes 2621440 | tf_op jit(solution)/shard_map/all_to_all | solution.py:254
  136.2 6.5 %collective-permute-start.13 = (bf16[32,2048]{1,0:T(8,128)(2,1)S(1)}, bf16[32,2048]{1,0:T(8,128)(2,1)S(1)}, u32[]{:S(2)}, u32[]{:S(2)}) collective-permute-start(bf16[32,2048]{1,0:T(8,128)(2,1)S(1)} %get-tuple-element.14), channel_id=1, source_target_pairs={{0,12},{4,0},{8,4},{12,8},{1,13},{5,1},{9,5},{13,9},{2,14},{6,2},{... | collective-permute-start | bytes 393224 | tf_op jit(solution)/shard_map/ppermute | solution.py:29
  142.7 7.4 %collective-permute-start.14 = (bf16[32,2048]{1,0:T(8,128)(2,1)S(1)}, bf16[32,2048]{1,0:T(8,128)(2,1)S(1)}, u32[]{:S(2)}, u32[]{:S(2)}) collective-permute-start(bf16[32,2048]{1,0:T(8,128)(2,1)S(1)} %get-tuple-element.15), channel_id=1, source_target_pairs={{0,8},{4,12},{8,0},{12,4},{1,9},{5,13},{9,1},{13,5},{2,10},{6,14},... | collective-permute-start | bytes 393224 | tf_op jit(solution)/shard_map/ppermute | solution.py:29
  150.2 1.9 collective-permute-start.15
  152.4 13.5 %collective-permute-done.14 = bf16[32,2048]{1,0:T(8,128)(2,1)S(1)} collective-permute-done((bf16[32,2048]{1,0:T(8,128)(2,1)S(1)}, bf16[32,2048]{1,0:T(8,128)(2,1)S(1)}, u32[]{:S(2)}, u32[]{:S(2)}) %collective-permute-start.14) | collective-permute-done | bytes 131104 | tf_op jit(solution)/shard_map/ppermute | solution.py:29
  171.1 17.4 %all_to_all.35 = f32[16,1,128]{2,1,0:T(1,128)S(1)} all-to-all(f32[16,1,128]{2,1,0:T(1,128)S(1)} %broadcast_in_dim.42), channel_id=1, replica_groups=mesh['y'=4,'core'=2,'x'=4,'z4'=4,'zl'=4] {'x','zl'}, dimensions={0} | all-to-all | bytes 16384 | tf_op jit(solution)/shard_map/all_to_all | solution.py:280
  188.6 23.7 %all_to_all.36 = f32[32,1,128]{2,1,0:T(1,128)S(1)} all-to-all(f32[32,1,128]{2,1,0:T(1,128)S(1)} %broadcast_in_dim.43), channel_id=1, replica_groups=mesh['y'=4,'core'=2,'x'=4,'z4'=4,'zl'=4] {'y','core','z4'}, dimensions={0} | all-to-all | bytes 32768 | tf_op jit(solution)/shard_map/all_to_all | solution.py:280
  (115 shorter events, 38.9 us)
Async XLA Ops:
  0.6 167.3 %copy-start = (bf16[1,2048,512]{2,1,0:T(8,128)(2,1)S(1)}, bf16[1,2048,512]{2,1,0:T(8,128)(2,1)}, u32[]{:S(2)}) copy-start(bf16[1,2048,512]{2,1,0:T(8,128)(2,1)} %param.22) | copy-start | bytes 6291460
  3.3 59.3 %collective-permute-start.5 = (bf16[2,1024,256]{2,1,0:T(8,128)(2,1)S(1)}, bf16[2,1024,256]{2,1,0:T(8,128)(2,1)}, u32[]{:S(2)}, u32[]{:S(2)}) collective-permute-start(bf16[2,1024,256]{2,1,0:T(8,128)(2,1)S(1)} %shard_map.132), channel_id=1, source_target_pairs={{0,15},{1,0},{2,1},{3,2},{4,3},{5,4},{6,5},{7,6},{8,7},{9,8},{10,9... | collective-permute-start | bytes 3145736 | tf_op jit(solution)/shard_map/ppermute | solution.py:29
  15.3 52.3 %collective-permute-start.6 = (bf16[2,1024,256]{2,1,0:T(8,128)(2,1)S(1)}, bf16[2,1024,256]{2,1,0:T(8,128)(2,1)}, u32[]{:S(2)}, u32[]{:S(2)}) collective-permute-start(bf16[2,1024,256]{2,1,0:T(8,128)(2,1)S(1)} %shard_map.132), channel_id=1, source_target_pairs={{0,1},{1,2},{2,3},{3,4},{4,5},{5,6},{6,7},{7,8},{8,9},{9,10},{10,1... | collective-permute-start | bytes 3145736 | tf_op jit(solution)/shard_map/ppermute | solution.py:29
  17.2 13.6 %collective-permute-start.1 = (bf16[32,2048]{1,0:T(8,128)(2,1)}, bf16[32,2048]{1,0:T(8,128)(2,1)}, u32[]{:S(2)}, u32[]{:S(2)}) collective-permute-start(bf16[32,2048]{1,0:T(8,128)(2,1)} %bitcast.3), channel_id=1, source_target_pairs={{0,256},{128,384},{1,257},{129,385},{2,258},{130,386},{3,259},{131... | collective-permute-start | bytes 393224 | tf_op jit(solution)/shard_map/ppermute | solution.py:24
  23.9 6.2 %collective-permute-start = (bf16[32]{0:T(256)(128)(2,1)}, bf16[32]{0:T(256)(128)(2,1)}, u32[]{:S(2)}, u32[]{:S(2)}) collective-permute-start(bf16[32]{0:T(256)(128)(2,1)} %compare_convert_fusion.1), channel_id=1, source_target_pairs={{0,256},{128,384},{1,257},{129,385},{2,258},{130,386},{3,259},{131... | collective-permute-start | bytes 200 | tf_op jit(solution)/shard_map/ppermute | solution.py:24
  45.7 25.9 %collective-permute-start.2 = (bf16[32,2176]{1,0:T(8,128)(2,1)S(1)}, bf16[32,2176]{1,0:T(8,128)(2,1)S(1)}, u32[]{:S(2)}, u32[]{:S(2)}) collective-permute-start(bf16[32,2176]{1,0:T(8,128)(2,1)S(1)} %concatenate.3.own), channel_id=1, source_target_pairs={{0,4},{4,8},{8,12},{12,0},{1,5},{5,9},{9,13},{13,1},{2,6},{6,10},{... | collective-permute-start | bytes 417800 | tf_op jit(solution)/shard_map/ppermute | solution.py:29
  47.6 30.4 %collective-permute-start.3 = (bf16[32,2176]{1,0:T(8,128)(2,1)S(1)}, bf16[32,2176]{1,0:T(8,128)(2,1)S(1)}, u32[]{:S(2)}, u32[]{:S(2)}) collective-permute-start(bf16[32,2176]{1,0:T(8,128)(2,1)S(1)} %concatenate.3.own), channel_id=1, source_target_pairs={{0,8},{4,12},{8,0},{12,4},{1,9},{5,13},{9,1},{13,5},{2,10},{6,14},... | collective-permute-start | bytes 417800 | tf_op jit(solution)/shard_map/ppermute | solution.py:29
  57.9 24.0 %collective-permute-start.4 = (bf16[32,2176]{1,0:T(8,128)(2,1)S(1)}, bf16[32,2176]{1,0:T(8,128)(2,1)S(1)}, u32[]{:S(2)}, u32[]{:S(2)}) collective-permute-start(bf16[32,2176]{1,0:T(8,128)(2,1)S(1)} %concatenate.3.own), channel_id=1, source_target_pairs={{0,12},{4,0},{8,4},{12,8},{1,13},{5,1},{9,5},{13,9},{2,14},{6,2},{... | collective-permute-start | bytes 417800 | tf_op jit(solution)/shard_map/ppermute | solution.py:29
  64.5 29.1 %collective-permute-start.7 = (bf16[1024,256]{1,0:T(8,128)(2,1)}, bf16[1024,256]{1,0:T(8,128)(2,1)}, u32[]{:S(2)}, u32[]{:S(2)}) collective-permute-start(bf16[1024,256]{1,0:T(8,128)(2,1)} %slice_bitcast_fusion.1), channel_id=1, source_target_pairs={{0,15},{1,0},{2,1},{3,2},{4,3},{5,4},{6,5},{7,6},{8,7},{9,8},{10,9... | collective-permute-start | bytes 1572872 | tf_op jit(solution)/shard_map/ppermute | solution.py:29
  69.5 27.2 %collective-permute-start.8 = (bf16[1024,256]{1,0:T(8,128)(2,1)}, bf16[1024,256]{1,0:T(8,128)(2,1)}, u32[]{:S(2)}, u32[]{:S(2)}) collective-permute-start(bf16[1024,256]{1,0:T(8,128)(2,1)} %slice_bitcast_fusion), channel_id=1, source_target_pairs={{0,1},{1,2},{2,3},{3,4},{4,5},{5,6},{6,7},{7,8},{8,9},{9,10},{10,1... | collective-permute-start | bytes 1572872 | tf_op jit(solution)/shard_map/ppermute | solution.py:29
  71.7 34.5 %collective-permute-start.10 = (bf16[2,1024,256]{2,1,0:T(8,128)(2,1)}, bf16[2,1024,256]{2,1,0:T(8,128)(2,1)}, u32[]{:S(2)}, u32[]{:S(2)}) collective-permute-start(bf16[2,1024,256]{2,1,0:T(8,128)(2,1)} %collective-permute-done.6.dn0), channel_id=1, source_target_pairs={{0,64},{64,0},{1,65},{65,1},{2,66},{66,2},{3,67},{67,3},{4,68},{68... | collective-permute-start | bytes 3145736 | tf_op jit(solution)/shard_map/ppermute | solution.py:29
  78.1 28.1 %collective-permute-start.9 = (bf16[2,1024,256]{2,1,0:T(8,128)(2,1)}, bf16[2,1024,256]{2,1,0:T(8,128)(2,1)}, u32[]{:S(2)}, u32[]{:S(2)}) collective-permute-start(bf16[2,1024,256]{2,1,0:T(8,128)(2,1)} %collective-permute-done.5.up0), channel_id=1, source_target_pairs={{0,64},{64,0},{1,65},{65,1},{2,66},{66,2},{3,67},{67,3},{4,68},{68... | collective-permute-start | bytes 3145736 | tf_op jit(solution)/shard_map/ppermute | solution.py:29
  84.4 21.8 %all-to-all-start = ((bf16[4,80,2048]{2,1,0:T(8,128)(2,1)}), bf16[4,80,2048]{2,1,0:T(8,128)(2,1)S(1)}, u32[]{:S(2)}, u32[]{:S(2)}) async-start(bf16[4,80,2048]{2,1,0:T(8,128)(2,1)} %bitcast.129), calls=%async_computation | async-start | bytes 2621440 | tf_op jit(solution)/shard_map/all_to_all | solution.py:241
  93.6 12.6 %collective-permute-start.11 = (bf16[1024,256]{1,0:T(8,128)(2,1)}, bf16[1024,256]{1,0:T(8,128)(2,1)}, u32[]{:S(2)}, u32[]{:S(2)}) collective-permute-start(bf16[1024,256]{1,0:T(8,128)(2,1)} %collective-permute-done.7.fu0), channel_id=1, source_target_pairs={{0,64},{64,0},{1,65},{65,1},{2,66},{66,2},{3,67},{67,3},{4,68},{68... | collective-permute-start | bytes 1572872 | tf_op jit(solution)/shard_map/ppermute | solution.py:29
  96.7 9.5 %collective-permute-start.12 = (bf16[1024,256]{1,0:T(8,128)(2,1)}, bf16[1024,256]{1,0:T(8,128)(2,1)}, u32[]{:S(2)}, u32[]{:S(2)}) collective-permute-start(bf16[1024,256]{1,0:T(8,128)(2,1)} %collective-permute-done.8.fd0), channel_id=1, source_target_pairs={{0,64},{64,0},{1,65},{65,1},{2,66},{66,2},{3,67},{67,3},{4,68},{68... | collective-permute-start | bytes 1572872 | tf_op jit(solution)/shard_map/ppermute | solution.py:29
  116.0 36.1 %copy-start.13 = (f32[1,32,512]{2,1,0:T(8,128)S(1)}, f32[1,32,512]{2,1,0:T(8,128)}, u32[]{:S(2)}) copy-start(f32[1,32,512]{2,1,0:T(8,128)} %param.23) | copy-start | bytes 196612
  116.0 51.4 %copy-start.9 = (f32[1,32,16,128]{3,2,1,0:T(8,128)S(1)}, f32[1,32,16,128]{3,2,1,0:T(8,128)}, u32[]{:S(2)}) copy-start(f32[1,32,16,128]{3,2,1,0:T(8,128)} %copy-done.8) | copy-start | bytes 786436
  116.0 51.4 %copy-start.11 = (bf16[1,32,2048]{2,1,0:T(8,128)(2,1)S(1)}, bf16[1,32,2048]{2,1,0:T(8,128)(2,1)}, u32[]{:S(2)}) copy-start(bf16[1,32,2048]{2,1,0:T(8,128)(2,1)} %param.13) | copy-start | bytes 393220
  136.1 32.7 %copy-start.20 = (s32[1,32]{1,0:T(1,128)S(1)}, s32[1,32]{1,0:T(1,128)}, u32[]{:S(2)}) copy-start(s32[1,32]{1,0:T(1,128)} %param.24) | copy-start | bytes 388
  136.2 52.4 %copy-start.22 = (pred[128]{0:T(512)(128)(4,1)S(1)}, pred[128]{0:T(512)(128)(4,1)}, u32[]{:S(2)}) copy-start(pred[128]{0:T(512)(128)(4,1)} %constant.81.clone.1) | copy-start | bytes 388
  136.2 16.2 %collective-permute-start.13 = (bf16[32,2048]{1,0:T(8,128)(2,1)S(1)}, bf16[32,2048]{1,0:T(8,128)(2,1)S(1)}, u32[]{:S(2)}, u32[]{:S(2)}) collective-permute-start(bf16[32,2048]{1,0:T(8,128)(2,1)S(1)} %get-tuple-element.14), channel_id=1, source_target_pairs={{0,12},{4,0},{8,4},{12,8},{1,13},{5,1},{9,5},{13,9},{2,14},{6,2},{... | collective-permute-start | bytes 393224 | tf_op jit(solution)/shard_map/ppermute | solution.py:29
  142.7 23.2 %collective-permute-start.14 = (bf16[32,2048]{1,0:T(8,128)(2,1)S(1)}, bf16[32,2048]{1,0:T(8,128)(2,1)S(1)}, u32[]{:S(2)}, u32[]{:S(2)}) collective-permute-start(bf16[32,2048]{1,0:T(8,128)(2,1)S(1)} %get-tuple-element.15), channel_id=1, source_target_pairs={{0,8},{4,12},{8,0},{12,4},{1,9},{5,13},{9,1},{13,5},{2,10},{6,14},... | collective-permute-start | bytes 393224 | tf_op jit(solution)/shard_map/ppermute | solution.py:29
  150.2 17.3 %collective-permute-start.15 = (bf16[32,2048]{1,0:T(8,128)(2,1)S(1)}, bf16[32,2048]{1,0:T(8,128)(2,1)S(1)}, u32[]{:S(2)}, u32[]{:S(2)}) collective-permute-start(bf16[32,2048]{1,0:T(8,128)(2,1)S(1)} %get-tuple-element.16), channel_id=1, source_target_pairs={{0,4},{4,8},{8,12},{12,0},{1,5},{5,9},{9,13},{13,1},{2,6},{6,10},{... | collective-permute-start | bytes 393224 | tf_op jit(solution)/shard_map/ppermute | solution.py:29
  167.7 46.6 %copy-start.12 = (bf16[32,2048]{1,0:T(8,128)(2,1)}, bf16[32,2048]{1,0:T(8,128)(2,1)S(1)}, u32[]{:S(2)}) copy-start(bf16[32,2048]{1,0:T(8,128)(2,1)S(1)} %get-tuple-element.22) | copy-start | bytes 393220
  (17 other events, 129.3 us)

commit v3 on v2

--- a/solution.py
+++ b/solution.py
@@ -48,66 +48,179 @@
     )
 
 
-def share_body(core, w_in, w_out, out):
+def share_body(core, w_in, w_out, out, sems):
     width, hidden = w_in.shape
     half, deep = hidden // 2, width // 2
 
+    def carried(pairs):
+        copies = [
+            pltpu.make_async_copy(src, dst, sems.at[k]) for k, (src, dst) in enumerate(pairs)
+        ]
+        for copy in copies:
+            copy.start()
+        for copy in copies:
+            copy.wait()
+
     @pl.when(core[0] == 0)
     def _():
-        for h in range(2):
-            for d in range(2):
-                out[h, :, d * half : (d + 1) * half] = w_in[
-                    d * deep : (d + 1) * deep, h * half : (h + 1) * half
-                ]
+        carried(
+            [
+                (
+                    w_in.at[pl.ds(d * deep, deep), pl.ds(h * half, half)],
+                    out.at[h, :, pl.ds(d * half, half)],
+                )
+                for h in range(2)
+                for d in range(2)
+            ]
+        )
 
     @pl.when(core[0] != 0)
     def _():
-        for h in range(2):
-            for p in range(width // hidden):
-                out[h, p * half : (p + 1) * half, :] = w_out[
-                    h * half : (h + 1) * half, p * hidden : (p + 1) * hidden
-                ]
-
-
-def mlp_body(core, rows, w_in, w_out, up0, dn0, fu0, fd0, up1, dn1, fu1, fd1, out, acc):
+        carried(
+            [
+                (
+                    w_out.at[pl.ds(h * half, half), pl.ds(p * hidden, hidden)],
+                    out.at[h, pl.ds(p * half, half), :],
+                )
+                for h in range(2)
+                for p in range(width // hidden)
+            ]
+        )
+
+
+def mlp_body(
+    core, rows, w_in, w_out, up0, dn0, fu0, fd0, up1, dn1, fu1, fd1, out,
+    own_in, own_out, near_in, near_out, far_in, far_out, act, sems,
+):
     width, hidden = w_in.shape
     half, deep = hidden // 2, width // 2
+    copy = pltpu.make_async_copy
+    first_in = copy(w_in, own_in, sems.at[0])
+    first_out = copy(w_out, own_out, sems.at[1])
+
+    def pieces(a, b):
+        ins = [
+            copy(a[0], near_in.at[0], sems.at[2]),
+            copy(a[1], near_in.at[1], sems.at[3]),
+            copy(a[2], far_in.at[0], sems.at[4]),
+            copy(a[3], far_in.at[1], sems.at[5]),
+        ]
+        outs = [
+            copy(b[0], near_out.at[0], sems.at[6]),
+            copy(b[1], near_out.at[1], sems.at[7]),
+            copy(b[2], far_out.at[0], sems.at[8]),
+            copy(b[3], far_out.at[1], sems.at[9]),
+        ]
+        return ins, outs
+
+    mine, other = (up0, dn0, fu0, fd0), (up1, dn1, fu1, fd1)
+    first_in.start()
+
+    @pl.when(core[0] == 0)
+    def _():
+        ins, outs = pieces(mine, other)
+        for c in ins:
+            c.start()
+        first_out.start()
+        for c in outs:
+            c.start()
+
+    @pl.when(core[0] != 0)
+    def _():
+        ins, outs = pieces(other, mine)
+        for c in ins:
+            c.start()
+        first_out.start()
+        for c in outs:
+            c.start()
+
+    ins, outs = pieces(mine, other)
 
     def hidden_of(product):
         return jnp.maximum(product, 0.0).astype(bf16)
 
-    first = hidden_of(jnp.dot(rows[...], w_in[...], preferred_element_type=f32))
-    acc[...] = jnp.dot(first, w_out[...], preferred_element_type=f32)
-
-    def pair(in_a, in_b, out_a, out_b):
+    first_in.wait()
+    act[:, :hidden] = hidden_of(jnp.dot(rows[...], own_in[...], preferred_element_type=f32))
+    pairs = (
+        (near_in.at[0, 0], near_in.at[0, 1], near_out.at[0, 0], near_out.at[0, 1]),
+        (near_in.at[1, 0], near_in.at[1, 1], near_out.at[1, 0], near_out.at[1, 1]),
+        (far_in.at[0], far_in.at[1], far_out.at[0], far_out.at[1]),
+    )
+    for k, (in_a, in_b, _, _) in enumerate(pairs):
+        for c in ins[k : k + 1] if k < 2 else ins[2:]:
+            c.wait()
         low = jnp.concatenate([in_a[:, :half], in_b[:, :half]], axis=1)
         high = jnp.concatenate([in_a[:, half:], in_b[:, half:]], axis=1)
-        act = hidden_of(
+        act[:, (k + 1) * hidden : (k + 2) * hidden] = hidden_of(
             jnp.dot(rows[:, :deep], low, preferred_element_type=f32)
             + jnp.dot(rows[:, deep:], high, preferred_element_type=f32)
         )
-        for p in range(width // hidden):
-            at = slice(p * half, (p + 1) * half)
-            panel = jnp.concatenate([out_a[at, :], out_b[at, :]], axis=0)
-            cols = slice(p * hidden, (p + 1) * hidden)
-            acc[:, cols] += jnp.dot(act, panel, preferred_element_type=f32)
-
-    def rest(a, b):
-        for k in range(2):
-            pair(a[k].at[0], a[k].at[1], b[k].at[0], b[k].at[1])
-        pair(a[2], a[3], b[2], b[3])
-
-    mine, other = (up0, dn0, fu0, fd0), (up1, dn1, fu1, fd1)
-
-    @pl.when(core[0] == 0)
-    def _():
-        rest(mine, other)
-
-    @pl.when(core[0] != 0)
-    def _():
-        rest(other, mine)
-
-    out[...] = acc[...].astype(bf16)
+    first_out.wait()
+    for c in outs:
+        c.wait()
+    for p in range(width // hidden):
+        at = slice(p * half, (p + 1) * half)
+        cols = slice(p * hidden, (p + 1) * hidden)
+        panel = jnp.concatenate(
+            [own_out[:, cols]] + [o[at, :] for pair in pairs for o in pair[2:]], axis=0
+        )
+        out[:, cols] = jnp.dot(act[...], panel, preferred_element_type=f32).astype(bf16)
+
+
+def normed_of(values, gain):
+    centred = values - jnp.mean(values, axis=-1, keepdims=True)
+    spread = jnp.mean(centred * centred, axis=-1, keepdims=True)
+    return centred * lax.rsqrt(spread + epsilon) * gain
+
+
+def before_body(facts, hidden, memory, gains, router, routes, mid, block):
+    rows, width = hidden.shape
+    states = hidden[...].astype(f32)
+    queries = normed_of(states, gains[0:1, :]).astype(bf16)
+    keys = memory[...]
+    heads = [slice(h * HEAD_DIM, (h + 1) * HEAD_DIM) for h in range(HEADS)]
+    scores = jnp.concatenate(
+        [
+            lax.dot_general(
+                queries[:, h], keys[:, h], (((1,), (1,)), ((), ())), preferred_element_type=f32
+            )
+            for h in heads
+        ],
+        axis=0,
+    ) * (1.0 / math.sqrt(HEAD_DIM))
+    key_at = lax.broadcasted_iota(jnp.int32, scores.shape, 1)
+    scores = jnp.where(key_at < facts[1], scores, -1e30)
+    raised = jnp.exp(scores - jnp.max(scores, axis=-1, keepdims=True))
+    weights = (raised / jnp.sum(raised, axis=-1, keepdims=True)).astype(bf16)
+    attended = jnp.concatenate(
+        [
+            jnp.dot(weights[i * rows : (i + 1) * rows], keys[:, h], preferred_element_type=f32)
+            for i, h in enumerate(heads)
+        ],
+        axis=1,
+    )
+    middle = states + jnp.where(facts[2] > 0, attended, 0.0)
+    mid[...] = middle
+    normed = normed_of(middle, gains[1:2, :]).astype(bf16)
+    block[:, :width] = normed
+    logits = lax.dot_general(
+        normed, router[...], (((1,), (1,)), ((), ())), preferred_element_type=f32
+    )
+    lane = lax.broadcasted_iota(jnp.int32, logits.shape, 1)
+    expert = lane % 8
+    real = (expert < 4) & (lane < 16)
+    logits = jnp.where(real, logits, -jnp.inf)
+    raised = jnp.exp(logits - jnp.max(logits, axis=-1, keepdims=True))
+    probs = raised / (0.5 * jnp.sum(raised, axis=-1, keepdims=True))
+    first = jnp.where(real & (expert == routes[:, 0:1]), 1.0, 0.0)
+    second = jnp.where(real & (expert == routes[:, 1:2]), 1.0, 0.0)
+    prob_first = 0.5 * jnp.sum(probs * first, axis=-1, keepdims=True)
+    prob_second = 0.5 * jnp.sum(probs * second, axis=-1, keepdims=True)
+    gates = (prob_first * first + prob_second * second) / (prob_first + prob_second)
+    token = lax.broadcasted_iota(jnp.int32, gates.shape, 0)
+    gates = jnp.where(token < facts[0], gates, 0.0)
+    upper = gates.astype(bf16).astype(f32)
+    block[:, width:] = jnp.where(lane < 8, upper, gates - upper).astype(bf16)
 
 
 def pack_body(slots, own, b1, b2, b3, rows, high, low):
@@ -168,64 +281,41 @@
     model_width = hidden.shape[2]
     capacity = 5 * tok_rows // 8
     decoder = lax.axis_index("y") >= chips // 2
-    positions = jnp.arange(tok_rows) % LEN
-    seq_index = jnp.arange(tok_rows) // LEN
-    is_valid = positions < lengths[0][seq_index]
-    key_mask = (positions < memory_lengths[0][seq_index]).astype(jnp.bfloat16)
-    arrived, arrived_mask = passed_along((memory[0], key_mask), "y", chips // 2)
+    is_valid = jnp.arange(tok_rows) < lengths[0, 0]
+    arrived, arrived_length = passed_along((memory[0], memory_lengths[0]), "y", chips // 2)
     core = lax.axis_index("core").astype(jnp.int32)[None]
     model_hidden = w_in.shape[2]
-    shared = kernel_call(
+    gain_rows = norm_gain[0]
+    router_rows = jnp.pad(router[0].T, ((0, 8 - experts), (0, 0)))
+    router_rows = jnp.pad(jnp.concatenate([router_rows, router_rows], axis=0), ((0, 112), (0, 0)))
+    whole = pl.BlockSpec(memory_space=pltpu.VMEM)
+    scalars = pl.BlockSpec(memory_space=pltpu.SMEM)
+    anywhere = pl.BlockSpec(memory_space=pl.ANY)
+    shared = pl.pallas_call(
         share_body,
-        jax.ShapeDtypeStruct((2, model_width // 2, model_hidden), bf16),
-        "svv",
-        (0, 3 << 20),
+        out_shape=jax.ShapeDtypeStruct((2, model_width // 2, model_hidden), bf16),
+        in_specs=[scalars] + [anywhere] * 2,
+        out_specs=anywhere,
+        scratch_shapes=[pltpu.SemaphoreType.DMA((2 * model_width // model_hidden,))],
+        cost_estimate=pl.CostEstimate(flops=0, bytes_accessed=2 << 20, transcendentals=0),
     )(core, w_in[0], w_out[0])
     line = ("z4", "zl")
     up, down = turned(shared, line, -1), turned(shared, line, 1)
     far_up, far_down = turned(up[0], line, -1), turned(down[1], line, 1)
     mine = (up, down, far_up, far_down)
     other = [turned(piece, "core", 1) for piece in mine]
-    states = hidden[0].astype(jnp.float32)
-    gain_rows = norm_gain[0]
-    seq_count = tok_rows // LEN
-    score_scale = 1.0 / math.sqrt(HEAD_DIM)
-    queries = (
-        layer_norm(states, gain_rows[0])
-        .astype(jnp.bfloat16)
-        .reshape(seq_count, LEN, HEADS, HEAD_DIM)
-    )
-    key_rows = arrived.reshape(seq_count, LEN, HEADS, HEAD_DIM)
-    scores = (
-        jnp.einsum("bqhd,bkhd->bhqk", queries, key_rows, preferred_element_type=jnp.float32)
-        * score_scale
-    )
-    allowed = arrived_mask.reshape(seq_count, 1, 1, LEN) > 0.5
-    scores = jnp.where(allowed, scores, -1e30)
-    weights = jax.nn.softmax(scores, axis=-1).astype(jnp.bfloat16)
-    attended = jnp.einsum(
-        "bhqk,bkhd->bqhd", weights, key_rows, preferred_element_type=jnp.float32
-    ).reshape(tok_rows, model_width)
-    mid_states = states + jnp.where(decoder, attended, 0.0)
-    normed = layer_norm(mid_states, gain_rows[1]).astype(jnp.bfloat16)
-    router_probs = jax.nn.softmax(
-        jnp.dot(normed, router[0], preferred_element_type=jnp.float32), axis=-1
-    )
-    expert_ids = jnp.arange(experts)
-    first_hot = (routes[0][:, 0:1] == expert_ids).astype(jnp.float32)
-    second = (routes[0][:, 1:2] == expert_ids).astype(jnp.float32)
-    prob_first = jnp.sum(router_probs * first_hot, axis=-1, keepdims=True)
-    prob_second = jnp.sum(router_probs * second, axis=-1, keepdims=True)
-    prob_total = prob_first + prob_second
-    gate_rows = (prob_first * first_hot + prob_second * second) / prob_total
-    combine = gate_rows * (first_hot + second) * is_valid[:, None].astype(f32)
-    combine_high = combine.astype(bf16)
-    combine_low = (combine - lax.reduce_precision(combine, 8, 7)).astype(bf16)
-    pad = jnp.zeros((tok_rows, 8 - experts), bf16)
-    block = jnp.concatenate(
-        [normed, combine_high, pad, combine_low, pad, jnp.zeros((tok_rows, 112), bf16)], axis=1
-    )
-    visitors = [turned(block, "z4", k) for k in (1, 2, 3)]
+    facts = jnp.stack([lengths[0, 0], arrived_length[0], decoder.astype(jnp.int32)])
+    mid_states, block = kernel_call(
+        before_body,
+        (
+            jax.ShapeDtypeStruct((tok_rows, model_width), f32),
+            jax.ShapeDtypeStruct((tok_rows, model_width + 128), bf16),
+        ),
+        "svvvvv",
+        (4 * tok_rows * LEN * model_width, 1 << 20),
+    )(facts, hidden[0], arrived, gain_rows, router_rows, routes[0])
+    order = (1, 3, 2)
+    visitors = [turned(block, "z4", k) for k in order]
     slots = 4 * capacity
     lanes = experts * slots
     packed, gates_high, gates_low = kernel_call(
@@ -239,15 +329,24 @@
         (2 * lanes * 4 * tok_rows * model_width, 2 << 20),
     )(block, *visitors)
     rows = lax.all_to_all(packed, "x", split_axis=0, concat_axis=0, tiled=True)
-    whole = pl.BlockSpec(memory_space=pltpu.VMEM)
+    deep, near = model_width // 2, (2, 2, model_width // 2, model_hidden)
     partial_out = pl.pallas_call(
         mlp_body,
         out_shape=jax.ShapeDtypeStruct((lanes, model_width), bf16),
-        in_specs=[pl.BlockSpec(memory_space=pltpu.SMEM)] + [whole] * 11,
+        in_specs=[scalars, whole] + [anywhere] * 10,
         out_specs=whole,
-        scratch_shapes=[pltpu.VMEM((lanes, model_width), f32)],
+        scratch_shapes=[
+            pltpu.VMEM((model_width, model_hidden), bf16),
+            pltpu.VMEM((model_hidden, model_width), bf16),
+            pltpu.VMEM(near, bf16),
+            pltpu.VMEM(near, bf16),
+            pltpu.VMEM((2, deep, model_hidden), bf16),
+            pltpu.VMEM((2, deep, model_hidden), bf16),
+            pltpu.VMEM((lanes, 4 * model_hidden), bf16),
+            pltpu.SemaphoreType.DMA((10,)),
+        ],
         cost_estimate=pl.CostEstimate(
-            flops=4 * lanes * model_width * 1024, bytes_accessed=11 << 20, transcendentals=0
+            flops=16 * lanes * model_width * model_hidden, bytes_accessed=11 << 20, transcendentals=0
         ),
         compiler_params=pltpu.CompilerParams(vmem_limit_bytes=40 << 20),
     )(core, rows, w_in[0], w_out[0], *mine, *other)
@@ -260,7 +359,7 @@
         (4 * lanes * 4 * tok_rows * model_width, 2 << 20),
     )(returned, gates_high, gates_low)
     moe_out = own_part
-    for k, part in zip((1, 2, 3), parts):
+    for k, part in zip(order, parts):
         moe_out = moe_out + turned(part, "z4", -k).astype(f32)
     layer_out = (mid_states + moe_out).astype(jnp.bfloat16)
     final_normed = layer_norm(layer_out.astype(jnp.float32), gain_rows[2]).astype(jnp.bfloat16)

time: 217 us -> 231 us (1.065)
  Pallas kernels: 8.96 us -> 41.9 us
  local copies, waits for them, and re-layouts: 17.6 us -> 8.72 us
  starting transfers between devices: 76.9 us -> 84.9 us
  other arithmetic: 11.1 us -> 3.88 us
  matrix products: 6.15 us -> 0.61 us
  blocking collectives: 60.5 us -> 56.2 us
    pallas_call x1 -> x2, Pallas kernels: 0.07 us -> 35 us  [the longest x1 33 us: local(): pl.pallas_call(share_body, out_shape=jax.ShapeDtypeStruct((2, model_width...]
    ppermute x14, starting transfers between devices: 65.6 us -> 74.2 us  [turned(): lax.ppermute(block, axis, [(i, (i + distance) % count) for i in range(cou...]
    dot_general x3 -> x0, matrix products: 5.54 us -> none  [the longest x1 2.32 us: local(): jnp.dot(normed, router[0], preferred_element_type=jnp.float32)]
    convert_element_type x4 -> x0, other arithmetic: 3.92 us -> none  [the longest x1 1.46 us: local(): normed = layer_norm(mid_states, gain_rows[1]).astype(jnp.bfloat16)]
    all_to_all x2, blocking collectives: 41.1 us -> 37.4 us  [local(): lax.all_to_all(spread_out, axes, split_axis=0, concat_axis=0, tiled=True)]
    unnamed x49 -> x35, local copies, waits for them, and re-layouts: 7.85 us -> 4.24 us
  transfers between devices with their start and end apart: 17 -> 17, of which waited for: 5 -> 6; matrix products, arithmetic and copies ran while one was open for 11% -> 2% of each run, Pallas kernels for 0% -> 1%
where the time goes in v3:
time: 231 us; the launch traced here: 230 us
  starting transfers between devices  84.9 us (37%)
  blocking collectives  56.2 us (24%)
  Pallas kernels  41.9 us (18%)
  waiting for transfers between devices  29.6 us (13%)
  local copies, waits for them, and re-layouts  8.72 us (4%)
  between operations  4.19 us (2%)
  other arithmetic  3.88 us (2%)
    ppermute x14, starting transfers between devices, turned(): lax.ppermute(block, axis, [(i, (i + distance) % count) for i in range(cou...  74.2 us
    all_to_all x2, blocking collectives, local(): lax.all_to_all(spread_out, axes, split_axis=0, concat_axis=0, tiled=True)  37.4 us
    pallas_call x1, Pallas kernels, local(): pl.pallas_call(share_body, out_shape=jax.ShapeDtypeStruct((2, model_width...  33 us
    ppermute x14, waiting for transfers between devices, turned(): lax.ppermute(block, axis, [(i, (i + distance) % count) for i in range(cou...  23.1 us
    all_to_all x1, blocking collectives, local(): lax.all_to_all(partial_out, 'x', split_axis=0, concat_axis=0, tiled=True)  18.8 us
    ppermute x2, starting transfers between devices, passed_along(): return lax.ppermute(block, axis, route)  6.64 us
    all_to_all x1, waiting for transfers between devices, local(): rows = lax.all_to_all(packed, 'x', split_axis=0, concat_axis=0, tiled=True)  6.07 us
    pallas_call x1, Pallas kernels, local(): pl.pallas_call(mlp_body, out_shape=jax.ShapeDtypeStruct((lanes, model_wid...  5.39 us
  transfers between devices with their start and end apart: 17, of which 6 were waited for; matrix products, arithmetic and copies ran while one was open for 2% of the time, Pallas kernels for 1%

profile of v3, /device:TPU:1, one launch (start us, length us, event | category | flops | bytes accessed | tf_op | source)
XLA Modules:
  0.0 230.1 jit_solution(13519084625002037659)
XLA Ops:
  0.7 33.0 %shard_map.133 = bf16[2,1024,256]{2,1,0:T(8,128)(2,1)} custom-call(s32[1]{0:T(128)} %bitcast.8.core, bf16[2048,256]{1,0:T(8,128)(2,1)} %bitcast.53, bf16[256,2048]{1,0:T(8,128)(2,1)} %bitcast.55), custom_call_target="tpu_custom_call" | custom-call | bytes 2097152 | tf_op jit(solution)/shard_map/pallas_call | solution.py:294
  33.7 12.0 %collective-permute-start.5 = (bf16[2,1024,256]{2,1,0:T(8,128)(2,1)}, bf16[2,1024,256]{2,1,0:T(8,128)(2,1)}, u32[]{:S(2)}, u32[]{:S(2)}) collective-permute-start(bf16[2,1024,256]{2,1,0:T(8,128)(2,1)} %shard_map.133), channel_id=1, source_target_pairs={{0,15},{1,0},{2,1},{3,2},{4,3},{5,4},{6,5},{7,6},{8,7},{9,8},{10,9... | collective-permute-start | bytes 3145736 | tf_op jit(solution)/shard_map/ppermute | solution.py:29
  45.7 1.9 collective-permute-start.6
  47.6 5.4 %collective-permute-start = (s32[1]{0:T(128)}, s32[1]{0:T(128)}, u32[]{:S(2)}, u32[]{:S(2)}) collective-permute-start(s32[1]{0:T(128)} %bitcast.1), channel_id=1, source_target_pairs={{0,256},{128,384},{1,257},{129,385},{2,258},{130,386},{3,259},{131... | collective-permute-start | bytes 20 | tf_op jit(solution)/shard_map/ppermute | solution.py:24
  56.2 2.0 shard_map.131
  58.2 1.9 collective-permute-start.2
  60.1 7.3 %collective-permute-start.3 = (bf16[32,2176]{1,0:T(8,128)(2,1)S(1)}, bf16[32,2176]{1,0:T(8,128)(2,1)S(1)}, u32[]{:S(2)}, u32[]{:S(2)}) collective-permute-start(bf16[32,2176]{1,0:T(8,128)(2,1)S(1)} %get-tuple-element.13.own), channel_id=1, source_target_pairs={{0,12},{4,0},{8,4},{12,8},{1,13},{5,1},{9,5},{13,9},{2,14},{6,2},{... | collective-permute-start | bytes 417800 | tf_op jit(solution)/shard_map/ppermute | solution.py:29
  67.4 7.7 %collective-permute-start.4 = (bf16[32,2176]{1,0:T(8,128)(2,1)S(1)}, bf16[32,2176]{1,0:T(8,128)(2,1)S(1)}, u32[]{:S(2)}, u32[]{:S(2)}) collective-permute-start(bf16[32,2176]{1,0:T(8,128)(2,1)S(1)} %get-tuple-element.13.own), channel_id=1, source_target_pairs={{0,8},{4,12},{8,0},{12,4},{1,9},{5,13},{9,1},{13,5},{2,10},{6,14},... | collective-permute-start | bytes 417800 | tf_op jit(solution)/shard_map/ppermute | solution.py:29
  77.3 5.5 %collective-permute-start.7 = (bf16[1024,256]{1,0:T(8,128)(2,1)}, bf16[1024,256]{1,0:T(8,128)(2,1)}, u32[]{:S(2)}, u32[]{:S(2)}) collective-permute-start(bf16[1024,256]{1,0:T(8,128)(2,1)} %slice_bitcast_fusion.1), channel_id=1, source_target_pairs={{0,15},{1,0},{2,1},{3,2},{4,3},{5,4},{6,5},{7,6},{8,7},{9,8},{10,9... | collective-permute-start | bytes 1572872 | tf_op jit(solution)/shard_map/ppermute | solution.py:29
  82.7 16.2 %collective-permute-start.9 = (bf16[2,1024,256]{2,1,0:T(8,128)(2,1)}, bf16[2,1024,256]{2,1,0:T(8,128)(2,1)}, u32[]{:S(2)}, u32[]{:S(2)}) collective-permute-start(bf16[2,1024,256]{2,1,0:T(8,128)(2,1)} %collective-permute-done.5.up0), channel_id=1, source_target_pairs={{0,64},{64,0},{1,65},{65,1},{2,66},{66,2},{3,67},{67,3},{4,68},{68... | collective-permute-start | bytes 3145736 | tf_op jit(solution)/shard_map/ppermute | solution.py:29
  102.7 1.9 collective-permute-start.8
  107.3 4.0 %all-to-all-start = ((bf16[4,80,2048]{2,1,0:T(8,128)(2,1)}), bf16[4,80,2048]{2,1,0:T(8,128)(2,1)S(1)}, u32[]{:S(2)}, u32[]{:S(2)}) async-start(bf16[4,80,2048]{2,1,0:T(8,128)(2,1)} %bitcast.57), calls=%async_computation | async-start | bytes 2621440 | tf_op jit(solution)/shard_map/all_to_all | solution.py:331
  111.3 2.7 %collective-permute-start.11 = (bf16[1024,256]{1,0:T(8,128)(2,1)}, bf16[1024,256]{1,0:T(8,128)(2,1)}, u32[]{:S(2)}, u32[]{:S(2)}) collective-permute-start(bf16[1024,256]{1,0:T(8,128)(2,1)} %collective-permute-done.7.fu0), channel_id=1, source_target_pairs={{0,64},{64,0},{1,65},{65,1},{2,66},{66,2},{3,67},{67,3},{4,68},{68... | collective-permute-start | bytes 1572872 | tf_op jit(solution)/shard_map/ppermute | solution.py:29
  114.0 5.2 %collective-permute-done.8.fd0 = bf16[1024,256]{1,0:T(8,128)(2,1)} collective-permute-done((bf16[1024,256]{1,0:T(8,128)(2,1)}, bf16[1024,256]{1,0:T(8,128)(2,1)}, u32[]{:S(2)}, u32[]{:S(2)}) %collective-permute-start.8) | collective-permute-done | bytes 524320 | tf_op jit(solution)/shard_map/ppermute | solution.py:29
  119.2 3.2 %collective-permute-start.12 = (bf16[1024,256]{1,0:T(8,128)(2,1)}, bf16[1024,256]{1,0:T(8,128)(2,1)}, u32[]{:S(2)}, u32[]{:S(2)}) collective-permute-start(bf16[1024,256]{1,0:T(8,128)(2,1)} %collective-permute-done.8.fd0), channel_id=1, source_target_pairs={{0,64},{64,0},{1,65},{65,1},{2,66},{66,2},{3,67},{67,3},{4,68},{68... | collective-permute-start | bytes 1572872 | tf_op jit(solution)/shard_map/ppermute | solution.py:29
  122.4 6.1 %all-to-all-done = bf16[4,80,2048]{2,1,0:T(8,128)(2,1)S(1)} async-done(((bf16[4,80,2048]{2,1,0:T(8,128)(2,1)}), bf16[4,80,2048]{2,1,0:T(8,128)(2,1)S(1)}, u32[]{:S(2)}, u32[]{:S(2)}) %all-to-all-start) | async-done | bytes 1310752 | tf_op jit(solution)/shard_map/all_to_all | solution.py:331
  131.0 5.4 %shard_map.134 = bf16[320,2048]{1,0:T(8,128)(2,1)S(1)} custom-call(s32[1]{0:T(128)} %bitcast.8.core, bf16[320,2048]{1,0:T(8,128)(2,1)S(1)} %bitcast.51, bf16[2048,256]{1,0:T(8,128)(2,1)S(1)} %bitcast.54, bf16[256,2048]{1,0:T(8,128)(2,1)S(1)} %bitcast.56, bf16[2,1024,256]{2,1,0:T(8,128)(2,1)} %collective-permute-done.5.up0, ...), custom_call_target="tpu_custom_call" | custom-call | flops 2684354560 | bytes 11534336 | tf_op jit(solution)/shard_map/pallas_call | solution.py:333
  136.4 18.8 %all_to_all.34 = bf16[4,80,2048]{2,1,0:T(8,128)(2,1)S(1)} all-to-all(bf16[4,80,2048]{2,1,0:T(8,128)(2,1)S(1)} %bitcast.52), channel_id=1, replica_groups=mesh['y'=4,'core'=2,'x'=4,'z4'=4,'zl'=4] {'x'}, dimensions={0} | all-to-all | bytes 2621440 | tf_op jit(solution)/shard_map/all_to_all | solution.py:353
  156.0 1.9 collective-permute-start.15
  157.9 8.2 %collective-permute-start.14 = (bf16[32,2048]{1,0:T(8,128)(2,1)S(1)}, bf16[32,2048]{1,0:T(8,128)(2,1)S(1)}, u32[]{:S(2)}, u32[]{:S(2)}) collective-permute-start(bf16[32,2048]{1,0:T(8,128)(2,1)S(1)} %get-tuple-element.19), channel_id=1, source_target_pairs={{0,4},{4,8},{8,12},{12,0},{1,5},{5,9},{9,13},{13,1},{2,6},{6,10},{... | collective-permute-start | bytes 393224 | tf_op jit(solution)/shard_map/ppermute | solution.py:29
  168.4 8.1 %collective-permute-done.15 = bf16[32,2048]{1,0:T(8,128)(2,1)S(1)} collective-permute-done((bf16[32,2048]{1,0:T(8,128)(2,1)S(1)}, bf16[32,2048]{1,0:T(8,128)(2,1)S(1)}, u32[]{:S(2)}, u32[]{:S(2)}) %collective-permute-start.15) | collective-permute-done | bytes 131104 | tf_op jit(solution)/shard_map/ppermute | solution.py:29
  176.5 9.5 %collective-permute-done.13 = bf16[32,2048]{1,0:T(8,128)(2,1)S(1)} collective-permute-done((bf16[32,2048]{1,0:T(8,128)(2,1)S(1)}, bf16[32,2048]{1,0:T(8,128)(2,1)S(1)}, u32[]{:S(2)}, u32[]{:S(2)}) %collective-permute-start.13) | collective-permute-done | bytes 131104 | tf_op jit(solution)/shard_map/ppermute | solution.py:29
  189.5 10.0 %all_to_all.35 = f32[16,1,128]{2,1,0:T(1,128)S(1)} all-to-all(f32[16,1,128]{2,1,0:T(1,128)S(1)} %broadcast_in_dim.17), channel_id=1, replica_groups=mesh['y'=4,'core'=2,'x'=4,'z4'=4,'zl'=4] {'x','zl'}, dimensions={0} | all-to-all | bytes 16384 | tf_op jit(solution)/shard_map/all_to_all | solution.py:379
  199.6 27.4 %all_to_all.36 = f32[32,1,128]{2,1,0:T(1,128)S(1)} all-to-all(f32[32,1,128]{2,1,0:T(1,128)S(1)} %broadcast_in_dim.18), channel_id=1, replica_groups=mesh['y'=4,'core'=2,'x'=4,'z4'=4,'zl'=4] {'y','core','z4'}, dimensions={0} | all-to-all | bytes 32768 | tf_op jit(solution)/shard_map/all_to_all | solution.py:379
  (80 shorter events, 20.6 us)
Async XLA Ops:
  0.6 185.8 %copy-start = (bf16[1,2048,512]{2,1,0:T(8,128)(2,1)S(1)}, bf16[1,2048,512]{2,1,0:T(8,128)(2,1)}, u32[]{:S(2)}) copy-start(bf16[1,2048,512]{2,1,0:T(8,128)(2,1)} %param.22) | copy-start | bytes 6291460
  0.6 52.3 %copy-start.15 = (bf16[1,32,2048]{2,1,0:T(8,128)(2,1)S(1)}, bf16[1,32,2048]{2,1,0:T(8,128)(2,1)}, u32[]{:S(2)}) copy-start(bf16[1,32,2048]{2,1,0:T(8,128)(2,1)} %param.14) | copy-start | bytes 393220
  0.7 53.6 %copy-start.12 = (bf16[1,2048,4]{1,2,0:T(4,128)(2,1)S(1)}, bf16[1,2048,4]{1,2,0:T(4,128)(2,1)}, u32[]{:S(2)}) copy-start(bf16[1,2048,4]{1,2,0:T(4,128)(2,1)} %param.19) | copy-start | bytes 49156
  0.7 54.4 %copy-start.11 = (f32[1,3,2048]{2,0,1:T(1,128)S(1)}, f32[1,3,2048]{2,0,1:T(1,128)}, u32[]{:S(2)}) copy-start(f32[1,3,2048]{2,0,1:T(1,128)} %param.18) | copy-start | bytes 73732
  0.7 54.4 %copy-start.13 = (s32[1,32,2]{1,2,0:T(2,128)S(1)}, s32[1,32,2]{1,2,0:T(2,128)}, u32[]{:S(2)}) copy-start(s32[1,32,2]{1,2,0:T(2,128)} %param.17) | copy-start | bytes 772
  0.7 55.5 %copy-start.6 = (bf16[1,32,2048]{2,1,0:T(8,128)(2,1)S(1)}, bf16[1,32,2048]{2,1,0:T(8,128)(2,1)}, u32[]{:S(2)}) copy-start(bf16[1,32,2048]{2,1,0:T(8,128)(2,1)} %param.13) | copy-start | bytes 393220
  33.7 41.7 %collective-permute-start.5 = (bf16[2,1024,256]{2,1,0:T(8,128)(2,1)}, bf16[2,1024,256]{2,1,0:T(8,128)(2,1)}, u32[]{:S(2)}, u32[]{:S(2)}) collective-permute-start(bf16[2,1024,256]{2,1,0:T(8,128)(2,1)} %shard_map.133), channel_id=1, source_target_pairs={{0,15},{1,0},{2,1},{3,2},{4,3},{5,4},{6,5},{7,6},{8,7},{9,8},{10,9... | collective-permute-start | bytes 3145736 | tf_op jit(solution)/shard_map/ppermute | solution.py:29
  45.7 37.0 %collective-permute-start.6 = (bf16[2,1024,256]{2,1,0:T(8,128)(2,1)}, bf16[2,1024,256]{2,1,0:T(8,128)(2,1)}, u32[]{:S(2)}, u32[]{:S(2)}) collective-permute-start(bf16[2,1024,256]{2,1,0:T(8,128)(2,1)} %shard_map.133), channel_id=1, source_target_pairs={{0,1},{1,2},{2,3},{3,4},{4,5},{5,6},{6,7},{7,8},{8,9},{9,10},{10,1... | collective-permute-start | bytes 3145736 | tf_op jit(solution)/shard_map/ppermute | solution.py:29
  47.6 7.5 %collective-permute-start = (s32[1]{0:T(128)}, s32[1]{0:T(128)}, u32[]{:S(2)}, u32[]{:S(2)}) collective-permute-start(s32[1]{0:T(128)} %bitcast.1), channel_id=1, source_target_pairs={{0,256},{128,384},{1,257},{129,385},{2,258},{130,386},{3,259},{131... | collective-permute-start | bytes 20 | tf_op jit(solution)/shard_map/ppermute | solution.py:24
  53.0 3.2 %collective-permute-start.1 = (bf16[32,2048]{1,0:T(8,128)(2,1)S(1)}, bf16[32,2048]{1,0:T(8,128)(2,1)S(1)}, u32[]{:S(2)}, u32[]{:S(2)}) collective-permute-start(bf16[32,2048]{1,0:T(8,128)(2,1)S(1)} %bitcast.67), channel_id=1, source_target_pairs={{0,256},{128,384},{1,257},{129,385},{2,258},{130,386},{3,259},{131... | collective-permute-start | bytes 393224 | tf_op jit(solution)/shard_map/ppermute | solution.py:24
  58.2 42.6 %collective-permute-start.2 = (bf16[32,2176]{1,0:T(8,128)(2,1)S(1)}, bf16[32,2176]{1,0:T(8,128)(2,1)S(1)}, u32[]{:S(2)}, u32[]{:S(2)}) collective-permute-start(bf16[32,2176]{1,0:T(8,128)(2,1)S(1)} %get-tuple-element.13.own), channel_id=1, source_target_pairs={{0,4},{4,8},{8,12},{12,0},{1,5},{5,9},{9,13},{13,1},{2,6},{6,10},{... | collective-permute-start | bytes 417800 | tf_op jit(solution)/shard_map/ppermute | solution.py:29
  60.1 42.6 %collective-permute-start.3 = (bf16[32,2176]{1,0:T(8,128)(2,1)S(1)}, bf16[32,2176]{1,0:T(8,128)(2,1)S(1)}, u32[]{:S(2)}, u32[]{:S(2)}) collective-permute-start(bf16[32,2176]{1,0:T(8,128)(2,1)S(1)} %get-tuple-element.13.own), channel_id=1, source_target_pairs={{0,12},{4,0},{8,4},{12,8},{1,13},{5,1},{9,5},{13,9},{2,14},{6,2},{... | collective-permute-start | bytes 417800 | tf_op jit(solution)/shard_map/ppermute | solution.py:29
  67.4 37.3 %collective-permute-start.4 = (bf16[32,2176]{1,0:T(8,128)(2,1)S(1)}, bf16[32,2176]{1,0:T(8,128)(2,1)S(1)}, u32[]{:S(2)}, u32[]{:S(2)}) collective-permute-start(bf16[32,2176]{1,0:T(8,128)(2,1)S(1)} %get-tuple-element.13.own), channel_id=1, source_target_pairs={{0,8},{4,12},{8,0},{12,4},{1,9},{5,13},{9,1},{13,5},{2,10},{6,14},... | collective-permute-start | bytes 417800 | tf_op jit(solution)/shard_map/ppermute | solution.py:29
  77.3 34.0 %collective-permute-start.7 = (bf16[1024,256]{1,0:T(8,128)(2,1)}, bf16[1024,256]{1,0:T(8,128)(2,1)}, u32[]{:S(2)}, u32[]{:S(2)}) collective-permute-start(bf16[1024,256]{1,0:T(8,128)(2,1)} %slice_bitcast_fusion.1), channel_id=1, source_target_pairs={{0,15},{1,0},{2,1},{3,2},{4,3},{5,4},{6,5},{7,6},{8,7},{9,8},{10,9... | collective-permute-start | bytes 1572872 | tf_op jit(solution)/shard_map/ppermute | solution.py:29
  82.7 45.7 %collective-permute-start.9 = (bf16[2,1024,256]{2,1,0:T(8,128)(2,1)}, bf16[2,1024,256]{2,1,0:T(8,128)(2,1)}, u32[]{:S(2)}, u32[]{:S(2)}) collective-permute-start(bf16[2,1024,256]{2,1,0:T(8,128)(2,1)} %collective-permute-done.5.up0), channel_id=1, source_target_pairs={{0,64},{64,0},{1,65},{65,1},{2,66},{66,2},{3,67},{67,3},{4,68},{68... | collective-permute-start | bytes 3145736 | tf_op jit(solution)/shard_map/ppermute | solution.py:29
  100.8 27.7 %collective-permute-start.10 = (bf16[2,1024,256]{2,1,0:T(8,128)(2,1)}, bf16[2,1024,256]{2,1,0:T(8,128)(2,1)}, u32[]{:S(2)}, u32[]{:S(2)}) collective-permute-start(bf16[2,1024,256]{2,1,0:T(8,128)(2,1)} %collective-permute-done.6.dn0), channel_id=1, source_target_pairs={{0,64},{64,0},{1,65},{65,1},{2,66},{66,2},{3,67},{67,3},{4,68},{68... | collective-permute-start | bytes 3145736 | tf_op jit(solution)/shard_map/ppermute | solution.py:29
  102.7 16.4 %collective-permute-start.8 = (bf16[1024,256]{1,0:T(8,128)(2,1)}, bf16[1024,256]{1,0:T(8,128)(2,1)}, u32[]{:S(2)}, u32[]{:S(2)}) collective-permute-start(bf16[1024,256]{1,0:T(8,128)(2,1)} %slice_bitcast_fusion), channel_id=1, source_target_pairs={{0,1},{1,2},{2,3},{3,4},{4,5},{5,6},{6,7},{7,8},{8,9},{9,10},{10,1... | collective-permute-start | bytes 1572872 | tf_op jit(solution)/shard_map/ppermute | solution.py:29
  107.3 21.2 %all-to-all-start = ((bf16[4,80,2048]{2,1,0:T(8,128)(2,1)}), bf16[4,80,2048]{2,1,0:T(8,128)(2,1)S(1)}, u32[]{:S(2)}, u32[]{:S(2)}) async-start(bf16[4,80,2048]{2,1,0:T(8,128)(2,1)} %bitcast.57), calls=%async_computation | async-start | bytes 2621440 | tf_op jit(solution)/shard_map/all_to_all | solution.py:331
  111.3 17.2 %collective-permute-start.11 = (bf16[1024,256]{1,0:T(8,128)(2,1)}, bf16[1024,256]{1,0:T(8,128)(2,1)}, u32[]{:S(2)}, u32[]{:S(2)}) collective-permute-start(bf16[1024,256]{1,0:T(8,128)(2,1)} %collective-permute-done.7.fu0), channel_id=1, source_target_pairs={{0,64},{64,0},{1,65},{65,1},{2,66},{66,2},{3,67},{67,3},{4,68},{68... | collective-permute-start | bytes 1572872 | tf_op jit(solution)/shard_map/ppermute | solution.py:29
  119.2 9.3 %collective-permute-start.12 = (bf16[1024,256]{1,0:T(8,128)(2,1)}, bf16[1024,256]{1,0:T(8,128)(2,1)}, u32[]{:S(2)}, u32[]{:S(2)}) collective-permute-start(bf16[1024,256]{1,0:T(8,128)(2,1)} %collective-permute-done.8.fd0), channel_id=1, source_target_pairs={{0,64},{64,0},{1,65},{65,1},{2,66},{66,2},{3,67},{67,3},{4,68},{68... | collective-permute-start | bytes 1572872 | tf_op jit(solution)/shard_map/ppermute | solution.py:29
  136.4 50.1 %slice-start = ((f32[1,3,2048]{2,0,1:T(1,128)}), f32[1,1,2048]{2,0,1:T(1,128)S(1)}, s32[]{:S(2)}) async-start(f32[1,3,2048]{2,0,1:T(1,128)} %param.18), calls=%async_computation.4 | async-start | bytes 16384 | tf_op jit(solution)/shard_map/slice | solution.py:365
  156.0 20.5 %collective-permute-start.15 = (bf16[32,2048]{1,0:T(8,128)(2,1)S(1)}, bf16[32,2048]{1,0:T(8,128)(2,1)S(1)}, u32[]{:S(2)}, u32[]{:S(2)}) collective-permute-start(bf16[32,2048]{1,0:T(8,128)(2,1)S(1)} %get-tuple-element.20), channel_id=1, source_target_pairs={{0,8},{4,12},{8,0},{12,4},{1,9},{5,13},{9,1},{13,5},{2,10},{6,14},... | collective-permute-start | bytes 393224 | tf_op jit(solution)/shard_map/ppermute | solution.py:29
  157.9 18.6 %collective-permute-start.14 = (bf16[32,2048]{1,0:T(8,128)(2,1)S(1)}, bf16[32,2048]{1,0:T(8,128)(2,1)S(1)}, u32[]{:S(2)}, u32[]{:S(2)}) collective-permute-start(bf16[32,2048]{1,0:T(8,128)(2,1)S(1)} %get-tuple-element.19), channel_id=1, source_target_pairs={{0,4},{4,8},{8,12},{12,0},{1,5},{5,9},{9,13},{13,1},{2,6},{6,10},{... | collective-permute-start | bytes 393224 | tf_op jit(solution)/shard_map/ppermute | solution.py:29
  166.2 19.8 %collective-permute-start.13 = (bf16[32,2048]{1,0:T(8,128)(2,1)S(1)}, bf16[32,2048]{1,0:T(8,128)(2,1)S(1)}, u32[]{:S(2)}, u32[]{:S(2)}) collective-permute-start(bf16[32,2048]{1,0:T(8,128)(2,1)S(1)} %get-tuple-element.18), channel_id=1, source_target_pairs={{0,12},{4,0},{8,4},{12,8},{1,13},{5,1},{9,5},{13,9},{2,14},{6,2},{... | collective-permute-start | bytes 393224 | tf_op jit(solution)/shard_map/ppermute | solution.py:29
  (11 other events, 268.6 us)

commit v4 on v3

--- a/solution.py
+++ b/solution.py
@@ -48,44 +48,31 @@
     )
 
 
-def share_body(core, w_in, w_out, out, sems):
+def share_body(core, w_in, w_out, out, block_in, block_out, sem):
     width, hidden = w_in.shape
     half, deep = hidden // 2, width // 2
 
-    def carried(pairs):
-        copies = [
-            pltpu.make_async_copy(src, dst, sems.at[k]) for k, (src, dst) in enumerate(pairs)
-        ]
-        for copy in copies:
-            copy.start()
-        for copy in copies:
-            copy.wait()
-
     @pl.when(core[0] == 0)
     def _():
-        carried(
-            [
-                (
-                    w_in.at[pl.ds(d * deep, deep), pl.ds(h * half, half)],
-                    out.at[h, :, pl.ds(d * half, half)],
-                )
-                for h in range(2)
-                for d in range(2)
-            ]
-        )
+        copy = pltpu.make_async_copy(w_in, block_in, sem)
+        copy.start()
+        copy.wait()
+        for h in range(2):
+            for d in range(2):
+                out[h, :, d * half : (d + 1) * half] = block_in[
+                    d * deep : (d + 1) * deep, h * half : (h + 1) * half
+                ]
 
     @pl.when(core[0] != 0)
     def _():
-        carried(
-            [
-                (
-                    w_out.at[pl.ds(h * half, half), pl.ds(p * hidden, hidden)],
-                    out.at[h, pl.ds(p * half, half), :],
-                )
-                for h in range(2)
-                for p in range(width // hidden)
-            ]
-        )
+        copy = pltpu.make_async_copy(w_out, block_out, sem)
+        copy.start()
+        copy.wait()
+        for h in range(2):
+            for p in range(width // hidden):
+                out[h, p * half : (p + 1) * half, :] = block_out[
+                    h * half : (h + 1) * half, p * hidden : (p + 1) * hidden
+                ]
 
 
 def mlp_body(
@@ -282,10 +269,10 @@
     capacity = 5 * tok_rows // 8
     decoder = lax.axis_index("y") >= chips // 2
     is_valid = jnp.arange(tok_rows) < lengths[0, 0]
-    arrived, arrived_length = passed_along((memory[0], memory_lengths[0]), "y", chips // 2)
     core = lax.axis_index("core").astype(jnp.int32)[None]
     model_hidden = w_in.shape[2]
     gain_rows = norm_gain[0]
+    arrived, arrived_length = passed_along((memory[0], memory_lengths[0]), "y", chips // 2)
     router_rows = jnp.pad(router[0].T, ((0, 8 - experts), (0, 0)))
     router_rows = jnp.pad(jnp.concatenate([router_rows, router_rows], axis=0), ((0, 112), (0, 0)))
     whole = pl.BlockSpec(memory_space=pltpu.VMEM)
@@ -295,9 +282,14 @@
         share_body,
         out_shape=jax.ShapeDtypeStruct((2, model_width // 2, model_hidden), bf16),
         in_specs=[scalars] + [anywhere] * 2,
-        out_specs=anywhere,
-        scratch_shapes=[pltpu.SemaphoreType.DMA((2 * model_width // model_hidden,))],
+        out_specs=whole,
+        scratch_shapes=[
+            pltpu.VMEM((model_width, model_hidden), bf16),
+            pltpu.VMEM((model_hidden, model_width), bf16),
+            pltpu.SemaphoreType.DMA,
+        ],
         cost_estimate=pl.CostEstimate(flops=0, bytes_accessed=2 << 20, transcendentals=0),
+        compiler_params=pltpu.CompilerParams(vmem_limit_bytes=56 << 20),
     )(core, w_in[0], w_out[0])
     line = ("z4", "zl")
     up, down = turned(shared, line, -1), turned(shared, line, 1)
@@ -348,7 +340,7 @@
         cost_estimate=pl.CostEstimate(
             flops=16 * lanes * model_width * model_hidden, bytes_accessed=11 << 20, transcendentals=0
         ),
-        compiler_params=pltpu.CompilerParams(vmem_limit_bytes=40 << 20),
+        compiler_params=pltpu.CompilerParams(vmem_limit_bytes=58 << 20),
     )(core, rows, w_in[0], w_out[0], *mine, *other)
     returned = lax.all_to_all(partial_out, "x", split_axis=0, concat_axis=0, tiled=True)
     own_part, *parts = kernel_call(

time: 231 us -> 203 us (0.88)
  Pallas kernels: 41.9 us -> 15.5 us
  local copies, waits for them, and re-layouts: 8.72 us -> 4.57 us
  waiting for transfers between devices: 29.6 us -> 26.2 us
  blocking collectives: 56.2 us -> 59.5 us
  starting transfers between devices: 84.9 us -> 87.9 us
    pallas_call x1, Pallas kernels: 33 us -> 2.43 us  [local(): pl.pallas_call(share_body, out_shape=jax.ShapeDtypeStruct((2, model_width...]
    unnamed x35 -> x23, local copies, waits for them, and re-layouts: 4.24 us -> 0.08 us
    ppermute x14, waiting for transfers between devices: 23.1 us -> 19.8 us  [turned(): lax.ppermute(block, axis, [(i, (i + distance) % count) for i in range(cou...]
    pallas_call x1, Pallas kernels: 5.39 us -> 8.53 us  [local(): pl.pallas_call(mlp_body, out_shape=jax.ShapeDtypeStruct((lanes, model_wid...]
    ppermute x14, starting transfers between devices: 74.2 us -> 77 us  [turned(): lax.ppermute(block, axis, [(i, (i + distance) % count) for i in range(cou...]
  transfers between devices with their start and end apart: 17 -> 17, of which waited for: 6 -> 7; matrix products, arithmetic and copies ran while one was open for 2% -> 2% of each run, Pallas kernels for 1% -> 2%
where the time goes in v4:
time: 203 us; the launch traced here: 202 us
  starting transfers between devices  87.9 us (43%)
  blocking collectives  59.5 us (29%)
  waiting for transfers between devices  26.2 us (13%)
  Pallas kernels  15.5 us (8%)
  local copies, waits for them, and re-layouts  4.57 us (2%)
  between operations  4.15 us (2%)
  other arithmetic  3.81 us (2%)
    ppermute x14, starting transfers between devices, turned(): lax.ppermute(block, axis, [(i, (i + distance) % count) for i in range(cou...  77 us
    all_to_all x2, blocking collectives, local(): lax.all_to_all(spread_out, axes, split_axis=0, concat_axis=0, tiled=True)  39.6 us
    all_to_all x1, blocking collectives, local(): lax.all_to_all(partial_out, 'x', split_axis=0, concat_axis=0, tiled=True)  19.9 us
    ppermute x14, waiting for transfers between devices, turned(): lax.ppermute(block, axis, [(i, (i + distance) % count) for i in range(cou...  19.8 us
    pallas_call x1, Pallas kernels, local(): pl.pallas_call(mlp_body, out_shape=jax.ShapeDtypeStruct((lanes, model_wid...  8.53 us
    ppermute x2, starting transfers between devices, passed_along(): return lax.ppermute(block, axis, route)  6.59 us
    all_to_all x1, waiting for transfers between devices, local(): rows = lax.all_to_all(packed, 'x', split_axis=0, concat_axis=0, tiled=True)  6.02 us
    all_to_all x1, starting transfers between devices, local(): rows = lax.all_to_all(packed, 'x', split_axis=0, concat_axis=0, tiled=True)  4.29 us
  transfers between devices with their start and end apart: 17, of which 7 were waited for; matrix products, arithmetic and copies ran while one was open for 2% of the time, Pallas kernels for 2%

profile of v4, /device:TPU:1, one launch (start us, length us, event | category | flops | bytes accessed | tf_op | source)
XLA Modules:
  0.0 202.3 jit_solution(12254764318025114105)
XLA Ops:
  0.7 2.4 %shard_map.133 = bf16[2,1024,256]{2,1,0:T(8,128)(2,1)} custom-call(s32[1]{0:T(128)} %bitcast.8.core, bf16[2048,256]{1,0:T(8,128)(2,1)} %bitcast.54, bf16[256,2048]{1,0:T(8,128)(2,1)} %bitcast.56), custom_call_target="tpu_custom_call" | custom-call | bytes 2097152 | tf_op jit(solution)/shard_map/pallas_call | solution.py:281
  3.1 12.0 %collective-permute-start.5 = (bf16[2,1024,256]{2,1,0:T(8,128)(2,1)}, bf16[2,1024,256]{2,1,0:T(8,128)(2,1)}, u32[]{:S(2)}, u32[]{:S(2)}) collective-permute-start(bf16[2,1024,256]{2,1,0:T(8,128)(2,1)} %shard_map.133), channel_id=1, source_target_pairs={{0,15},{1,0},{2,1},{3,2},{4,3},{5,4},{6,5},{7,6},{8,7},{9,8},{10,9... | collective-permute-start | bytes 3145736 | tf_op jit(solution)/shard_map/ppermute | solution.py:29
  15.1 1.9 collective-permute-start.6
  17.0 5.3 %collective-permute-start = (s32[1]{0:T(128)}, s32[1]{0:T(128)}, u32[]{:S(2)}, u32[]{:S(2)}) collective-permute-start(s32[1]{0:T(128)} %bitcast.1), channel_id=1, source_target_pairs={{0,256},{128,384},{1,257},{129,385},{2,258},{130,386},{3,259},{131... | collective-permute-start | bytes 20 | tf_op jit(solution)/shard_map/ppermute | solution.py:24
  25.6 1.9 shard_map.131
  29.4 7.3 %collective-permute-start.3 = (bf16[32,2176]{1,0:T(8,128)(2,1)S(1)}, bf16[32,2176]{1,0:T(8,128)(2,1)S(1)}, u32[]{:S(2)}, u32[]{:S(2)}) collective-permute-start(bf16[32,2176]{1,0:T(8,128)(2,1)S(1)} %get-tuple-element.13.own), channel_id=1, source_target_pairs={{0,12},{4,0},{8,4},{12,8},{1,13},{5,1},{9,5},{13,9},{2,14},{6,2},{... | collective-permute-start | bytes 417800 | tf_op jit(solution)/shard_map/ppermute | solution.py:29
  36.7 7.7 %collective-permute-start.4 = (bf16[32,2176]{1,0:T(8,128)(2,1)S(1)}, bf16[32,2176]{1,0:T(8,128)(2,1)S(1)}, u32[]{:S(2)}, u32[]{:S(2)}) collective-permute-start(bf16[32,2176]{1,0:T(8,128)(2,1)S(1)} %get-tuple-element.13.own), channel_id=1, source_target_pairs={{0,8},{4,12},{8,0},{12,4},{1,9},{5,13},{9,1},{13,5},{2,10},{6,14},... | collective-permute-start | bytes 417800 | tf_op jit(solution)/shard_map/ppermute | solution.py:29
  46.5 5.4 %collective-permute-start.7 = (bf16[1024,256]{1,0:T(8,128)(2,1)}, bf16[1024,256]{1,0:T(8,128)(2,1)S(1)}, u32[]{:S(2)}, u32[]{:S(2)}) collective-permute-start(bf16[1024,256]{1,0:T(8,128)(2,1)} %slice_bitcast_fusion.1), channel_id=1, source_target_pairs={{0,15},{1,0},{2,1},{3,2},{4,3},{5,4},{6,5},{7,6},{8,7},{9,8},{10,9... | collective-permute-start | bytes 1572872 | tf_op jit(solution)/shard_map/ppermute | solution.py:29
  52.0 16.2 %collective-permute-start.9 = (bf16[2,1024,256]{2,1,0:T(8,128)(2,1)}, bf16[2,1024,256]{2,1,0:T(8,128)(2,1)}, u32[]{:S(2)}, u32[]{:S(2)}) collective-permute-start(bf16[2,1024,256]{2,1,0:T(8,128)(2,1)} %collective-permute-done.5.up0), channel_id=1, source_target_pairs={{0,64},{64,0},{1,65},{65,1},{2,66},{66,2},{3,67},{67,3},{4,68},{68... | collective-permute-start | bytes 3145736 | tf_op jit(solution)/shard_map/ppermute | solution.py:29
  74.0 1.9 shard_map.132
  75.9 4.3 %all-to-all-start = ((bf16[4,80,2048]{2,1,0:T(8,128)(2,1)}), bf16[4,80,2048]{2,1,0:T(8,128)(2,1)}, u32[]{:S(2)}, u32[]{:S(2)}) async-start(bf16[4,80,2048]{2,1,0:T(8,128)(2,1)} %bitcast.9), calls=%async_computation | async-start | bytes 2621440 | tf_op jit(solution)/shard_map/all_to_all | solution.py:323
  80.2 2.4 %collective-permute-start.11 = (bf16[1024,256]{1,0:T(8,128)(2,1)S(1)}, bf16[1024,256]{1,0:T(8,128)(2,1)}, u32[]{:S(2)}, u32[]{:S(2)}) collective-permute-start(bf16[1024,256]{1,0:T(8,128)(2,1)S(1)} %collective-permute-done.7.fu0), channel_id=1, source_target_pairs={{0,64},{64,0},{1,65},{65,1},{2,66},{66,2},{3,67},{67,3},{4,68},{68... | collective-permute-start | bytes 1572872 | tf_op jit(solution)/shard_map/ppermute | solution.py:29
  82.7 5.8 %collective-permute-done.8.fd0 = bf16[1024,256]{1,0:T(8,128)(2,1)} collective-permute-done((bf16[1024,256]{1,0:T(8,128)(2,1)}, bf16[1024,256]{1,0:T(8,128)(2,1)}, u32[]{:S(2)}, u32[]{:S(2)}) %collective-permute-start.8) | collective-permute-done | bytes 524320 | tf_op jit(solution)/shard_map/ppermute | solution.py:29
  88.5 3.2 %collective-permute-start.12 = (bf16[1024,256]{1,0:T(8,128)(2,1)}, bf16[1024,256]{1,0:T(8,128)(2,1)}, u32[]{:S(2)}, u32[]{:S(2)}) collective-permute-start(bf16[1024,256]{1,0:T(8,128)(2,1)} %collective-permute-done.8.fd0), channel_id=1, source_target_pairs={{0,64},{64,0},{1,65},{65,1},{2,66},{66,2},{3,67},{67,3},{4,68},{68... | collective-permute-start | bytes 1572872 | tf_op jit(solution)/shard_map/ppermute | solution.py:29
  91.7 6.0 %all-to-all-done = bf16[4,80,2048]{2,1,0:T(8,128)(2,1)} async-done(((bf16[4,80,2048]{2,1,0:T(8,128)(2,1)}), bf16[4,80,2048]{2,1,0:T(8,128)(2,1)}, u32[]{:S(2)}, u32[]{:S(2)}) %all-to-all-start) | async-done | bytes 1310752 | tf_op jit(solution)/shard_map/all_to_all | solution.py:323
  97.8 8.5 %shard_map.134 = bf16[320,2048]{1,0:T(8,128)(2,1)} custom-call(s32[1]{0:T(128)} %bitcast.8.core, bf16[320,2048]{1,0:T(8,128)(2,1)} %bitcast.10.rows, bf16[2048,256]{1,0:T(8,128)(2,1)} %bitcast.55, bf16[256,2048]{1,0:T(8,128)(2,1)} %bitcast.57, bf16[2,1024,256]{2,1,0:T(8,128)(2,1)} %collective-permute-done.5.up0, ...), custom_call_target="tpu_custom_call" | custom-call | flops 2684354560 | bytes 11534336 | tf_op jit(solution)/shard_map/pallas_call | solution.py:325
  106.3 19.9 %all_to_all.34 = bf16[4,80,2048]{2,1,0:T(8,128)(2,1)S(1)} all-to-all(bf16[4,80,2048]{2,1,0:T(8,128)(2,1)} %bitcast.53), channel_id=1, replica_groups=mesh['y'=4,'core'=2,'x'=4,'z4'=4,'zl'=4] {'x'}, dimensions={0} | all-to-all | bytes 2621440 | tf_op jit(solution)/shard_map/all_to_all | solution.py:345
  127.0 5.9 %collective-permute-start.15 = (bf16[32,2048]{1,0:T(8,128)(2,1)S(1)}, bf16[32,2048]{1,0:T(8,128)(2,1)S(1)}, u32[]{:S(2)}, u32[]{:S(2)}) collective-permute-start(bf16[32,2048]{1,0:T(8,128)(2,1)S(1)} %get-tuple-element.20), channel_id=1, source_target_pairs={{0,8},{4,12},{8,0},{12,4},{1,9},{5,13},{9,1},{13,5},{2,10},{6,14},... | collective-permute-start | bytes 393224 | tf_op jit(solution)/shard_map/ppermute | solution.py:29
  132.9 4.5 %collective-permute-start.14 = (bf16[32,2048]{1,0:T(8,128)(2,1)S(1)}, bf16[32,2048]{1,0:T(8,128)(2,1)S(1)}, u32[]{:S(2)}, u32[]{:S(2)}) collective-permute-start(bf16[32,2048]{1,0:T(8,128)(2,1)S(1)} %get-tuple-element.19), channel_id=1, source_target_pairs={{0,4},{4,8},{8,12},{12,0},{1,5},{5,9},{9,13},{13,1},{2,6},{6,10},{... | collective-permute-start | bytes 393224 | tf_op jit(solution)/shard_map/ppermute | solution.py:29
  137.4 4.7 %collective-permute-start.13 = (bf16[32,2048]{1,0:T(8,128)(2,1)S(1)}, bf16[32,2048]{1,0:T(8,128)(2,1)S(1)}, u32[]{:S(2)}, u32[]{:S(2)}) collective-permute-start(bf16[32,2048]{1,0:T(8,128)(2,1)S(1)} %get-tuple-element.18), channel_id=1, source_target_pairs={{0,12},{4,0},{8,4},{12,8},{1,13},{5,1},{9,5},{13,9},{2,14},{6,2},{... | collective-permute-start | bytes 393224 | tf_op jit(solution)/shard_map/ppermute | solution.py:29
  142.4 8.0 %collective-permute-done.15 = bf16[32,2048]{1,0:T(8,128)(2,1)S(1)} collective-permute-done((bf16[32,2048]{1,0:T(8,128)(2,1)S(1)}, bf16[32,2048]{1,0:T(8,128)(2,1)S(1)}, u32[]{:S(2)}, u32[]{:S(2)}) %collective-permute-start.15) | collective-permute-done | bytes 131104 | tf_op jit(solution)/shard_map/ppermute | solution.py:29
  151.3 4.8 %collective-permute-done.13 = bf16[32,2048]{1,0:T(8,128)(2,1)S(1)} collective-permute-done((bf16[32,2048]{1,0:T(8,128)(2,1)S(1)}, bf16[32,2048]{1,0:T(8,128)(2,1)S(1)}, u32[]{:S(2)}, u32[]{:S(2)}) %collective-permute-start.13) | collective-permute-done | bytes 131104 | tf_op jit(solution)/shard_map/ppermute | solution.py:29
  159.6 11.6 %all_to_all.35 = f32[16,1,128]{2,1,0:T(1,128)S(1)} all-to-all(f32[16,1,128]{2,1,0:T(1,128)S(1)} %broadcast_in_dim.17), channel_id=1, replica_groups=mesh['y'=4,'core'=2,'x'=4,'z4'=4,'zl'=4] {'x','zl'}, dimensions={0} | all-to-all | bytes 16384 | tf_op jit(solution)/shard_map/all_to_all | solution.py:371
  171.3 28.0 %all_to_all.36 = f32[32,1,128]{2,1,0:T(1,128)S(1)} all-to-all(f32[32,1,128]{2,1,0:T(1,128)S(1)} %broadcast_in_dim.18), channel_id=1, replica_groups=mesh['y'=4,'core'=2,'x'=4,'z4'=4,'zl'=4] {'y','core','z4'}, dimensions={0} | all-to-all | bytes 32768 | tf_op jit(solution)/shard_map/all_to_all | solution.py:371
  (68 shorter events, 18.3 us)
Async XLA Ops:
  0.6 155.9 %copy-start = (bf16[1,2048,512]{2,1,0:T(8,128)(2,1)S(1)}, bf16[1,2048,512]{2,1,0:T(8,128)(2,1)}, u32[]{:S(2)}) copy-start(bf16[1,2048,512]{2,1,0:T(8,128)(2,1)} %param.22) | copy-start | bytes 6291460
  0.7 24.9 %copy-start.1 = (bf16[1,32,2048]{2,1,0:T(8,128)(2,1)S(1)}, bf16[1,32,2048]{2,1,0:T(8,128)(2,1)}, u32[]{:S(2)}) copy-start(bf16[1,32,2048]{2,1,0:T(8,128)(2,1)} %param.13) | copy-start | bytes 393220
  3.1 41.5 %collective-permute-start.5 = (bf16[2,1024,256]{2,1,0:T(8,128)(2,1)}, bf16[2,1024,256]{2,1,0:T(8,128)(2,1)}, u32[]{:S(2)}, u32[]{:S(2)}) collective-permute-start(bf16[2,1024,256]{2,1,0:T(8,128)(2,1)} %shard_map.133), channel_id=1, source_target_pairs={{0,15},{1,0},{2,1},{3,2},{4,3},{5,4},{6,5},{7,6},{8,7},{9,8},{10,9... | collective-permute-start | bytes 3145736 | tf_op jit(solution)/shard_map/ppermute | solution.py:29
  15.1 36.9 %collective-permute-start.6 = (bf16[2,1024,256]{2,1,0:T(8,128)(2,1)}, bf16[2,1024,256]{2,1,0:T(8,128)(2,1)}, u32[]{:S(2)}, u32[]{:S(2)}) collective-permute-start(bf16[2,1024,256]{2,1,0:T(8,128)(2,1)} %shard_map.133), channel_id=1, source_target_pairs={{0,1},{1,2},{2,3},{3,4},{4,5},{5,6},{6,7},{7,8},{8,9},{9,10},{10,1... | collective-permute-start | bytes 3145736 | tf_op jit(solution)/shard_map/ppermute | solution.py:29
  17.0 7.5 %collective-permute-start = (s32[1]{0:T(128)}, s32[1]{0:T(128)}, u32[]{:S(2)}, u32[]{:S(2)}) collective-permute-start(s32[1]{0:T(128)} %bitcast.1), channel_id=1, source_target_pairs={{0,256},{128,384},{1,257},{129,385},{2,258},{130,386},{3,259},{131... | collective-permute-start | bytes 20 | tf_op jit(solution)/shard_map/ppermute | solution.py:24
  22.3 3.2 %collective-permute-start.1 = (bf16[32,2048]{1,0:T(8,128)(2,1)S(1)}, bf16[32,2048]{1,0:T(8,128)(2,1)S(1)}, u32[]{:S(2)}, u32[]{:S(2)}) collective-permute-start(bf16[32,2048]{1,0:T(8,128)(2,1)S(1)} %bitcast.65), channel_id=1, source_target_pairs={{0,256},{128,384},{1,257},{129,385},{2,258},{130,386},{3,259},{131... | collective-permute-start | bytes 393224 | tf_op jit(solution)/shard_map/ppermute | solution.py:24
  27.5 42.6 %collective-permute-start.2 = (bf16[32,2176]{1,0:T(8,128)(2,1)S(1)}, bf16[32,2176]{1,0:T(8,128)(2,1)S(1)}, u32[]{:S(2)}, u32[]{:S(2)}) collective-permute-start(bf16[32,2176]{1,0:T(8,128)(2,1)S(1)} %get-tuple-element.13.own), channel_id=1, source_target_pairs={{0,4},{4,8},{8,12},{12,0},{1,5},{5,9},{9,13},{13,1},{2,6},{6,10},{... | collective-permute-start | bytes 417800 | tf_op jit(solution)/shard_map/ppermute | solution.py:29
  29.4 42.6 %collective-permute-start.3 = (bf16[32,2176]{1,0:T(8,128)(2,1)S(1)}, bf16[32,2176]{1,0:T(8,128)(2,1)S(1)}, u32[]{:S(2)}, u32[]{:S(2)}) collective-permute-start(bf16[32,2176]{1,0:T(8,128)(2,1)S(1)} %get-tuple-element.13.own), channel_id=1, source_target_pairs={{0,12},{4,0},{8,4},{12,8},{1,13},{5,1},{9,5},{13,9},{2,14},{6,2},{... | collective-permute-start | bytes 417800 | tf_op jit(solution)/shard_map/ppermute | solution.py:29
  36.7 37.3 %collective-permute-start.4 = (bf16[32,2176]{1,0:T(8,128)(2,1)S(1)}, bf16[32,2176]{1,0:T(8,128)(2,1)S(1)}, u32[]{:S(2)}, u32[]{:S(2)}) collective-permute-start(bf16[32,2176]{1,0:T(8,128)(2,1)S(1)} %get-tuple-element.13.own), channel_id=1, source_target_pairs={{0,8},{4,12},{8,0},{12,4},{1,9},{5,13},{9,1},{13,5},{2,10},{6,14},... | collective-permute-start | bytes 417800 | tf_op jit(solution)/shard_map/ppermute | solution.py:29
  46.5 33.7 %collective-permute-start.7 = (bf16[1024,256]{1,0:T(8,128)(2,1)}, bf16[1024,256]{1,0:T(8,128)(2,1)S(1)}, u32[]{:S(2)}, u32[]{:S(2)}) collective-permute-start(bf16[1024,256]{1,0:T(8,128)(2,1)} %slice_bitcast_fusion.1), channel_id=1, source_target_pairs={{0,15},{1,0},{2,1},{3,2},{4,3},{5,4},{6,5},{7,6},{8,7},{9,8},{10,9... | collective-permute-start | bytes 1572872 | tf_op jit(solution)/shard_map/ppermute | solution.py:29
  52.0 45.8 %collective-permute-start.9 = (bf16[2,1024,256]{2,1,0:T(8,128)(2,1)}, bf16[2,1024,256]{2,1,0:T(8,128)(2,1)}, u32[]{:S(2)}, u32[]{:S(2)}) collective-permute-start(bf16[2,1024,256]{2,1,0:T(8,128)(2,1)} %collective-permute-done.5.up0), channel_id=1, source_target_pairs={{0,64},{64,0},{1,65},{65,1},{2,66},{66,2},{3,67},{67,3},{4,68},{68... | collective-permute-start | bytes 3145736 | tf_op jit(solution)/shard_map/ppermute | solution.py:29
  70.1 27.6 %collective-permute-start.10 = (bf16[2,1024,256]{2,1,0:T(8,128)(2,1)}, bf16[2,1024,256]{2,1,0:T(8,128)(2,1)}, u32[]{:S(2)}, u32[]{:S(2)}) collective-permute-start(bf16[2,1024,256]{2,1,0:T(8,128)(2,1)} %collective-permute-done.6.dn0), channel_id=1, source_target_pairs={{0,64},{64,0},{1,65},{65,1},{2,66},{66,2},{3,67},{67,3},{4,68},{68... | collective-permute-start | bytes 3145736 | tf_op jit(solution)/shard_map/ppermute | solution.py:29
  72.1 16.4 %collective-permute-start.8 = (bf16[1024,256]{1,0:T(8,128)(2,1)}, bf16[1024,256]{1,0:T(8,128)(2,1)}, u32[]{:S(2)}, u32[]{:S(2)}) collective-permute-start(bf16[1024,256]{1,0:T(8,128)(2,1)} %slice_bitcast_fusion), channel_id=1, source_target_pairs={{0,1},{1,2},{2,3},{3,4},{4,5},{5,6},{6,7},{7,8},{8,9},{9,10},{10,1... | collective-permute-start | bytes 1572872 | tf_op jit(solution)/shard_map/ppermute | solution.py:29
  75.9 21.8 %all-to-all-start = ((bf16[4,80,2048]{2,1,0:T(8,128)(2,1)}), bf16[4,80,2048]{2,1,0:T(8,128)(2,1)}, u32[]{:S(2)}, u32[]{:S(2)}) async-start(bf16[4,80,2048]{2,1,0:T(8,128)(2,1)} %bitcast.9), calls=%async_computation | async-start | bytes 2621440 | tf_op jit(solution)/shard_map/all_to_all | solution.py:323
  80.2 17.5 %collective-permute-start.11 = (bf16[1024,256]{1,0:T(8,128)(2,1)S(1)}, bf16[1024,256]{1,0:T(8,128)(2,1)}, u32[]{:S(2)}, u32[]{:S(2)}) collective-permute-start(bf16[1024,256]{1,0:T(8,128)(2,1)S(1)} %collective-permute-done.7.fu0), channel_id=1, source_target_pairs={{0,64},{64,0},{1,65},{65,1},{2,66},{66,2},{3,67},{67,3},{4,68},{68... | collective-permute-start | bytes 1572872 | tf_op jit(solution)/shard_map/ppermute | solution.py:29
  88.5 9.3 %collective-permute-start.12 = (bf16[1024,256]{1,0:T(8,128)(2,1)}, bf16[1024,256]{1,0:T(8,128)(2,1)}, u32[]{:S(2)}, u32[]{:S(2)}) collective-permute-start(bf16[1024,256]{1,0:T(8,128)(2,1)} %collective-permute-done.8.fd0), channel_id=1, source_target_pairs={{0,64},{64,0},{1,65},{65,1},{2,66},{66,2},{3,67},{67,3},{4,68},{68... | collective-permute-start | bytes 1572872 | tf_op jit(solution)/shard_map/ppermute | solution.py:29
  106.3 35.8 %copy-start.3 = (f32[1,32,512]{2,1,0:T(8,128)S(1)}, f32[1,32,512]{2,1,0:T(8,128)}, u32[]{:S(2)}) copy-start(f32[1,32,512]{2,1,0:T(8,128)} %param.23) | copy-start | bytes 196612
  106.3 50.2 %slice-start = ((f32[1,3,2048]{2,0,1:T(1,128)}), f32[1,1,2048]{2,0,1:T(1,128)S(1)}, s32[]{:S(2)}) async-start(f32[1,3,2048]{2,0,1:T(1,128)} %param.18), calls=%async_computation.4 | async-start | bytes 16384 | tf_op jit(solution)/shard_map/slice | solution.py:357
  127.0 30.5 %copy-start.8 = (s32[1,32]{1,0:T(1,128)S(1)}, s32[1,32]{1,0:T(1,128)}, u32[]{:S(2)}) copy-start(s32[1,32]{1,0:T(1,128)} %param.24) | copy-start | bytes 388
  127.0 44.3 %copy-start.10 = (pred[128]{0:T(512)(128)(4,1)S(1)}, pred[128]{0:T(512)(128)(4,1)}, u32[]{:S(2)}) copy-start(pred[128]{0:T(512)(128)(4,1)} %constant.30.clone.1) | copy-start | bytes 388
  127.0 23.5 %collective-permute-start.15 = (bf16[32,2048]{1,0:T(8,128)(2,1)S(1)}, bf16[32,2048]{1,0:T(8,128)(2,1)S(1)}, u32[]{:S(2)}, u32[]{:S(2)}) collective-permute-start(bf16[32,2048]{1,0:T(8,128)(2,1)S(1)} %get-tuple-element.20), channel_id=1, source_target_pairs={{0,8},{4,12},{8,0},{12,4},{1,9},{5,13},{9,1},{13,5},{2,10},{6,14},... | collective-permute-start | bytes 393224 | tf_op jit(solution)/shard_map/ppermute | solution.py:29
  132.9 18.4 %collective-permute-start.14 = (bf16[32,2048]{1,0:T(8,128)(2,1)S(1)}, bf16[32,2048]{1,0:T(8,128)(2,1)S(1)}, u32[]{:S(2)}, u32[]{:S(2)}) collective-permute-start(bf16[32,2048]{1,0:T(8,128)(2,1)S(1)} %get-tuple-element.19), channel_id=1, source_target_pairs={{0,4},{4,8},{8,12},{12,0},{1,5},{5,9},{9,13},{13,1},{2,6},{6,10},{... | collective-permute-start | bytes 393224 | tf_op jit(solution)/shard_map/ppermute | solution.py:29
  137.4 18.7 %collective-permute-start.13 = (bf16[32,2048]{1,0:T(8,128)(2,1)S(1)}, bf16[32,2048]{1,0:T(8,128)(2,1)S(1)}, u32[]{:S(2)}, u32[]{:S(2)}) collective-permute-start(bf16[32,2048]{1,0:T(8,128)(2,1)S(1)} %get-tuple-element.18), channel_id=1, source_target_pairs={{0,12},{4,0},{8,4},{12,8},{1,13},{5,1},{9,5},{13,9},{2,14},{6,2},{... | collective-permute-start | bytes 393224 | tf_op jit(solution)/shard_map/ppermute | solution.py:29
  156.3 44.8 %copy-start.2 = (bf16[32,2048]{1,0:T(8,128)(2,1)}, bf16[32,2048]{1,0:T(8,128)(2,1)S(1)}, u32[]{:S(2)}) copy-start(bf16[32,2048]{1,0:T(8,128)(2,1)S(1)} %get-tuple-element.24) | copy-start | bytes 393220
  (5 other events, 109.6 us)

commit v5 on v4

--- a/solution.py
+++ b/solution.py
@@ -35,7 +35,7 @@
     return centred * lax.rsqrt(spread + epsilon) * gain_row
 
 
-def kernel_call(body, out_shape, in_specs, cost, limit=40 << 20):
+def kernel_call(body, out_shape, in_specs, cost, limit=24 << 20):
     whole = pl.BlockSpec(memory_space=pltpu.VMEM)
     scalar = pl.BlockSpec(memory_space=pltpu.SMEM)
     return pl.pallas_call(
@@ -48,80 +48,56 @@
     )
 
 
-def share_body(core, w_in, w_out, out, block_in, block_out, sem):
+def share_body(w_in, w_out, out, block_in, block_out, sems):
     width, hidden = w_in.shape
     half, deep = hidden // 2, width // 2
-
-    @pl.when(core[0] == 0)
-    def _():
-        copy = pltpu.make_async_copy(w_in, block_in, sem)
-        copy.start()
-        copy.wait()
-        for h in range(2):
-            for d in range(2):
-                out[h, :, d * half : (d + 1) * half] = block_in[
-                    d * deep : (d + 1) * deep, h * half : (h + 1) * half
-                ]
-
-    @pl.when(core[0] != 0)
-    def _():
-        copy = pltpu.make_async_copy(w_out, block_out, sem)
-        copy.start()
-        copy.wait()
-        for h in range(2):
-            for p in range(width // hidden):
-                out[h, p * half : (p + 1) * half, :] = block_out[
-                    h * half : (h + 1) * half, p * hidden : (p + 1) * hidden
-                ]
+    first = pltpu.make_async_copy(w_in, block_in, sems.at[0])
+    second = pltpu.make_async_copy(w_out, block_out, sems.at[1])
+    first.start()
+    second.start()
+    first.wait()
+    for h in range(2):
+        for d in range(2):
+            out[h, 0, :, d * half : (d + 1) * half] = block_in[
+                d * deep : (d + 1) * deep, h * half : (h + 1) * half
+            ]
+    second.wait()
+    for h in range(2):
+        for p in range(width // hidden):
+            out[h, 1, p * half : (p + 1) * half, :] = block_out[
+                h * half : (h + 1) * half, p * hidden : (p + 1) * hidden
+            ]
+
+
+def relay_body(core, near, after, near_out, out, sem):
+    del after, near_out
+    copy = pltpu.make_async_copy(near.at[core[0]], out, sem)
+    copy.start()
+    copy.wait()
+
+
+def later_body(block, after, out):
+    del block, after, out
 
 
 def mlp_body(
-    core, rows, w_in, w_out, up0, dn0, fu0, fd0, up1, dn1, fu1, fd1, out,
-    own_in, own_out, near_in, near_out, far_in, far_out, act, sems,
+    rows, w_in, w_out, near_a, near_b, far_a, far_b, out, own_in, own_out, near, far, act, sems
 ):
     width, hidden = w_in.shape
     half, deep = hidden // 2, width // 2
     copy = pltpu.make_async_copy
     first_in = copy(w_in, own_in, sems.at[0])
     first_out = copy(w_out, own_out, sems.at[1])
-
-    def pieces(a, b):
-        ins = [
-            copy(a[0], near_in.at[0], sems.at[2]),
-            copy(a[1], near_in.at[1], sems.at[3]),
-            copy(a[2], far_in.at[0], sems.at[4]),
-            copy(a[3], far_in.at[1], sems.at[5]),
-        ]
-        outs = [
-            copy(b[0], near_out.at[0], sems.at[6]),
-            copy(b[1], near_out.at[1], sems.at[7]),
-            copy(b[2], far_out.at[0], sems.at[8]),
-            copy(b[3], far_out.at[1], sems.at[9]),
-        ]
-        return ins, outs
-
-    mine, other = (up0, dn0, fu0, fd0), (up1, dn1, fu1, fd1)
+    others = [
+        copy(near_a, near.at[0], sems.at[2]),
+        copy(near_b, near.at[1], sems.at[3]),
+        copy(far_a, far.at[0], sems.at[4]),
+        copy(far_b, far.at[1], sems.at[5]),
+    ]
     first_in.start()
-
-    @pl.when(core[0] == 0)
-    def _():
-        ins, outs = pieces(mine, other)
-        for c in ins:
-            c.start()
-        first_out.start()
-        for c in outs:
-            c.start()
-
-    @pl.when(core[0] != 0)
-    def _():
-        ins, outs = pieces(other, mine)
-        for c in ins:
-            c.start()
-        first_out.start()
-        for c in outs:
-            c.start()
-
-    ins, outs = pieces(mine, other)
+    for c in others:
+        c.start()
+    first_out.start()
 
     def hidden_of(product):
         return jnp.maximum(product, 0.0).astype(bf16)
@@ -129,27 +105,25 @@
     first_in.wait()
     act[:, :hidden] = hidden_of(jnp.dot(rows[...], own_in[...], preferred_element_type=f32))
     pairs = (
-        (near_in.at[0, 0], near_in.at[0, 1], near_out.at[0, 0], near_out.at[0, 1]),
-        (near_in.at[1, 0], near_in.at[1, 1], near_out.at[1, 0], near_out.at[1, 1]),
-        (far_in.at[0], far_in.at[1], far_out.at[0], far_out.at[1]),
-    )
-    for k, (in_a, in_b, _, _) in enumerate(pairs):
-        for c in ins[k : k + 1] if k < 2 else ins[2:]:
+        (near.at[0, 0], near.at[0, 1]),
+        (near.at[1, 0], near.at[1, 1]),
+        (far.at[0], far.at[1]),
+    )
+    for k, (a, b) in enumerate(pairs):
+        for c in others[k : k + 1] if k < 2 else others[2:]:
             c.wait()
-        low = jnp.concatenate([in_a[:, :half], in_b[:, :half]], axis=1)
-        high = jnp.concatenate([in_a[:, half:], in_b[:, half:]], axis=1)
+        low = jnp.concatenate([a[0, :, :half], b[0, :, :half]], axis=1)
+        high = jnp.concatenate([a[0, :, half:], b[0, :, half:]], axis=1)
         act[:, (k + 1) * hidden : (k + 2) * hidden] = hidden_of(
             jnp.dot(rows[:, :deep], low, preferred_element_type=f32)
             + jnp.dot(rows[:, deep:], high, preferred_element_type=f32)
         )
     first_out.wait()
-    for c in outs:
-        c.wait()
     for p in range(width // hidden):
         at = slice(p * half, (p + 1) * half)
         cols = slice(p * hidden, (p + 1) * hidden)
         panel = jnp.concatenate(
-            [own_out[:, cols]] + [o[at, :] for pair in pairs for o in pair[2:]], axis=0
+            [own_out[:, cols]] + [o[1, at, :] for pair in pairs for o in pair], axis=0
         )
         out[:, cols] = jnp.dot(act[...], panel, preferred_element_type=f32).astype(bf16)
 
@@ -278,24 +252,24 @@
     whole = pl.BlockSpec(memory_space=pltpu.VMEM)
     scalars = pl.BlockSpec(memory_space=pltpu.SMEM)
     anywhere = pl.BlockSpec(memory_space=pl.ANY)
+    piece = (2, model_width // 2, model_hidden)
     shared = pl.pallas_call(
         share_body,
-        out_shape=jax.ShapeDtypeStruct((2, model_width // 2, model_hidden), bf16),
-        in_specs=[scalars] + [anywhere] * 2,
+        out_shape=jax.ShapeDtypeStruct((2,) + piece, bf16),
+        in_specs=[anywhere] * 2,
         out_specs=whole,
         scratch_shapes=[
             pltpu.VMEM((model_width, model_hidden), bf16),
             pltpu.VMEM((model_hidden, model_width), bf16),
-            pltpu.SemaphoreType.DMA,
+            pltpu.SemaphoreType.DMA((2,)),
         ],
-        cost_estimate=pl.CostEstimate(flops=0, bytes_accessed=2 << 20, transcendentals=0),
+        cost_estimate=pl.CostEstimate(flops=0, bytes_accessed=4 << 20, transcendentals=0),
         compiler_params=pltpu.CompilerParams(vmem_limit_bytes=56 << 20),
-    )(core, w_in[0], w_out[0])
-    line = ("z4", "zl")
-    up, down = turned(shared, line, -1), turned(shared, line, 1)
-    far_up, far_down = turned(up[0], line, -1), turned(down[1], line, 1)
-    mine = (up, down, far_up, far_down)
-    other = [turned(piece, "core", 1) for piece in mine]
+    )(w_in[0], w_out[0])
+    line = lax.axis_size("z4") * lax.axis_size("zl")
+    onward = [(i, (i - 1) % line) for i in range(line)] + [
+        (line + i, line + (i + 1) % line) for i in range(line)
+    ]
     facts = jnp.stack([lengths[0, 0], arrived_length[0], decoder.astype(jnp.int32)])
     mid_states, block = kernel_call(
         before_body,
@@ -308,6 +282,7 @@
     )(facts, hidden[0], arrived, gain_rows, router_rows, routes[0])
     order = (1, 3, 2)
     visitors = [turned(block, "z4", k) for k in order]
+    near_mine = lax.ppermute(shared, ("core", "z4", "zl"), onward)
     slots = 4 * capacity
     lanes = experts * slots
     packed, gates_high, gates_low = kernel_call(
@@ -320,28 +295,50 @@
         "vvvv",
         (2 * lanes * 4 * tok_rows * model_width, 2 << 20),
     )(block, *visitors)
+    near_mine, relayed = pl.pallas_call(
+        relay_body,
+        out_shape=(
+            jax.ShapeDtypeStruct((2,) + piece, bf16),
+            jax.ShapeDtypeStruct(piece, bf16),
+        ),
+        in_specs=[scalars] + [anywhere] * 2,
+        out_specs=(anywhere, whole),
+        scratch_shapes=[pltpu.SemaphoreType.DMA],
+        input_output_aliases={1: 0},
+        cost_estimate=pl.CostEstimate(flops=0, bytes_accessed=2 << 20, transcendentals=0),
+        compiler_params=pltpu.CompilerParams(vmem_limit_bytes=8 << 20),
+    )(core, near_mine, gates_high)
+    far_mine = lax.ppermute(relayed, ("core", "z4", "zl"), onward)
+    near_other = turned(near_mine, "core", 1)
     rows = lax.all_to_all(packed, "x", split_axis=0, concat_axis=0, tiled=True)
-    deep, near = model_width // 2, (2, 2, model_width // 2, model_hidden)
+    far_mine = pl.pallas_call(
+        later_body,
+        out_shape=jax.ShapeDtypeStruct(piece, bf16),
+        in_specs=[anywhere] * 2,
+        out_specs=anywhere,
+        input_output_aliases={0: 0},
+        cost_estimate=pl.CostEstimate(flops=0, bytes_accessed=0, transcendentals=0),
+        compiler_params=pltpu.CompilerParams(vmem_limit_bytes=4 << 20),
+    )(far_mine, rows)
+    far_other = turned(far_mine, "core", 1)
     partial_out = pl.pallas_call(
         mlp_body,
         out_shape=jax.ShapeDtypeStruct((lanes, model_width), bf16),
-        in_specs=[scalars, whole] + [anywhere] * 10,
+        in_specs=[whole] + [anywhere] * 6,
         out_specs=whole,
         scratch_shapes=[
             pltpu.VMEM((model_width, model_hidden), bf16),
             pltpu.VMEM((model_hidden, model_width), bf16),
-            pltpu.VMEM(near, bf16),
-            pltpu.VMEM(near, bf16),
-            pltpu.VMEM((2, deep, model_hidden), bf16),
-            pltpu.VMEM((2, deep, model_hidden), bf16),
+            pltpu.VMEM((2, 2) + piece, bf16),
+            pltpu.VMEM((2,) + piece, bf16),
             pltpu.VMEM((lanes, 4 * model_hidden), bf16),
-            pltpu.SemaphoreType.DMA((10,)),
+            pltpu.SemaphoreType.DMA((6,)),
         ],
         cost_estimate=pl.CostEstimate(
             flops=16 * lanes * model_width * model_hidden, bytes_accessed=11 << 20, transcendentals=0
         ),
         compiler_params=pltpu.CompilerParams(vmem_limit_bytes=58 << 20),
-    )(core, rows, w_in[0], w_out[0], *mine, *other)
+    )(rows, w_in[0], w_out[0], near_mine, near_other, far_mine, far_other)
     returned = lax.all_to_all(partial_out, "x", split_axis=0, concat_axis=0, tiled=True)
     own_part, *parts = kernel_call(
         combine_body,

time: 203 us -> 207 us (1.020)
  starting transfers between devices: 87.9 us -> 65.1 us
  blocking collectives: 59.5 us -> 78 us
  waiting for transfers between devices: 26.2 us -> 37.4 us
  local copies, waits for them, and re-layouts: 4.57 us -> 0.81 us
    ppermute x14 -> x8, starting transfers between devices: 77 us -> 52.1 us  [turned(): lax.ppermute(block, axis, [(i, (i + distance) % count) for i in range(cou...]
    all_to_all x0 -> x1, blocking collectives: none -> 21.6 us  [local(): rows = lax.all_to_all(packed, 'x', split_axis=0, concat_axis=0, tiled=True)]
    ppermute x14 -> x8, waiting for transfers between devices: 19.8 us -> 37 us  [turned(): lax.ppermute(block, axis, [(i, (i + distance) % count) for i in range(cou...]
    ppermute x0 -> x2, starting transfers between devices: none -> 6.3 us  [the longest x1 4.38 us: local(): near_mine = lax.ppermute(shared, ('core', 'z4', 'zl'), onward)]
    all_to_all x1 -> x0, waiting for transfers between devices: 6.02 us -> none  [local(): rows = lax.all_to_all(packed, 'x', split_axis=0, concat_axis=0, tiled=True)]
    all_to_all x2, blocking collectives: 39.6 us -> 35.1 us  [local(): lax.all_to_all(spread_out, axes, split_axis=0, concat_axis=0, tiled=True)]
    all_to_all x1 -> x0, starting transfers between devices: 4.29 us -> none  [local(): rows = lax.all_to_all(packed, 'x', split_axis=0, concat_axis=0, tiled=True)]
    squeeze x2 -> x0, local copies, waits for them, and re-layouts: 3.76 us -> none  [local(): far_up, far_down = (turned(up[0], line, -1), turned(down[1], line, 1))]
  transfers between devices with their start and end apart: 17 -> 12, of which waited for: 7 -> 6; matrix products, arithmetic and copies ran while one was open for 2% -> 1% of each run, Pallas kernels for 2% -> 1%
where the time goes in v5:
time: 207 us; the launch traced here: 206 us
  blocking collectives  78 us (38%)
  starting transfers between devices  65.1 us (31%)
  waiting for transfers between devices  37.4 us (18%)
  Pallas kernels  16.3 us (8%)
  between operations  4.17 us (2%)
  other arithmetic  3.99 us (2%)
    ppermute x8, starting transfers between devices, turned(): lax.ppermute(block, axis, [(i, (i + distance) % count) for i in range(cou...  52.1 us
    ppermute x8, waiting for transfers between devices, turned(): lax.ppermute(block, axis, [(i, (i + distance) % count) for i in range(cou...  37 us
    all_to_all x2, blocking collectives, local(): lax.all_to_all(spread_out, axes, split_axis=0, concat_axis=0, tiled=True)  35.1 us
    all_to_all x1, blocking collectives, local(): rows = lax.all_to_all(packed, 'x', split_axis=0, concat_axis=0, tiled=True)  21.6 us
    all_to_all x1, blocking collectives, local(): lax.all_to_all(partial_out, 'x', split_axis=0, concat_axis=0, tiled=True)  21.3 us
    pallas_call x1, Pallas kernels, local(): pl.pallas_call(mlp_body, out_shape=jax.ShapeDtypeStruct((lanes, model_wid...  8.52 us
    ppermute x2, starting transfers between devices, passed_along(): return lax.ppermute(block, axis, route)  6.62 us
    ppermute x1, starting transfers between devices, local(): near_mine = lax.ppermute(shared, ('core', 'z4', 'zl'), onward)  4.38 us
  transfers between devices with their start and end apart: 12, of which 6 were waited for; matrix products, arithmetic and copies ran while one was open for 1% of the time, Pallas kernels for 1%

profile of v5, /device:TPU:1, one launch (start us, length us, event | category | flops | bytes accessed | tf_op | source)
XLA Modules:
  0.0 206.4 jit_solution(8521320239866412198)
XLA Ops:
  0.7 3.1 %shard_map.133 = bf16[2,2,1024,256]{3,2,1,0:T(8,128)(2,1)} custom-call(bf16[2048,256]{1,0:T(8,128)(2,1)} %bitcast.53, bf16[256,2048]{1,0:T(8,128)(2,1)} %bitcast.55), custom_call_target="tpu_custom_call" | custom-call | bytes 4194304 | tf_op jit(solution)/shard_map/pallas_call | solution.py:256
  3.8 4.4 %collective-permute-start.5 = (bf16[2,2,1024,256]{3,2,1,0:T(8,128)(2,1)}, bf16[2,2,1024,256]{3,2,1,0:T(8,128)(2,1)}, u32[]{:S(2)}, u32[]{:S(2)}) collective-permute-start(bf16[2,2,1024,256]{3,2,1,0:T(8,128)(2,1)} %shard_map.133), channel_id=1, source_target_pairs={{0,15},{1,0},{2,1},{3,2},{4,3},{5,4},{6,5},{7,6},{8,7},{9,8},{10,9... | collective-permute-start | bytes 6291464 | tf_op jit(solution)/shard_map/ppermute | solution.py:285
  8.2 5.3 %collective-permute-start = (s32[1]{0:T(128)}, s32[1]{0:T(128)}, u32[]{:S(2)}, u32[]{:S(2)}) collective-permute-start(s32[1]{0:T(128)} %bitcast.1), channel_id=1, source_target_pairs={{0,256},{128,384},{1,257},{129,385},{2,258},{130,386},{3,259},{131... | collective-permute-start | bytes 20 | tf_op jit(solution)/shard_map/ppermute | solution.py:24
  16.7 2.0 shard_map.131
  18.7 9.8 %collective-permute-start.2 = (bf16[32,2176]{1,0:T(8,128)(2,1)S(1)}, bf16[32,2176]{1,0:T(8,128)(2,1)S(1)}, u32[]{:S(2)}, u32[]{:S(2)}) collective-permute-start(bf16[32,2176]{1,0:T(8,128)(2,1)S(1)} %get-tuple-element.15.own), channel_id=1, source_target_pairs={{0,4},{4,8},{8,12},{12,0},{1,5},{5,9},{9,13},{13,1},{2,6},{6,10},{... | collective-permute-start | bytes 417800 | tf_op jit(solution)/shard_map/ppermute | solution.py:29
  28.5 3.7 %collective-permute-start.3 = (bf16[32,2176]{1,0:T(8,128)(2,1)S(1)}, bf16[32,2176]{1,0:T(8,128)(2,1)S(1)}, u32[]{:S(2)}, u32[]{:S(2)}) collective-permute-start(bf16[32,2176]{1,0:T(8,128)(2,1)S(1)} %get-tuple-element.15.own), channel_id=1, source_target_pairs={{0,12},{4,0},{8,4},{12,8},{1,13},{5,1},{9,5},{13,9},{2,14},{6,2},{... | collective-permute-start | bytes 417800 | tf_op jit(solution)/shard_map/ppermute | solution.py:29
  32.2 11.2 %collective-permute-start.4 = (bf16[32,2176]{1,0:T(8,128)(2,1)S(1)}, bf16[32,2176]{1,0:T(8,128)(2,1)S(1)}, u32[]{:S(2)}, u32[]{:S(2)}) collective-permute-start(bf16[32,2176]{1,0:T(8,128)(2,1)S(1)} %get-tuple-element.15.own), channel_id=1, source_target_pairs={{0,8},{4,12},{8,0},{12,4},{1,9},{5,13},{9,1},{13,5},{2,10},{6,14},... | collective-permute-start | bytes 417800 | tf_op jit(solution)/shard_map/ppermute | solution.py:29
  43.4 13.3 %collective-permute-done.2.b1 = bf16[32,2176]{1,0:T(8,128)(2,1)S(1)} collective-permute-done((bf16[32,2176]{1,0:T(8,128)(2,1)S(1)}, bf16[32,2176]{1,0:T(8,128)(2,1)S(1)}, u32[]{:S(2)}, u32[]{:S(2)}) %collective-permute-start.2) | collective-permute-done | bytes 139296 | tf_op jit(solution)/shard_map/ppermute | solution.py:29
  56.7 6.6 %collective-permute-done.4.b3 = bf16[32,2176]{1,0:T(8,128)(2,1)S(1)} collective-permute-done((bf16[32,2176]{1,0:T(8,128)(2,1)S(1)}, bf16[32,2176]{1,0:T(8,128)(2,1)S(1)}, u32[]{:S(2)}, u32[]{:S(2)}) %collective-permute-start.4) | collective-permute-done | bytes 139296 | tf_op jit(solution)/shard_map/ppermute | solution.py:29
  65.4 1.9 collective-permute-start.7
  67.3 4.4 %collective-permute-start.6 = (bf16[2,2,1024,256]{3,2,1,0:T(8,128)(2,1)}, bf16[2,2,1024,256]{3,2,1,0:T(8,128)(2,1)}, u32[]{:S(2)}, u32[]{:S(2)}) collective-permute-start(bf16[2,2,1024,256]{3,2,1,0:T(8,128)(2,1)} %get-tuple-element.18.near_a), channel_id=1, source_target_pairs={{0,64},{64,0},{1,65},{65,1},{2,66},{66,2},{3,67},{67,3},{4,68},{68... | collective-permute-start | bytes 6291464 | tf_op jit(solution)/shard_map/ppermute | solution.py:29
  71.7 21.6 %all_to_all.34 = bf16[4,80,2048]{2,1,0:T(8,128)(2,1)S(1)} all-to-all(bf16[4,80,2048]{2,1,0:T(8,128)(2,1)S(1)} %bitcast.49), channel_id=1, replica_groups=mesh['y'=4,'core'=2,'x'=4,'z4'=4,'zl'=4] {'x'}, dimensions={0} | all-to-all | bytes 2621440 | tf_op jit(solution)/shard_map/all_to_all | solution.py:313
  93.3 3.0 %collective-permute-start.8 = (bf16[2,1024,256]{2,1,0:T(8,128)(2,1)S(1)}, bf16[2,1024,256]{2,1,0:T(8,128)(2,1)}, u32[]{:S(2)}, u32[]{:S(2)}) collective-permute-start(bf16[2,1024,256]{2,1,0:T(8,128)(2,1)S(1)} %shard_map.135.far_a), channel_id=1, source_target_pairs={{0,64},{64,0},{1,65},{65,1},{2,66},{66,2},{3,67},{67,3},{4,68},{68... | collective-permute-start | bytes 3145736 | tf_op jit(solution)/shard_map/ppermute | solution.py:29
  96.3 2.4 %collective-permute-done.8.far_b = bf16[2,1024,256]{2,1,0:T(8,128)(2,1)} collective-permute-done((bf16[2,1024,256]{2,1,0:T(8,128)(2,1)S(1)}, bf16[2,1024,256]{2,1,0:T(8,128)(2,1)}, u32[]{:S(2)}, u32[]{:S(2)}) %collective-permute-start.8) | collective-permute-done | bytes 1048608 | tf_op jit(solution)/shard_map/ppermute | solution.py:29
  98.7 8.5 %shard_map.136 = bf16[320,2048]{1,0:T(8,128)(2,1)} custom-call(bf16[320,2048]{1,0:T(8,128)(2,1)} %bitcast.47, bf16[2048,256]{1,0:T(8,128)(2,1)} %bitcast.54, bf16[256,2048]{1,0:T(8,128)(2,1)} %bitcast.56, bf16[2,2,1024,256]{3,2,1,0:T(8,128)(2,1)} %get-tuple-element.18.near_a, bf16[2,2,1024,256]{3,2,1,0:T(8,128)(2,1)} %collective-permute-done.6.near_b, ...), custom_call_target="tpu_custom_call" | custom-call | flops 2684354560 | bytes 11534336 | tf_op jit(solution)/shard_map/pallas_call | solution.py:324
  107.2 21.3 %all_to_all.35 = bf16[4,80,2048]{2,1,0:T(8,128)(2,1)S(1)} all-to-all(bf16[4,80,2048]{2,1,0:T(8,128)(2,1)} %bitcast.52), channel_id=1, replica_groups=mesh['y'=4,'core'=2,'x'=4,'z4'=4,'zl'=4] {'x'}, dimensions={0} | all-to-all | bytes 2621440 | tf_op jit(solution)/shard_map/all_to_all | solution.py:342
  129.3 10.9 %collective-permute-start.11 = (bf16[32,2048]{1,0:T(8,128)(2,1)S(1)}, bf16[32,2048]{1,0:T(8,128)(2,1)S(1)}, u32[]{:S(2)}, u32[]{:S(2)}) collective-permute-start(bf16[32,2048]{1,0:T(8,128)(2,1)S(1)} %get-tuple-element.24), channel_id=1, source_target_pairs={{0,8},{4,12},{8,0},{12,4},{1,9},{5,13},{9,1},{13,5},{2,10},{6,14},... | collective-permute-start | bytes 393224 | tf_op jit(solution)/shard_map/ppermute | solution.py:29
  140.2 2.7 %collective-permute-start.10 = (bf16[32,2048]{1,0:T(8,128)(2,1)S(1)}, bf16[32,2048]{1,0:T(8,128)(2,1)S(1)}, u32[]{:S(2)}, u32[]{:S(2)}) collective-permute-start(bf16[32,2048]{1,0:T(8,128)(2,1)S(1)} %get-tuple-element.23), channel_id=1, source_target_pairs={{0,4},{4,8},{8,12},{12,0},{1,5},{5,9},{9,13},{13,1},{2,6},{6,10},{... | collective-permute-start | bytes 393224 | tf_op jit(solution)/shard_map/ppermute | solution.py:29
  142.9 6.5 %collective-permute-start.9 = (bf16[32,2048]{1,0:T(8,128)(2,1)S(1)}, bf16[32,2048]{1,0:T(8,128)(2,1)S(1)}, u32[]{:S(2)}, u32[]{:S(2)}) collective-permute-start(bf16[32,2048]{1,0:T(8,128)(2,1)S(1)} %get-tuple-element.22), channel_id=1, source_target_pairs={{0,12},{4,0},{8,4},{12,8},{1,13},{5,1},{9,5},{13,9},{2,14},{6,2},{... | collective-permute-start | bytes 393224 | tf_op jit(solution)/shard_map/ppermute | solution.py:29
  149.8 12.3 %collective-permute-done.10 = bf16[32,2048]{1,0:T(8,128)(2,1)S(1)} collective-permute-done((bf16[32,2048]{1,0:T(8,128)(2,1)S(1)}, bf16[32,2048]{1,0:T(8,128)(2,1)S(1)}, u32[]{:S(2)}, u32[]{:S(2)}) %collective-permute-start.10) | collective-permute-done | bytes 131104 | tf_op jit(solution)/shard_map/ppermute | solution.py:29
  162.1 2.4 %collective-permute-done.9 = bf16[32,2048]{1,0:T(8,128)(2,1)S(1)} collective-permute-done((bf16[32,2048]{1,0:T(8,128)(2,1)S(1)}, bf16[32,2048]{1,0:T(8,128)(2,1)S(1)}, u32[]{:S(2)}, u32[]{:S(2)}) %collective-permute-start.9) | collective-permute-done | bytes 131104 | tf_op jit(solution)/shard_map/ppermute | solution.py:29
  166.7 1.4 fusion.15
  168.1 9.9 %all_to_all.36 = f32[16,1,128]{2,1,0:T(1,128)S(1)} all-to-all(f32[16,1,128]{2,1,0:T(1,128)S(1)} %broadcast_in_dim.17), channel_id=1, replica_groups=mesh['y'=4,'core'=2,'x'=4,'z4'=4,'zl'=4] {'x','zl'}, dimensions={0} | all-to-all | bytes 16384 | tf_op jit(solution)/shard_map/all_to_all | solution.py:368
  178.0 25.2 %all_to_all.37 = f32[32,1,128]{2,1,0:T(1,128)S(1)} all-to-all(f32[32,1,128]{2,1,0:T(1,128)S(1)} %broadcast_in_dim.18), channel_id=1, replica_groups=mesh['y'=4,'core'=2,'x'=4,'z4'=4,'zl'=4] {'y','core','z4'}, dimensions={0} | all-to-all | bytes 32768 | tf_op jit(solution)/shard_map/all_to_all | solution.py:368
  (61 shorter events, 8.5 us)
Async XLA Ops:
  0.6 164.3 %copy-start = (bf16[1,2048,512]{2,1,0:T(8,128)(2,1)S(1)}, bf16[1,2048,512]{2,1,0:T(8,128)(2,1)}, u32[]{:S(2)}) copy-start(bf16[1,2048,512]{2,1,0:T(8,128)(2,1)} %param.22) | copy-start | bytes 6291460
  0.6 12.9 %copy-start.10 = (bf16[1,32,2048]{2,1,0:T(8,128)(2,1)S(1)}, bf16[1,32,2048]{2,1,0:T(8,128)(2,1)}, u32[]{:S(2)}) copy-start(bf16[1,32,2048]{2,1,0:T(8,128)(2,1)} %param.14) | copy-start | bytes 393220
  0.7 14.1 %copy-start.7 = (bf16[1,2048,4]{1,2,0:T(4,128)(2,1)S(1)}, bf16[1,2048,4]{1,2,0:T(4,128)(2,1)}, u32[]{:S(2)}) copy-start(bf16[1,2048,4]{1,2,0:T(4,128)(2,1)} %param.19) | copy-start | bytes 49156
  0.7 14.9 %copy-start.6 = (f32[1,3,2048]{2,0,1:T(1,128)S(1)}, f32[1,3,2048]{2,0,1:T(1,128)}, u32[]{:S(2)}) copy-start(f32[1,3,2048]{2,0,1:T(1,128)} %param.18) | copy-start | bytes 73732
  0.7 14.9 %copy-start.8 = (s32[1,32,2]{1,2,0:T(2,128)S(1)}, s32[1,32,2]{1,2,0:T(2,128)}, u32[]{:S(2)}) copy-start(s32[1,32,2]{1,2,0:T(2,128)} %param.17) | copy-start | bytes 772
  0.7 16.0 %copy-start.3 = (bf16[1,32,2048]{2,1,0:T(8,128)(2,1)S(1)}, bf16[1,32,2048]{2,1,0:T(8,128)(2,1)}, u32[]{:S(2)}) copy-start(bf16[1,32,2048]{2,1,0:T(8,128)(2,1)} %param.13) | copy-start | bytes 393220
  3.8 60.4 %collective-permute-start.5 = (bf16[2,2,1024,256]{3,2,1,0:T(8,128)(2,1)}, bf16[2,2,1024,256]{3,2,1,0:T(8,128)(2,1)}, u32[]{:S(2)}, u32[]{:S(2)}) collective-permute-start(bf16[2,2,1024,256]{3,2,1,0:T(8,128)(2,1)} %shard_map.133), channel_id=1, source_target_pairs={{0,15},{1,0},{2,1},{3,2},{4,3},{5,4},{6,5},{7,6},{8,7},{9,8},{10,9... | collective-permute-start | bytes 6291464 | tf_op jit(solution)/shard_map/ppermute | solution.py:285
  8.2 7.5 %collective-permute-start = (s32[1]{0:T(128)}, s32[1]{0:T(128)}, u32[]{:S(2)}, u32[]{:S(2)}) collective-permute-start(s32[1]{0:T(128)} %bitcast.1), channel_id=1, source_target_pairs={{0,256},{128,384},{1,257},{129,385},{2,258},{130,386},{3,259},{131... | collective-permute-start | bytes 20 | tf_op jit(solution)/shard_map/ppermute | solution.py:24
  13.5 3.2 %collective-permute-start.1 = (bf16[32,2048]{1,0:T(8,128)(2,1)S(1)}, bf16[32,2048]{1,0:T(8,128)(2,1)S(1)}, u32[]{:S(2)}, u32[]{:S(2)}) collective-permute-start(bf16[32,2048]{1,0:T(8,128)(2,1)S(1)} %bitcast.64), channel_id=1, source_target_pairs={{0,256},{128,384},{1,257},{129,385},{2,258},{130,386},{3,259},{131... | collective-permute-start | bytes 393224 | tf_op jit(solution)/shard_map/ppermute | solution.py:24
  18.7 38.0 %collective-permute-start.2 = (bf16[32,2176]{1,0:T(8,128)(2,1)S(1)}, bf16[32,2176]{1,0:T(8,128)(2,1)S(1)}, u32[]{:S(2)}, u32[]{:S(2)}) collective-permute-start(bf16[32,2176]{1,0:T(8,128)(2,1)S(1)} %get-tuple-element.15.own), channel_id=1, source_target_pairs={{0,4},{4,8},{8,12},{12,0},{1,5},{5,9},{9,13},{13,1},{2,6},{6,10},{... | collective-permute-start | bytes 417800 | tf_op jit(solution)/shard_map/ppermute | solution.py:29
  28.5 28.2 %collective-permute-start.3 = (bf16[32,2176]{1,0:T(8,128)(2,1)S(1)}, bf16[32,2176]{1,0:T(8,128)(2,1)S(1)}, u32[]{:S(2)}, u32[]{:S(2)}) collective-permute-start(bf16[32,2176]{1,0:T(8,128)(2,1)S(1)} %get-tuple-element.15.own), channel_id=1, source_target_pairs={{0,12},{4,0},{8,4},{12,8},{1,13},{5,1},{9,5},{13,9},{2,14},{6,2},{... | collective-permute-start | bytes 417800 | tf_op jit(solution)/shard_map/ppermute | solution.py:29
  32.2 31.1 %collective-permute-start.4 = (bf16[32,2176]{1,0:T(8,128)(2,1)S(1)}, bf16[32,2176]{1,0:T(8,128)(2,1)S(1)}, u32[]{:S(2)}, u32[]{:S(2)}) collective-permute-start(bf16[32,2176]{1,0:T(8,128)(2,1)S(1)} %get-tuple-element.15.own), channel_id=1, source_target_pairs={{0,8},{4,12},{8,0},{12,4},{1,9},{5,13},{9,1},{13,5},{2,10},{6,14},... | collective-permute-start | bytes 417800 | tf_op jit(solution)/shard_map/ppermute | solution.py:29
  65.4 27.9 %collective-permute-start.7 = (bf16[2,1024,256]{2,1,0:T(8,128)(2,1)S(1)}, bf16[2,1024,256]{2,1,0:T(8,128)(2,1)S(1)}, u32[]{:S(2)}, u32[]{:S(2)}) collective-permute-start(bf16[2,1024,256]{2,1,0:T(8,128)(2,1)S(1)} %get-tuple-element.19), channel_id=1, source_target_pairs={{0,15},{1,0},{2,1},{3,2},{4,3},{5,4},{6,5},{7,6},{8,7},{9,8},{10,9... | collective-permute-start | bytes 3145736 | tf_op jit(solution)/shard_map/ppermute | solution.py:311
  67.3 29.0 %collective-permute-start.6 = (bf16[2,2,1024,256]{3,2,1,0:T(8,128)(2,1)}, bf16[2,2,1024,256]{3,2,1,0:T(8,128)(2,1)}, u32[]{:S(2)}, u32[]{:S(2)}) collective-permute-start(bf16[2,2,1024,256]{3,2,1,0:T(8,128)(2,1)} %get-tuple-element.18.near_a), channel_id=1, source_target_pairs={{0,64},{64,0},{1,65},{65,1},{2,66},{66,2},{3,67},{67,3},{4,68},{68... | collective-permute-start | bytes 6291464 | tf_op jit(solution)/shard_map/ppermute | solution.py:29
  93.2 5.4 %copy-start.1 = (bf16[4,80,2048]{2,1,0:T(8,128)(2,1)}, bf16[4,80,2048]{2,1,0:T(8,128)(2,1)S(1)}, u32[]{:S(2)}) copy-start(bf16[4,80,2048]{2,1,0:T(8,128)(2,1)S(1)} %all_to_all.34) | copy-start | bytes 3932164
  93.3 5.4 %collective-permute-start.8 = (bf16[2,1024,256]{2,1,0:T(8,128)(2,1)S(1)}, bf16[2,1024,256]{2,1,0:T(8,128)(2,1)}, u32[]{:S(2)}, u32[]{:S(2)}) collective-permute-start(bf16[2,1024,256]{2,1,0:T(8,128)(2,1)S(1)} %shard_map.135.far_a), channel_id=1, source_target_pairs={{0,64},{64,0},{1,65},{65,1},{2,66},{66,2},{3,67},{67,3},{4,68},{68... | collective-permute-start | bytes 3145736 | tf_op jit(solution)/shard_map/ppermute | solution.py:29
  107.2 42.2 %copy-start.5 = (f32[1,32,512]{2,1,0:T(8,128)S(1)}, f32[1,32,512]{2,1,0:T(8,128)}, u32[]{:S(2)}) copy-start(f32[1,32,512]{2,1,0:T(8,128)} %param.23) | copy-start | bytes 196612
  107.2 57.7 %slice-start = ((f32[1,3,2048]{2,0,1:T(1,128)}), f32[1,1,2048]{2,0,1:T(1,128)S(1)}, s32[]{:S(2)}) async-start(f32[1,3,2048]{2,0,1:T(1,128)} %param.18), calls=%async_computation.4 | async-start | bytes 16384 | tf_op jit(solution)/shard_map/slice | solution.py:354
  129.3 36.5 %copy-start.9 = (s32[1,32]{1,0:T(1,128)S(1)}, s32[1,32]{1,0:T(1,128)}, u32[]{:S(2)}) copy-start(s32[1,32]{1,0:T(1,128)} %param.24) | copy-start | bytes 388
  129.3 48.7 %copy-start.11 = (pred[128]{0:T(512)(128)(4,1)S(1)}, pred[128]{0:T(512)(128)(4,1)}, u32[]{:S(2)}) copy-start(pred[128]{0:T(512)(128)(4,1)} %constant.30.clone.1) | copy-start | bytes 388
  129.3 20.5 %collective-permute-start.11 = (bf16[32,2048]{1,0:T(8,128)(2,1)S(1)}, bf16[32,2048]{1,0:T(8,128)(2,1)S(1)}, u32[]{:S(2)}, u32[]{:S(2)}) collective-permute-start(bf16[32,2048]{1,0:T(8,128)(2,1)S(1)} %get-tuple-element.24), channel_id=1, source_target_pairs={{0,8},{4,12},{8,0},{12,4},{1,9},{5,13},{9,1},{13,5},{2,10},{6,14},... | collective-permute-start | bytes 393224 | tf_op jit(solution)/shard_map/ppermute | solution.py:29
  140.2 21.9 %collective-permute-start.10 = (bf16[32,2048]{1,0:T(8,128)(2,1)S(1)}, bf16[32,2048]{1,0:T(8,128)(2,1)S(1)}, u32[]{:S(2)}, u32[]{:S(2)}) collective-permute-start(bf16[32,2048]{1,0:T(8,128)(2,1)S(1)} %get-tuple-element.23), channel_id=1, source_target_pairs={{0,4},{4,8},{8,12},{12,0},{1,5},{5,9},{9,13},{13,1},{2,6},{6,10},{... | collective-permute-start | bytes 393224 | tf_op jit(solution)/shard_map/ppermute | solution.py:29
  142.9 21.6 %collective-permute-start.9 = (bf16[32,2048]{1,0:T(8,128)(2,1)S(1)}, bf16[32,2048]{1,0:T(8,128)(2,1)S(1)}, u32[]{:S(2)}, u32[]{:S(2)}) collective-permute-start(bf16[32,2048]{1,0:T(8,128)(2,1)S(1)} %get-tuple-element.22), channel_id=1, source_target_pairs={{0,12},{4,0},{8,4},{12,8},{1,13},{5,1},{9,5},{13,9},{2,14},{6,2},{... | collective-permute-start | bytes 393224 | tf_op jit(solution)/shard_map/ppermute | solution.py:29
  164.7 40.6 %copy-start.4 = (bf16[32,2048]{1,0:T(8,128)(2,1)}, bf16[32,2048]{1,0:T(8,128)(2,1)S(1)}, u32[]{:S(2)}) copy-start(bf16[32,2048]{1,0:T(8,128)(2,1)S(1)} %get-tuple-element.28) | copy-start | bytes 393220
  (1 other events, 5.4 us)

commit v6 on v5

--- a/solution.py
+++ b/solution.py
@@ -80,52 +80,29 @@
     del block, after, out
 
 
-def mlp_body(
-    rows, w_in, w_out, near_a, near_b, far_a, far_b, out, own_in, own_out, near, far, act, sems
-):
-    width, hidden = w_in.shape
-    half, deep = hidden // 2, width // 2
-    copy = pltpu.make_async_copy
-    first_in = copy(w_in, own_in, sems.at[0])
-    first_out = copy(w_out, own_out, sems.at[1])
-    others = [
-        copy(near_a, near.at[0], sems.at[2]),
-        copy(near_b, near.at[1], sems.at[3]),
-        copy(far_a, far.at[0], sems.at[4]),
-        copy(far_b, far.at[1], sems.at[5]),
-    ]
-    first_in.start()
-    for c in others:
-        c.start()
-    first_out.start()
-
-    def hidden_of(product):
-        return jnp.maximum(product, 0.0).astype(bf16)
-
-    first_in.wait()
-    act[:, :hidden] = hidden_of(jnp.dot(rows[...], own_in[...], preferred_element_type=f32))
+def mlp_body(rows, own, near_a, near_b, far_a, far_b, out, act):
+    half = own.shape[3] // 2
+    deep = own.shape[2]
+    hidden = 2 * half
     pairs = (
-        (near.at[0, 0], near.at[0, 1]),
-        (near.at[1, 0], near.at[1, 1]),
-        (far.at[0], far.at[1]),
+        (own.at[0], own.at[1]),
+        (near_a.at[0], near_a.at[1]),
+        (near_b.at[0], near_b.at[1]),
+        (far_a, far_b),
     )
     for k, (a, b) in enumerate(pairs):
-        for c in others[k : k + 1] if k < 2 else others[2:]:
-            c.wait()
         low = jnp.concatenate([a[0, :, :half], b[0, :, :half]], axis=1)
         high = jnp.concatenate([a[0, :, half:], b[0, :, half:]], axis=1)
-        act[:, (k + 1) * hidden : (k + 2) * hidden] = hidden_of(
-            jnp.dot(rows[:, :deep], low, preferred_element_type=f32)
-            + jnp.dot(rows[:, deep:], high, preferred_element_type=f32)
+        product = jnp.dot(rows[:, :deep], low, preferred_element_type=f32) + jnp.dot(
+            rows[:, deep:], high, preferred_element_type=f32
         )
-    first_out.wait()
-    for p in range(width // hidden):
+        act[:, k * hidden : (k + 1) * hidden] = jnp.maximum(product, 0.0).astype(bf16)
+    for p in range(2 * deep // hidden):
         at = slice(p * half, (p + 1) * half)
-        cols = slice(p * hidden, (p + 1) * hidden)
-        panel = jnp.concatenate(
-            [own_out[:, cols]] + [o[1, at, :] for pair in pairs for o in pair], axis=0
-        )
-        out[:, cols] = jnp.dot(act[...], panel, preferred_element_type=f32).astype(bf16)
+        panel = jnp.concatenate([o[1, at, :] for pair in pairs for o in pair], axis=0)
+        out[:, p * hidden : (p + 1) * hidden] = jnp.dot(
+            act[...], panel, preferred_element_type=f32
+        ).astype(bf16)
 
 
 def normed_of(values, gain):
@@ -324,21 +301,16 @@
     partial_out = pl.pallas_call(
         mlp_body,
         out_shape=jax.ShapeDtypeStruct((lanes, model_width), bf16),
-        in_specs=[whole] + [anywhere] * 6,
+        in_specs=[whole] * 6,
         out_specs=whole,
         scratch_shapes=[
-            pltpu.VMEM((model_width, model_hidden), bf16),
-            pltpu.VMEM((model_hidden, model_width), bf16),
-            pltpu.VMEM((2, 2) + piece, bf16),
-            pltpu.VMEM((2,) + piece, bf16),
             pltpu.VMEM((lanes, 4 * model_hidden), bf16),
-            pltpu.SemaphoreType.DMA((6,)),
         ],
         cost_estimate=pl.CostEstimate(
             flops=16 * lanes * model_width * model_hidden, bytes_accessed=11 << 20, transcendentals=0
         ),
-        compiler_params=pltpu.CompilerParams(vmem_limit_bytes=58 << 20),
-    )(rows, w_in[0], w_out[0], near_mine, near_other, far_mine, far_other)
+        compiler_params=pltpu.CompilerParams(vmem_limit_bytes=24 << 20),
+    )(rows, shared, near_mine, near_other, far_mine, far_other)
     returned = lax.all_to_all(partial_out, "x", split_axis=0, concat_axis=0, tiled=True)
     own_part, *parts = kernel_call(
         combine_body,
@@ -362,7 +334,7 @@
     )
     counted = jnp.where(decoder, is_valid.astype(jnp.float32), 0.0)
     totals = jnp.stack([jnp.sum(token_loss * counted), jnp.sum(counted)])
-    for axes in (("x", "zl"), ("y", "core", "z4")):
+    for axes in (("y", "core", "x", "z4", "zl"),):
         count = math.prod(lax.axis_size(a) for a in axes)
         spread_out = jnp.broadcast_to(jnp.pad(totals, (0, 126))[None], (count, 128))
         totals = lax.all_to_all(spread_out, axes, split_axis=0, concat_axis=0, tiled=True).sum(0)[:2]

time: 207 us -> 204 us (0.986)
  Pallas kernels: 16.3 us -> 12.3 us
    pallas_call x1, Pallas kernels: 8.52 us -> 4.46 us  [local(): pl.pallas_call(mlp_body, out_shape=jax.ShapeDtypeStruct((lanes, model_wid...]
    all_to_all x2 -> x1, blocking collectives: 35.1 us -> 37.3 us  [local(): lax.all_to_all(spread_out, axes, split_axis=0, concat_axis=0, tiled=True)]
where the time goes in v6:
time: 204 us; the launch traced here: 203 us
  blocking collectives  79 us (39%)
  starting transfers between devices  65.3 us (32%)
  waiting for transfers between devices  37.1 us (18%)
  Pallas kernels  12.3 us (6%)
  between operations  4.02 us (2%)
  other arithmetic  3.89 us (2%)
    ppermute x8, starting transfers between devices, turned(): lax.ppermute(block, axis, [(i, (i + distance) % count) for i in range(cou...  52.3 us
    all_to_all x1, blocking collectives, local(): lax.all_to_all(spread_out, axes, split_axis=0, concat_axis=0, tiled=True)  37.3 us
    ppermute x8, waiting for transfers between devices, turned(): lax.ppermute(block, axis, [(i, (i + distance) % count) for i in range(cou...  36.8 us
    all_to_all x1, blocking collectives, local(): rows = lax.all_to_all(packed, 'x', split_axis=0, concat_axis=0, tiled=True)  21.6 us
    all_to_all x1, blocking collectives, local(): lax.all_to_all(partial_out, 'x', split_axis=0, concat_axis=0, tiled=True)  20.2 us
    ppermute x2, starting transfers between devices, passed_along(): return lax.ppermute(block, axis, route)  6.7 us
    pallas_call x1, Pallas kernels, local(): pl.pallas_call(mlp_body, out_shape=jax.ShapeDtypeStruct((lanes, model_wid...  4.46 us
    ppermute x1, starting transfers between devices, local(): near_mine = lax.ppermute(shared, ('core', 'z4', 'zl'), onward)  4.38 us
  transfers between devices with their start and end apart: 12, of which 6 were waited for; matrix products, arithmetic and copies ran while one was open for 1% of the time, Pallas kernels for 1%

profile of v6, /device:TPU:1, one launch (start us, length us, event | category | flops | bytes accessed | tf_op | source)
XLA Modules:
  0.0 203.2 jit_solution(1821019995799644401)
XLA Ops:
  0.7 3.1 %shard_map.133.own = bf16[2,2,1024,256]{3,2,1,0:T(8,128)(2,1)} custom-call(bf16[2048,256]{1,0:T(8,128)(2,1)} %bitcast.54, bf16[256,2048]{1,0:T(8,128)(2,1)} %bitcast.55), custom_call_target="tpu_custom_call" | custom-call | bytes 4194304 | tf_op jit(solution)/shard_map/pallas_call | solution.py:233
  3.8 4.4 %collective-permute-start.5 = (bf16[2,2,1024,256]{3,2,1,0:T(8,128)(2,1)}, bf16[2,2,1024,256]{3,2,1,0:T(8,128)(2,1)}, u32[]{:S(2)}, u32[]{:S(2)}) collective-permute-start(bf16[2,2,1024,256]{3,2,1,0:T(8,128)(2,1)} %shard_map.133.own), channel_id=1, source_target_pairs={{0,15},{1,0},{2,1},{3,2},{4,3},{5,4},{6,5},{7,6},{8,7},{9,8},{10,9... | collective-permute-start | bytes 6291464 | tf_op jit(solution)/shard_map/ppermute | solution.py:262
  8.2 5.4 %collective-permute-start = (s32[1]{0:T(128)}, s32[1]{0:T(128)}, u32[]{:S(2)}, u32[]{:S(2)}) collective-permute-start(s32[1]{0:T(128)} %bitcast.1), channel_id=1, source_target_pairs={{0,256},{128,384},{1,257},{129,385},{2,258},{130,386},{3,259},{131... | collective-permute-start | bytes 20 | tf_op jit(solution)/shard_map/ppermute | solution.py:24
  13.6 1.3 collective-permute-start.1
  16.8 1.9 shard_map.131
  18.8 9.8 %collective-permute-start.2 = (bf16[32,2176]{1,0:T(8,128)(2,1)S(1)}, bf16[32,2176]{1,0:T(8,128)(2,1)S(1)}, u32[]{:S(2)}, u32[]{:S(2)}) collective-permute-start(bf16[32,2176]{1,0:T(8,128)(2,1)S(1)} %get-tuple-element.15.own), channel_id=1, source_target_pairs={{0,4},{4,8},{8,12},{12,0},{1,5},{5,9},{9,13},{13,1},{2,6},{6,10},{... | collective-permute-start | bytes 417800 | tf_op jit(solution)/shard_map/ppermute | solution.py:29
  28.6 3.7 %collective-permute-start.3 = (bf16[32,2176]{1,0:T(8,128)(2,1)S(1)}, bf16[32,2176]{1,0:T(8,128)(2,1)S(1)}, u32[]{:S(2)}, u32[]{:S(2)}) collective-permute-start(bf16[32,2176]{1,0:T(8,128)(2,1)S(1)} %get-tuple-element.15.own), channel_id=1, source_target_pairs={{0,12},{4,0},{8,4},{12,8},{1,13},{5,1},{9,5},{13,9},{2,14},{6,2},{... | collective-permute-start | bytes 417800 | tf_op jit(solution)/shard_map/ppermute | solution.py:29
  32.3 11.2 %collective-permute-start.4 = (bf16[32,2176]{1,0:T(8,128)(2,1)S(1)}, bf16[32,2176]{1,0:T(8,128)(2,1)S(1)}, u32[]{:S(2)}, u32[]{:S(2)}) collective-permute-start(bf16[32,2176]{1,0:T(8,128)(2,1)S(1)} %get-tuple-element.15.own), channel_id=1, source_target_pairs={{0,8},{4,12},{8,0},{12,4},{1,9},{5,13},{9,1},{13,5},{2,10},{6,14},... | collective-permute-start | bytes 417800 | tf_op jit(solution)/shard_map/ppermute | solution.py:29
  43.5 13.3 %collective-permute-done.2.b1 = bf16[32,2176]{1,0:T(8,128)(2,1)S(1)} collective-permute-done((bf16[32,2176]{1,0:T(8,128)(2,1)S(1)}, bf16[32,2176]{1,0:T(8,128)(2,1)S(1)}, u32[]{:S(2)}, u32[]{:S(2)}) %collective-permute-start.2) | collective-permute-done | bytes 139296 | tf_op jit(solution)/shard_map/ppermute | solution.py:29
  56.8 6.4 %collective-permute-done.4.b3 = bf16[32,2176]{1,0:T(8,128)(2,1)S(1)} collective-permute-done((bf16[32,2176]{1,0:T(8,128)(2,1)S(1)}, bf16[32,2176]{1,0:T(8,128)(2,1)S(1)}, u32[]{:S(2)}, u32[]{:S(2)}) %collective-permute-start.4) | collective-permute-done | bytes 139296 | tf_op jit(solution)/shard_map/ppermute | solution.py:29
  65.4 1.9 collective-permute-start.7
  67.3 4.4 %collective-permute-start.6 = (bf16[2,2,1024,256]{3,2,1,0:T(8,128)(2,1)}, bf16[2,2,1024,256]{3,2,1,0:T(8,128)(2,1)S(1)}, u32[]{:S(2)}, u32[]{:S(2)}) collective-permute-start(bf16[2,2,1024,256]{3,2,1,0:T(8,128)(2,1)} %get-tuple-element.18.near_a), channel_id=1, source_target_pairs={{0,64},{64,0},{1,65},{65,1},{2,66},{66,2},{3,67},{67,3},{4,68},{68... | collective-permute-start | bytes 6291464 | tf_op jit(solution)/shard_map/ppermute | solution.py:29
  71.7 21.6 %all_to_all.28 = bf16[4,80,2048]{2,1,0:T(8,128)(2,1)S(1)} all-to-all(bf16[4,80,2048]{2,1,0:T(8,128)(2,1)S(1)} %bitcast.49), channel_id=1, replica_groups=mesh['y'=4,'core'=2,'x'=4,'z4'=4,'zl'=4] {'x'}, dimensions={0} | all-to-all | bytes 2621440 | tf_op jit(solution)/shard_map/all_to_all | solution.py:290
  93.3 3.1 %collective-permute-start.8 = (bf16[2,1024,256]{2,1,0:T(8,128)(2,1)S(1)}, bf16[2,1024,256]{2,1,0:T(8,128)(2,1)S(1)}, u32[]{:S(2)}, u32[]{:S(2)}) collective-permute-start(bf16[2,1024,256]{2,1,0:T(8,128)(2,1)S(1)} %shard_map.135.far_a), channel_id=1, source_target_pairs={{0,64},{64,0},{1,65},{65,1},{2,66},{66,2},{3,67},{67,3},{4,68},{68... | collective-permute-start | bytes 3145736 | tf_op jit(solution)/shard_map/ppermute | solution.py:29
  96.5 2.3 %collective-permute-done.8.far_b = bf16[2,1024,256]{2,1,0:T(8,128)(2,1)S(1)} collective-permute-done((bf16[2,1024,256]{2,1,0:T(8,128)(2,1)S(1)}, bf16[2,1024,256]{2,1,0:T(8,128)(2,1)S(1)}, u32[]{:S(2)}, u32[]{:S(2)}) %collective-permute-start.8) | collective-permute-done | bytes 1048608 | tf_op jit(solution)/shard_map/ppermute | solution.py:29
  98.7 4.5 %shard_map.136 = bf16[320,2048]{1,0:T(8,128)(2,1)S(1)} custom-call(bf16[320,2048]{1,0:T(8,128)(2,1)S(1)} %bitcast.46, bf16[2,2,1024,256]{3,2,1,0:T(8,128)(2,1)S(1)} %copy-done.1, bf16[2,2,1024,256]{3,2,1,0:T(8,128)(2,1)} %get-tuple-element.18.near_a, bf16[2,2,1024,256]{3,2,1,0:T(8,128)(2,1)S(1)} %collective-permute-done.6.near_b, ...), custom_call_target="tpu_custom_call" | custom-call | flops 2684354560 | bytes 11534336 | tf_op jit(solution)/shard_map/pallas_call | solution.py:301
  103.2 20.2 %all_to_all.29 = bf16[4,80,2048]{2,1,0:T(8,128)(2,1)S(1)} all-to-all(bf16[4,80,2048]{2,1,0:T(8,128)(2,1)S(1)} %bitcast.48), channel_id=1, replica_groups=mesh['y'=4,'core'=2,'x'=4,'z4'=4,'zl'=4] {'x'}, dimensions={0} | all-to-all | bytes 2621440 | tf_op jit(solution)/shard_map/all_to_all | solution.py:314
  124.2 10.9 %collective-permute-start.11 = (bf16[32,2048]{1,0:T(8,128)(2,1)S(1)}, bf16[32,2048]{1,0:T(8,128)(2,1)S(1)}, u32[]{:S(2)}, u32[]{:S(2)}) collective-permute-start(bf16[32,2048]{1,0:T(8,128)(2,1)S(1)} %get-tuple-element.24), channel_id=1, source_target_pairs={{0,8},{4,12},{8,0},{12,4},{1,9},{5,13},{9,1},{13,5},{2,10},{6,14},... | collective-permute-start | bytes 393224 | tf_op jit(solution)/shard_map/ppermute | solution.py:29
  135.1 2.7 %collective-permute-start.10 = (bf16[32,2048]{1,0:T(8,128)(2,1)S(1)}, bf16[32,2048]{1,0:T(8,128)(2,1)S(1)}, u32[]{:S(2)}, u32[]{:S(2)}) collective-permute-start(bf16[32,2048]{1,0:T(8,128)(2,1)S(1)} %get-tuple-element.23), channel_id=1, source_target_pairs={{0,4},{4,8},{8,12},{12,0},{1,5},{5,9},{9,13},{13,1},{2,6},{6,10},{... | collective-permute-start | bytes 393224 | tf_op jit(solution)/shard_map/ppermute | solution.py:29
  137.8 6.5 %collective-permute-start.9 = (bf16[32,2048]{1,0:T(8,128)(2,1)S(1)}, bf16[32,2048]{1,0:T(8,128)(2,1)S(1)}, u32[]{:S(2)}, u32[]{:S(2)}) collective-permute-start(bf16[32,2048]{1,0:T(8,128)(2,1)S(1)} %get-tuple-element.22), channel_id=1, source_target_pairs={{0,12},{4,0},{8,4},{12,8},{1,13},{5,1},{9,5},{13,9},{2,14},{6,2},{... | collective-permute-start | bytes 393224 | tf_op jit(solution)/shard_map/ppermute | solution.py:29
  144.6 12.3 %collective-permute-done.10 = bf16[32,2048]{1,0:T(8,128)(2,1)S(1)} collective-permute-done((bf16[32,2048]{1,0:T(8,128)(2,1)S(1)}, bf16[32,2048]{1,0:T(8,128)(2,1)S(1)}, u32[]{:S(2)}, u32[]{:S(2)}) %collective-permute-start.10) | collective-permute-done | bytes 131104 | tf_op jit(solution)/shard_map/ppermute | solution.py:29
  157.0 2.4 %collective-permute-done.9 = bf16[32,2048]{1,0:T(8,128)(2,1)S(1)} collective-permute-done((bf16[32,2048]{1,0:T(8,128)(2,1)S(1)}, bf16[32,2048]{1,0:T(8,128)(2,1)S(1)}, u32[]{:S(2)}, u32[]{:S(2)}) %collective-permute-start.9) | collective-permute-done | bytes 131104 | tf_op jit(solution)/shard_map/ppermute | solution.py:29
  161.5 1.3 fusion.15
  162.9 37.3 %all_to_all.30 = f32[512,1,128]{2,1,0:T(1,128)S(1)} all-to-all(f32[512,1,128]{2,1,0:T(1,128)S(1)} %broadcast_in_dim.24), channel_id=1, replica_groups=mesh['y'=4,'core'=2,'x'=4,'z4'=4,'zl'=4] {'y','core','x','z4','zl'}, dimensions={0} | all-to-all | bytes 524288 | tf_op jit(solution)/shard_map/all_to_all | solution.py:340
  (53 shorter events, 7.2 us)
Async XLA Ops:
  0.6 159.2 %copy-start = (bf16[1,2048,512]{2,1,0:T(8,128)(2,1)S(1)}, bf16[1,2048,512]{2,1,0:T(8,128)(2,1)}, u32[]{:S(2)}) copy-start(bf16[1,2048,512]{2,1,0:T(8,128)(2,1)} %param.22) | copy-start | bytes 6291460
  0.6 13.0 %copy-start.9 = (bf16[1,32,2048]{2,1,0:T(8,128)(2,1)S(1)}, bf16[1,32,2048]{2,1,0:T(8,128)(2,1)}, u32[]{:S(2)}) copy-start(bf16[1,32,2048]{2,1,0:T(8,128)(2,1)} %param.14) | copy-start | bytes 393220
  0.7 14.3 %copy-start.6 = (bf16[1,2048,4]{1,2,0:T(4,128)(2,1)S(1)}, bf16[1,2048,4]{1,2,0:T(4,128)(2,1)}, u32[]{:S(2)}) copy-start(bf16[1,2048,4]{1,2,0:T(4,128)(2,1)} %param.19) | copy-start | bytes 49156
  0.7 15.0 %copy-start.5 = (f32[1,3,2048]{2,0,1:T(1,128)S(1)}, f32[1,3,2048]{2,0,1:T(1,128)}, u32[]{:S(2)}) copy-start(f32[1,3,2048]{2,0,1:T(1,128)} %param.18) | copy-start | bytes 73732
  0.7 15.0 %copy-start.7 = (s32[1,32,2]{1,2,0:T(2,128)S(1)}, s32[1,32,2]{1,2,0:T(2,128)}, u32[]{:S(2)}) copy-start(s32[1,32,2]{1,2,0:T(2,128)} %param.17) | copy-start | bytes 772
  0.7 16.2 %copy-start.2 = (bf16[1,32,2048]{2,1,0:T(8,128)(2,1)S(1)}, bf16[1,32,2048]{2,1,0:T(8,128)(2,1)}, u32[]{:S(2)}) copy-start(bf16[1,32,2048]{2,1,0:T(8,128)(2,1)} %param.13) | copy-start | bytes 393220
  3.8 60.3 %collective-permute-start.5 = (bf16[2,2,1024,256]{3,2,1,0:T(8,128)(2,1)}, bf16[2,2,1024,256]{3,2,1,0:T(8,128)(2,1)}, u32[]{:S(2)}, u32[]{:S(2)}) collective-permute-start(bf16[2,2,1024,256]{3,2,1,0:T(8,128)(2,1)} %shard_map.133.own), channel_id=1, source_target_pairs={{0,15},{1,0},{2,1},{3,2},{4,3},{5,4},{6,5},{7,6},{8,7},{9,8},{10,9... | collective-permute-start | bytes 6291464 | tf_op jit(solution)/shard_map/ppermute | solution.py:262
  8.2 7.6 %collective-permute-start = (s32[1]{0:T(128)}, s32[1]{0:T(128)}, u32[]{:S(2)}, u32[]{:S(2)}) collective-permute-start(s32[1]{0:T(128)} %bitcast.1), channel_id=1, source_target_pairs={{0,256},{128,384},{1,257},{129,385},{2,258},{130,386},{3,259},{131... | collective-permute-start | bytes 20 | tf_op jit(solution)/shard_map/ppermute | solution.py:24
  13.6 3.2 %collective-permute-start.1 = (bf16[32,2048]{1,0:T(8,128)(2,1)S(1)}, bf16[32,2048]{1,0:T(8,128)(2,1)S(1)}, u32[]{:S(2)}, u32[]{:S(2)}) collective-permute-start(bf16[32,2048]{1,0:T(8,128)(2,1)S(1)} %bitcast.60), channel_id=1, source_target_pairs={{0,256},{128,384},{1,257},{129,385},{2,258},{130,386},{3,259},{131... | collective-permute-start | bytes 393224 | tf_op jit(solution)/shard_map/ppermute | solution.py:24
  18.8 38.0 %collective-permute-start.2 = (bf16[32,2176]{1,0:T(8,128)(2,1)S(1)}, bf16[32,2176]{1,0:T(8,128)(2,1)S(1)}, u32[]{:S(2)}, u32[]{:S(2)}) collective-permute-start(bf16[32,2176]{1,0:T(8,128)(2,1)S(1)} %get-tuple-element.15.own), channel_id=1, source_target_pairs={{0,4},{4,8},{8,12},{12,0},{1,5},{5,9},{9,13},{13,1},{2,6},{6,10},{... | collective-permute-start | bytes 417800 | tf_op jit(solution)/shard_map/ppermute | solution.py:29
  28.6 28.2 %collective-permute-start.3 = (bf16[32,2176]{1,0:T(8,128)(2,1)S(1)}, bf16[32,2176]{1,0:T(8,128)(2,1)S(1)}, u32[]{:S(2)}, u32[]{:S(2)}) collective-permute-start(bf16[32,2176]{1,0:T(8,128)(2,1)S(1)} %get-tuple-element.15.own), channel_id=1, source_target_pairs={{0,12},{4,0},{8,4},{12,8},{1,13},{5,1},{9,5},{13,9},{2,14},{6,2},{... | collective-permute-start | bytes 417800 | tf_op jit(solution)/shard_map/ppermute | solution.py:29
  32.3 31.0 %collective-permute-start.4 = (bf16[32,2176]{1,0:T(8,128)(2,1)S(1)}, bf16[32,2176]{1,0:T(8,128)(2,1)S(1)}, u32[]{:S(2)}, u32[]{:S(2)}) collective-permute-start(bf16[32,2176]{1,0:T(8,128)(2,1)S(1)} %get-tuple-element.15.own), channel_id=1, source_target_pairs={{0,8},{4,12},{8,0},{12,4},{1,9},{5,13},{9,1},{13,5},{2,10},{6,14},... | collective-permute-start | bytes 417800 | tf_op jit(solution)/shard_map/ppermute | solution.py:29
  65.4 27.9 %collective-permute-start.7 = (bf16[2,1024,256]{2,1,0:T(8,128)(2,1)S(1)}, bf16[2,1024,256]{2,1,0:T(8,128)(2,1)S(1)}, u32[]{:S(2)}, u32[]{:S(2)}) collective-permute-start(bf16[2,1024,256]{2,1,0:T(8,128)(2,1)S(1)} %get-tuple-element.19), channel_id=1, source_target_pairs={{0,15},{1,0},{2,1},{3,2},{4,3},{5,4},{6,5},{7,6},{8,7},{9,8},{10,9... | collective-permute-start | bytes 3145736 | tf_op jit(solution)/shard_map/ppermute | solution.py:288
  67.3 29.1 %collective-permute-start.6 = (bf16[2,2,1024,256]{3,2,1,0:T(8,128)(2,1)}, bf16[2,2,1024,256]{3,2,1,0:T(8,128)(2,1)S(1)}, u32[]{:S(2)}, u32[]{:S(2)}) collective-permute-start(bf16[2,2,1024,256]{3,2,1,0:T(8,128)(2,1)} %get-tuple-element.18.near_a), channel_id=1, source_target_pairs={{0,64},{64,0},{1,65},{65,1},{2,66},{66,2},{3,67},{67,3},{4,68},{68... | collective-permute-start | bytes 6291464 | tf_op jit(solution)/shard_map/ppermute | solution.py:29
  93.3 5.4 %copy-start.1 = (bf16[2,2,1024,256]{3,2,1,0:T(8,128)(2,1)S(1)}, bf16[2,2,1024,256]{3,2,1,0:T(8,128)(2,1)}, u32[]{:S(2)}) copy-start(bf16[2,2,1024,256]{3,2,1,0:T(8,128)(2,1)} %shard_map.133.own) | copy-start | bytes 6291460
  93.3 5.4 %collective-permute-start.8 = (bf16[2,1024,256]{2,1,0:T(8,128)(2,1)S(1)}, bf16[2,1024,256]{2,1,0:T(8,128)(2,1)S(1)}, u32[]{:S(2)}, u32[]{:S(2)}) collective-permute-start(bf16[2,1024,256]{2,1,0:T(8,128)(2,1)S(1)} %shard_map.135.far_a), channel_id=1, source_target_pairs={{0,64},{64,0},{1,65},{65,1},{2,66},{66,2},{3,67},{67,3},{4,68},{68... | collective-permute-start | bytes 3145736 | tf_op jit(solution)/shard_map/ppermute | solution.py:29
  103.2 41.1 %copy-start.4 = (f32[1,32,512]{2,1,0:T(8,128)S(1)}, f32[1,32,512]{2,1,0:T(8,128)}, u32[]{:S(2)}) copy-start(f32[1,32,512]{2,1,0:T(8,128)} %param.23) | copy-start | bytes 196612
  103.2 56.6 %slice-start = ((f32[1,3,2048]{2,0,1:T(1,128)}), f32[1,1,2048]{2,0,1:T(1,128)S(1)}, s32[]{:S(2)}) async-start(f32[1,3,2048]{2,0,1:T(1,128)} %param.18), calls=%async_computation.3 | async-start | bytes 16384 | tf_op jit(solution)/shard_map/slice | solution.py:326
  124.1 36.5 %copy-start.8 = (s32[1,32]{1,0:T(1,128)S(1)}, s32[1,32]{1,0:T(1,128)}, u32[]{:S(2)}) copy-start(s32[1,32]{1,0:T(1,128)} %param.24) | copy-start | bytes 388
  124.2 20.5 %collective-permute-start.11 = (bf16[32,2048]{1,0:T(8,128)(2,1)S(1)}, bf16[32,2048]{1,0:T(8,128)(2,1)S(1)}, u32[]{:S(2)}, u32[]{:S(2)}) collective-permute-start(bf16[32,2048]{1,0:T(8,128)(2,1)S(1)} %get-tuple-element.24), channel_id=1, source_target_pairs={{0,8},{4,12},{8,0},{12,4},{1,9},{5,13},{9,1},{13,5},{2,10},{6,14},... | collective-permute-start | bytes 393224 | tf_op jit(solution)/shard_map/ppermute | solution.py:29
  135.1 21.9 %collective-permute-start.10 = (bf16[32,2048]{1,0:T(8,128)(2,1)S(1)}, bf16[32,2048]{1,0:T(8,128)(2,1)S(1)}, u32[]{:S(2)}, u32[]{:S(2)}) collective-permute-start(bf16[32,2048]{1,0:T(8,128)(2,1)S(1)} %get-tuple-element.23), channel_id=1, source_target_pairs={{0,4},{4,8},{8,12},{12,0},{1,5},{5,9},{9,13},{13,1},{2,6},{6,10},{... | collective-permute-start | bytes 393224 | tf_op jit(solution)/shard_map/ppermute | solution.py:29
  137.8 21.6 %collective-permute-start.9 = (bf16[32,2048]{1,0:T(8,128)(2,1)S(1)}, bf16[32,2048]{1,0:T(8,128)(2,1)S(1)}, u32[]{:S(2)}, u32[]{:S(2)}) collective-permute-start(bf16[32,2048]{1,0:T(8,128)(2,1)S(1)} %get-tuple-element.22), channel_id=1, source_target_pairs={{0,12},{4,0},{8,4},{12,8},{1,13},{5,1},{9,5},{13,9},{2,14},{6,2},{... | collective-permute-start | bytes 393224 | tf_op jit(solution)/shard_map/ppermute | solution.py:29
  159.6 42.5 %copy-start.3 = (bf16[32,2048]{1,0:T(8,128)(2,1)}, bf16[32,2048]{1,0:T(8,128)(2,1)S(1)}, u32[]{:S(2)}) copy-start(bf16[32,2048]{1,0:T(8,128)(2,1)S(1)} %get-tuple-element.28) | copy-start | bytes 393220

commit v7 on v6

--- a/solution.py
+++ b/solution.py
@@ -27,12 +27,6 @@
 def turned(block, axis, distance):
     count = math.prod(lax.axis_size(a) for a in ([axis] if isinstance(axis, str) else axis))
     return lax.ppermute(block, axis, [(i, (i + distance) % count) for i in range(count)])
-
-
-def layer_norm(values, gain_row):
-    centred = values - jnp.mean(values, axis=-1, keepdims=True)
-    spread = jnp.mean(centred * centred, axis=-1, keepdims=True)
-    return centred * lax.rsqrt(spread + epsilon) * gain_row
 
 
 def kernel_call(body, out_shape, in_specs, cost, limit=24 << 20):
@@ -199,6 +193,34 @@
         o[...] = value[(k + 1) * n : (k + 2) * n].astype(bf16)
 
 
+def after_body(
+    facts, mid, own, p1, p2, p3, gains, shortlist, student, targets, out, totals
+):
+    def log_softmax(values):
+        moved = values - jnp.max(values, axis=-1, keepdims=True)
+        return moved - jnp.log(jnp.sum(jnp.exp(moved), axis=-1, keepdims=True))
+
+    value = mid[...] + own[...]
+    for p in (p1, p2, p3):
+        value = value + p[...].astype(f32)
+    layer = value.astype(bf16)
+    out[...] = layer
+    final = normed_of(layer.astype(f32), gains[2:3, :]).astype(bf16)
+    teacher = log_softmax(jnp.dot(final, shortlist[...], preferred_element_type=f32))
+    learner = log_softmax(student[...])
+    column = lax.broadcasted_iota(jnp.int32, learner.shape, 1)
+    picked = jnp.where(column == targets[...], learner, 0.0)
+    token_loss = jnp.sum(jnp.exp(teacher) * (teacher - learner), axis=-1, keepdims=True) - jnp.sum(
+        picked, axis=-1, keepdims=True
+    )
+    token = lax.broadcasted_iota(jnp.int32, token_loss.shape, 0)
+    counted = (token < facts[0]) & (facts[2] > 0)
+    loss_sum = jnp.sum(jnp.where(counted, token_loss, 0.0))
+    loss_count = jnp.sum(jnp.where(counted, 1.0, 0.0))
+    lane = lax.broadcasted_iota(jnp.int32, totals.shape, 1)
+    totals[...] = jnp.where(lane == 0, loss_sum, jnp.where(lane == 1, loss_count, 0.0))
+
+
 def local(
     hidden,
     memory,
@@ -219,7 +241,6 @@
     model_width = hidden.shape[2]
     capacity = 5 * tok_rows // 8
     decoder = lax.axis_index("y") >= chips // 2
-    is_valid = jnp.arange(tok_rows) < lengths[0, 0]
     core = lax.axis_index("core").astype(jnp.int32)[None]
     model_hidden = w_in.shape[2]
     gain_rows = norm_gain[0]
@@ -319,25 +340,21 @@
         "vvv",
         (4 * lanes * 4 * tok_rows * model_width, 2 << 20),
     )(returned, gates_high, gates_low)
-    moe_out = own_part
-    for k, part in zip(order, parts):
-        moe_out = moe_out + turned(part, "z4", -k).astype(f32)
-    layer_out = (mid_states + moe_out).astype(jnp.bfloat16)
-    final_normed = layer_norm(layer_out.astype(jnp.float32), gain_rows[2]).astype(jnp.bfloat16)
-    teacher = jax.nn.log_softmax(
-        jnp.dot(final_normed, shortlist[0], preferred_element_type=jnp.float32), axis=-1
-    )
-    learner = jax.nn.log_softmax(student[0], axis=-1)
-    picked = (targets[0][:, None] == jnp.arange(student.shape[2])).astype(jnp.float32)
-    token_loss = jnp.sum(jnp.exp(teacher) * (teacher - learner), axis=-1) - jnp.sum(
-        picked * learner, axis=-1
-    )
-    counted = jnp.where(decoder, is_valid.astype(jnp.float32), 0.0)
-    totals = jnp.stack([jnp.sum(token_loss * counted), jnp.sum(counted)])
-    for axes in (("y", "core", "x", "z4", "zl"),):
-        count = math.prod(lax.axis_size(a) for a in axes)
-        spread_out = jnp.broadcast_to(jnp.pad(totals, (0, 126))[None], (count, 128))
-        totals = lax.all_to_all(spread_out, axes, split_axis=0, concat_axis=0, tiled=True).sum(0)[:2]
+    home = [turned(part, "z4", -k) for k, part in zip(order, parts)]
+    local_axes, far_axes = ("x", "zl"), ("y", "core", "z4")
+    members = [math.prod(lax.axis_size(a) for a in axes) for axes in (local_axes, far_axes)]
+    layer_out, totals = kernel_call(
+        after_body,
+        (
+            jax.ShapeDtypeStruct((tok_rows, model_width), bf16),
+            jax.ShapeDtypeStruct((members[0], 128), f32),
+        ),
+        "svvvvvvvvv",
+        (2 * tok_rows * model_width * shortlist.shape[2], 4 << 20),
+    )(facts, mid_states, own_part, *home, gain_rows, shortlist[0], student[0], targets[0][:, None])
+    totals = lax.all_to_all(totals, local_axes, split_axis=0, concat_axis=0, tiled=True).sum(0)
+    totals = jnp.broadcast_to(totals[None], (members[1], 128))
+    totals = lax.all_to_all(totals, far_axes, split_axis=0, concat_axis=0, tiled=True).sum(0)
     return (layer_out[None], totals[0] / totals[1])
 
 

time: 204 us -> 201 us (0.985)
  other arithmetic: 3.89 us -> 0.79 us
  waiting for transfers between devices: 37.1 us -> 39.3 us
    ppermute x8, waiting for transfers between devices: 36.8 us -> 38.9 us  [turned(): lax.ppermute(block, axis, [(i, (i + distance) % count) for i in range(cou...]
    all_to_all x1 -> x2, blocking collectives: 37.3 us -> 36.3 us  [the longest x1 27 us: local(): lax.all_to_all(totals, far_axes, split_axis=0, concat_axis=0, tiled=True)]
  transfers between devices with their start and end apart: 12 -> 12, of which waited for: 6 -> 6; matrix products, arithmetic and copies ran while one was open for 1% -> 0% of each run, Pallas kernels for 1% -> 1%
where the time goes in v7:
time: 201 us; the launch traced here: 200 us
  blocking collectives  78.1 us (39%)
  starting transfers between devices  65.3 us (32%)
  waiting for transfers between devices  39.3 us (20%)
  Pallas kernels  11.8 us (6%)
  between operations  4.01 us (2%)
    ppermute x8, starting transfers between devices, turned(): lax.ppermute(block, axis, [(i, (i + distance) % count) for i in range(cou...  52.3 us
    ppermute x8, waiting for transfers between devices, turned(): lax.ppermute(block, axis, [(i, (i + distance) % count) for i in range(cou...  38.9 us
    all_to_all x1, blocking collectives, local(): lax.all_to_all(totals, far_axes, split_axis=0, concat_axis=0, tiled=True)  27 us
    all_to_all x1, blocking collectives, local(): rows = lax.all_to_all(packed, 'x', split_axis=0, concat_axis=0, tiled=True)  21.6 us
    all_to_all x1, blocking collectives, local(): lax.all_to_all(partial_out, 'x', split_axis=0, concat_axis=0, tiled=True)  20.2 us
    all_to_all x1, blocking collectives, local(): lax.all_to_all(totals, local_axes, split_axis=0, concat_axis=0, tiled=True)  9.28 us
    ppermute x2, starting transfers between devices, passed_along(): return lax.ppermute(block, axis, route)  6.68 us
    ppermute x1, starting transfers between devices, local(): near_mine = lax.ppermute(shared, ('core', 'z4', 'zl'), onward)  4.37 us
  transfers between devices with their start and end apart: 12, of which 6 were waited for; matrix products, arithmetic and copies ran while one was open for 0% of the time, Pallas kernels for 1%

profile of v7, /device:TPU:1, one launch (start us, length us, event | category | flops | bytes accessed | tf_op | source)
XLA Modules:
  0.0 200.1 jit_solution(16209212829308983075)
XLA Ops:
  0.7 3.0 %shard_map.133.own = bf16[2,2,1024,256]{3,2,1,0:T(8,128)(2,1)} custom-call(bf16[2048,256]{1,0:T(8,128)(2,1)} %bitcast.40, bf16[256,2048]{1,0:T(8,128)(2,1)} %bitcast.41), custom_call_target="tpu_custom_call" | custom-call | bytes 4194304 | tf_op jit(solution)/shard_map/pallas_call | solution.py:254
  3.7 4.4 %collective-permute-start.5 = (bf16[2,2,1024,256]{3,2,1,0:T(8,128)(2,1)}, bf16[2,2,1024,256]{3,2,1,0:T(8,128)(2,1)S(1)}, u32[]{:S(2)}, u32[]{:S(2)}) collective-permute-start(bf16[2,2,1024,256]{3,2,1,0:T(8,128)(2,1)} %shard_map.133.own), channel_id=1, source_target_pairs={{0,15},{1,0},{2,1},{3,2},{4,3},{5,4},{6,5},{7,6},{8,7},{9,8},{10,9... | collective-permute-start | bytes 6291464 | tf_op jit(solution)/shard_map/ppermute | solution.py:283
  8.1 5.4 %collective-permute-start = (s32[1]{0:T(128)}, s32[1]{0:T(128)}, u32[]{:S(2)}, u32[]{:S(2)}) collective-permute-start(s32[1]{0:T(128)} %bitcast.1), channel_id=1, source_target_pairs={{0,256},{128,384},{1,257},{129,385},{2,258},{130,386},{3,259},{131... | collective-permute-start | bytes 20 | tf_op jit(solution)/shard_map/ppermute | solution.py:24
  16.7 2.0 shard_map.131
  18.7 9.8 %collective-permute-start.2 = (bf16[32,2176]{1,0:T(8,128)(2,1)S(1)}, bf16[32,2176]{1,0:T(8,128)(2,1)S(1)}, u32[]{:S(2)}, u32[]{:S(2)}) collective-permute-start(bf16[32,2176]{1,0:T(8,128)(2,1)S(1)} %get-tuple-element.16.own), channel_id=1, source_target_pairs={{0,4},{4,8},{8,12},{12,0},{1,5},{5,9},{9,13},{13,1},{2,6},{6,10},{... | collective-permute-start | bytes 417800 | tf_op jit(solution)/shard_map/ppermute | solution.py:29
  28.5 3.7 %collective-permute-start.3 = (bf16[32,2176]{1,0:T(8,128)(2,1)S(1)}, bf16[32,2176]{1,0:T(8,128)(2,1)S(1)}, u32[]{:S(2)}, u32[]{:S(2)}) collective-permute-start(bf16[32,2176]{1,0:T(8,128)(2,1)S(1)} %get-tuple-element.16.own), channel_id=1, source_target_pairs={{0,12},{4,0},{8,4},{12,8},{1,13},{5,1},{9,5},{13,9},{2,14},{6,2},{... | collective-permute-start | bytes 417800 | tf_op jit(solution)/shard_map/ppermute | solution.py:29
  32.2 11.2 %collective-permute-start.4 = (bf16[32,2176]{1,0:T(8,128)(2,1)S(1)}, bf16[32,2176]{1,0:T(8,128)(2,1)S(1)}, u32[]{:S(2)}, u32[]{:S(2)}) collective-permute-start(bf16[32,2176]{1,0:T(8,128)(2,1)S(1)} %get-tuple-element.16.own), channel_id=1, source_target_pairs={{0,8},{4,12},{8,0},{12,4},{1,9},{5,13},{9,1},{13,5},{2,10},{6,14},... | collective-permute-start | bytes 417800 | tf_op jit(solution)/shard_map/ppermute | solution.py:29
  43.4 13.3 %collective-permute-done.2.b1 = bf16[32,2176]{1,0:T(8,128)(2,1)S(1)} collective-permute-done((bf16[32,2176]{1,0:T(8,128)(2,1)S(1)}, bf16[32,2176]{1,0:T(8,128)(2,1)S(1)}, u32[]{:S(2)}, u32[]{:S(2)}) %collective-permute-start.2) | collective-permute-done | bytes 139296 | tf_op jit(solution)/shard_map/ppermute | solution.py:29
  56.7 6.5 %collective-permute-done.4.b3 = bf16[32,2176]{1,0:T(8,128)(2,1)S(1)} collective-permute-done((bf16[32,2176]{1,0:T(8,128)(2,1)S(1)}, bf16[32,2176]{1,0:T(8,128)(2,1)S(1)}, u32[]{:S(2)}, u32[]{:S(2)}) %collective-permute-start.4) | collective-permute-done | bytes 139296 | tf_op jit(solution)/shard_map/ppermute | solution.py:29
  64.2 1.9 collective-permute-start.7
  66.1 4.3 %collective-permute-start.6 = (bf16[2,2,1024,256]{3,2,1,0:T(8,128)(2,1)S(1)}, bf16[2,2,1024,256]{3,2,1,0:T(8,128)(2,1)S(1)}, u32[]{:S(2)}, u32[]{:S(2)}) collective-permute-start(bf16[2,2,1024,256]{3,2,1,0:T(8,128)(2,1)S(1)} %get-tuple-element.19.near_a), channel_id=1, source_target_pairs={{0,64},{64,0},{1,65},{65,1},{2,66},{66,2},{3,67},{67,3},{4,68},{68... | collective-permute-start | bytes 6291464 | tf_op jit(solution)/shard_map/ppermute | solution.py:29
  70.4 21.6 %all_to_all.37 = bf16[4,80,2048]{2,1,0:T(8,128)(2,1)S(1)} all-to-all(bf16[4,80,2048]{2,1,0:T(8,128)(2,1)S(1)} %bitcast.34), channel_id=1, replica_groups=mesh['y'=4,'core'=2,'x'=4,'z4'=4,'zl'=4] {'x'}, dimensions={0} | all-to-all | bytes 2621440 | tf_op jit(solution)/shard_map/all_to_all | solution.py:311
  92.0 3.1 %collective-permute-start.8 = (bf16[2,1024,256]{2,1,0:T(8,128)(2,1)S(1)}, bf16[2,1024,256]{2,1,0:T(8,128)(2,1)S(1)}, u32[]{:S(2)}, u32[]{:S(2)}) collective-permute-start(bf16[2,1024,256]{2,1,0:T(8,128)(2,1)S(1)} %shard_map.135.far_a), channel_id=1, source_target_pairs={{0,64},{64,0},{1,65},{65,1},{2,66},{66,2},{3,67},{67,3},{4,68},{68... | collective-permute-start | bytes 3145736 | tf_op jit(solution)/shard_map/ppermute | solution.py:29
  95.1 2.3 %collective-permute-done.8.far_b = bf16[2,1024,256]{2,1,0:T(8,128)(2,1)S(1)} collective-permute-done((bf16[2,1024,256]{2,1,0:T(8,128)(2,1)S(1)}, bf16[2,1024,256]{2,1,0:T(8,128)(2,1)S(1)}, u32[]{:S(2)}, u32[]{:S(2)}) %collective-permute-start.8) | collective-permute-done | bytes 1048608 | tf_op jit(solution)/shard_map/ppermute | solution.py:29
  97.4 2.9 %shard_map.136 = bf16[320,2048]{1,0:T(8,128)(2,1)S(1)} custom-call(bf16[320,2048]{1,0:T(8,128)(2,1)S(1)} %bitcast.30, bf16[2,2,1024,256]{3,2,1,0:T(8,128)(2,1)S(1)} %copy-done, bf16[2,2,1024,256]{3,2,1,0:T(8,128)(2,1)S(1)} %get-tuple-element.19.near_a, bf16[2,2,1024,256]{3,2,1,0:T(8,128)(2,1)S(1)} %collective-permute-done.6.near_b, ...), custom_call_target="tpu_custom_call" | custom-call | flops 2684354560 | bytes 11534336 | tf_op jit(solution)/shard_map/pallas_call | solution.py:322
  100.3 20.2 %all_to_all.38 = bf16[4,80,2048]{2,1,0:T(8,128)(2,1)S(1)} all-to-all(bf16[4,80,2048]{2,1,0:T(8,128)(2,1)S(1)} %bitcast.32), channel_id=1, replica_groups=mesh['y'=4,'core'=2,'x'=4,'z4'=4,'zl'=4] {'x'}, dimensions={0} | all-to-all | bytes 2621440 | tf_op jit(solution)/shard_map/all_to_all | solution.py:335
  121.9 6.7 %collective-permute-start.9 = (bf16[32,2048]{1,0:T(8,128)(2,1)}, bf16[32,2048]{1,0:T(8,128)(2,1)S(1)}, u32[]{:S(2)}, u32[]{:S(2)}) collective-permute-start(bf16[32,2048]{1,0:T(8,128)(2,1)} %get-tuple-element.23), channel_id=1, source_target_pairs={{0,12},{4,0},{8,4},{12,8},{1,13},{5,1},{9,5},{13,9},{2,14},{6,2},{... | collective-permute-start | bytes 393224 | tf_op jit(solution)/shard_map/ppermute | solution.py:29
  128.6 2.9 %collective-permute-start.10 = (bf16[32,2048]{1,0:T(8,128)(2,1)S(1)}, bf16[32,2048]{1,0:T(8,128)(2,1)S(1)}, u32[]{:S(2)}, u32[]{:S(2)}) collective-permute-start(bf16[32,2048]{1,0:T(8,128)(2,1)S(1)} %get-tuple-element.24), channel_id=1, source_target_pairs={{0,4},{4,8},{8,12},{12,0},{1,5},{5,9},{9,13},{13,1},{2,6},{6,10},{... | collective-permute-start | bytes 393224 | tf_op jit(solution)/shard_map/ppermute | solution.py:29
  131.5 10.6 %collective-permute-start.11 = (bf16[32,2048]{1,0:T(8,128)(2,1)S(1)}, bf16[32,2048]{1,0:T(8,128)(2,1)S(1)}, u32[]{:S(2)}, u32[]{:S(2)}) collective-permute-start(bf16[32,2048]{1,0:T(8,128)(2,1)S(1)} %get-tuple-element.25), channel_id=1, source_target_pairs={{0,8},{4,12},{8,0},{12,4},{1,9},{5,13},{9,1},{13,5},{2,10},{6,14},... | collective-permute-start | bytes 393224 | tf_op jit(solution)/shard_map/ppermute | solution.py:29
  142.2 6.1 %collective-permute-done.10.p2 = bf16[32,2048]{1,0:T(8,128)(2,1)S(1)} collective-permute-done((bf16[32,2048]{1,0:T(8,128)(2,1)S(1)}, bf16[32,2048]{1,0:T(8,128)(2,1)S(1)}, u32[]{:S(2)}, u32[]{:S(2)}) %collective-permute-start.10) | collective-permute-done | bytes 131104 | tf_op jit(solution)/shard_map/ppermute | solution.py:29
  148.3 10.8 %collective-permute-done.11.p3 = bf16[32,2048]{1,0:T(8,128)(2,1)S(1)} collective-permute-done((bf16[32,2048]{1,0:T(8,128)(2,1)S(1)}, bf16[32,2048]{1,0:T(8,128)(2,1)S(1)}, u32[]{:S(2)}, u32[]{:S(2)}) %collective-permute-start.11) | collective-permute-done | bytes 131104 | tf_op jit(solution)/shard_map/ppermute | solution.py:29
  159.0 1.7 shard_map.138
  160.7 9.3 %all_to_all.39 = f32[16,1,128]{2,1,0:T(1,128)S(1)} all-to-all(f32[16,1,128]{2,1,0:T(1,128)S(1)} %bitcast.39), channel_id=1, replica_groups=mesh['y'=4,'core'=2,'x'=4,'z4'=4,'zl'=4] {'x','zl'}, dimensions={0} | all-to-all | bytes 16384 | tf_op jit(solution)/shard_map/all_to_all | solution.py:355
  170.1 27.0 %all_to_all.40 = f32[32,1,128]{2,1,0:T(1,128)S(1)} all-to-all(f32[32,1,128]{2,1,0:T(1,128)S(1)} %broadcast_in_dim.14), channel_id=1, replica_groups=mesh['y'=4,'core'=2,'x'=4,'z4'=4,'zl'=4] {'y','core','z4'}, dimensions={0} | all-to-all | bytes 32768 | tf_op jit(solution)/shard_map/all_to_all | solution.py:357
  (40 shorter events, 5.6 us)
Async XLA Ops:
  0.6 12.9 %copy-start.8 = (bf16[1,32,2048]{2,1,0:T(8,128)(2,1)S(1)}, bf16[1,32,2048]{2,1,0:T(8,128)(2,1)}, u32[]{:S(2)}) copy-start(bf16[1,32,2048]{2,1,0:T(8,128)(2,1)} %param.13) | copy-start | bytes 393220
  0.6 14.2 %copy-start.5 = (bf16[1,2048,4]{1,2,0:T(4,128)(2,1)S(1)}, bf16[1,2048,4]{1,2,0:T(4,128)(2,1)}, u32[]{:S(2)}) copy-start(bf16[1,2048,4]{1,2,0:T(4,128)(2,1)} %param.18) | copy-start | bytes 49156
  0.7 14.9 %copy-start.4 = (f32[1,3,2048]{2,0,1:T(1,128)S(1)}, f32[1,3,2048]{2,0,1:T(1,128)}, u32[]{:S(2)}) copy-start(f32[1,3,2048]{2,0,1:T(1,128)} %param.17) | copy-start | bytes 73732
  0.7 14.9 %copy-start.6 = (s32[1,32,2]{1,2,0:T(2,128)S(1)}, s32[1,32,2]{1,2,0:T(2,128)}, u32[]{:S(2)}) copy-start(s32[1,32,2]{1,2,0:T(2,128)} %param.16) | copy-start | bytes 772
  0.7 16.1 %copy-start.2 = (bf16[1,32,2048]{2,1,0:T(8,128)(2,1)S(1)}, bf16[1,32,2048]{2,1,0:T(8,128)(2,1)}, u32[]{:S(2)}) copy-start(bf16[1,32,2048]{2,1,0:T(8,128)(2,1)} %param.12) | copy-start | bytes 393220
  3.7 60.3 %collective-permute-start.5 = (bf16[2,2,1024,256]{3,2,1,0:T(8,128)(2,1)}, bf16[2,2,1024,256]{3,2,1,0:T(8,128)(2,1)S(1)}, u32[]{:S(2)}, u32[]{:S(2)}) collective-permute-start(bf16[2,2,1024,256]{3,2,1,0:T(8,128)(2,1)} %shard_map.133.own), channel_id=1, source_target_pairs={{0,15},{1,0},{2,1},{3,2},{4,3},{5,4},{6,5},{7,6},{8,7},{9,8},{10,9... | collective-permute-start | bytes 6291464 | tf_op jit(solution)/shard_map/ppermute | solution.py:283
  8.1 7.6 %collective-permute-start = (s32[1]{0:T(128)}, s32[1]{0:T(128)}, u32[]{:S(2)}, u32[]{:S(2)}) collective-permute-start(s32[1]{0:T(128)} %bitcast.1), channel_id=1, source_target_pairs={{0,256},{128,384},{1,257},{129,385},{2,258},{130,386},{3,259},{131... | collective-permute-start | bytes 20 | tf_op jit(solution)/shard_map/ppermute | solution.py:24
  13.5 3.2 %collective-permute-start.1 = (bf16[32,2048]{1,0:T(8,128)(2,1)S(1)}, bf16[32,2048]{1,0:T(8,128)(2,1)S(1)}, u32[]{:S(2)}, u32[]{:S(2)}) collective-permute-start(bf16[32,2048]{1,0:T(8,128)(2,1)S(1)} %bitcast.46), channel_id=1, source_target_pairs={{0,256},{128,384},{1,257},{129,385},{2,258},{130,386},{3,259},{131... | collective-permute-start | bytes 393224 | tf_op jit(solution)/shard_map/ppermute | solution.py:24
  18.7 38.0 %collective-permute-start.2 = (bf16[32,2176]{1,0:T(8,128)(2,1)S(1)}, bf16[32,2176]{1,0:T(8,128)(2,1)S(1)}, u32[]{:S(2)}, u32[]{:S(2)}) collective-permute-start(bf16[32,2176]{1,0:T(8,128)(2,1)S(1)} %get-tuple-element.16.own), channel_id=1, source_target_pairs={{0,4},{4,8},{8,12},{12,0},{1,5},{5,9},{9,13},{13,1},{2,6},{6,10},{... | collective-permute-start | bytes 417800 | tf_op jit(solution)/shard_map/ppermute | solution.py:29
  28.5 28.2 %collective-permute-start.3 = (bf16[32,2176]{1,0:T(8,128)(2,1)S(1)}, bf16[32,2176]{1,0:T(8,128)(2,1)S(1)}, u32[]{:S(2)}, u32[]{:S(2)}) collective-permute-start(bf16[32,2176]{1,0:T(8,128)(2,1)S(1)} %get-tuple-element.16.own), channel_id=1, source_target_pairs={{0,12},{4,0},{8,4},{12,8},{1,13},{5,1},{9,5},{13,9},{2,14},{6,2},{... | collective-permute-start | bytes 417800 | tf_op jit(solution)/shard_map/ppermute | solution.py:29
  32.2 31.0 %collective-permute-start.4 = (bf16[32,2176]{1,0:T(8,128)(2,1)S(1)}, bf16[32,2176]{1,0:T(8,128)(2,1)S(1)}, u32[]{:S(2)}, u32[]{:S(2)}) collective-permute-start(bf16[32,2176]{1,0:T(8,128)(2,1)S(1)} %get-tuple-element.16.own), channel_id=1, source_target_pairs={{0,8},{4,12},{8,0},{12,4},{1,9},{5,13},{9,1},{13,5},{2,10},{6,14},... | collective-permute-start | bytes 417800 | tf_op jit(solution)/shard_map/ppermute | solution.py:29
  64.2 27.8 %collective-permute-start.7 = (bf16[2,1024,256]{2,1,0:T(8,128)(2,1)S(1)}, bf16[2,1024,256]{2,1,0:T(8,128)(2,1)S(1)}, u32[]{:S(2)}, u32[]{:S(2)}) collective-permute-start(bf16[2,1024,256]{2,1,0:T(8,128)(2,1)S(1)} %get-tuple-element.20), channel_id=1, source_target_pairs={{0,15},{1,0},{2,1},{3,2},{4,3},{5,4},{6,5},{7,6},{8,7},{9,8},{10,9... | collective-permute-start | bytes 3145736 | tf_op jit(solution)/shard_map/ppermute | solution.py:309
  66.1 29.0 %collective-permute-start.6 = (bf16[2,2,1024,256]{3,2,1,0:T(8,128)(2,1)S(1)}, bf16[2,2,1024,256]{3,2,1,0:T(8,128)(2,1)S(1)}, u32[]{:S(2)}, u32[]{:S(2)}) collective-permute-start(bf16[2,2,1024,256]{3,2,1,0:T(8,128)(2,1)S(1)} %get-tuple-element.19.near_a), channel_id=1, source_target_pairs={{0,64},{64,0},{1,65},{65,1},{2,66},{66,2},{3,67},{67,3},{4,68},{68... | collective-permute-start | bytes 6291464 | tf_op jit(solution)/shard_map/ppermute | solution.py:29
  91.9 5.4 %copy-start = (bf16[2,2,1024,256]{3,2,1,0:T(8,128)(2,1)S(1)}, bf16[2,2,1024,256]{3,2,1,0:T(8,128)(2,1)}, u32[]{:S(2)}) copy-start(bf16[2,2,1024,256]{3,2,1,0:T(8,128)(2,1)} %shard_map.133.own) | copy-start | bytes 6291460
  92.0 5.4 %collective-permute-start.8 = (bf16[2,1024,256]{2,1,0:T(8,128)(2,1)S(1)}, bf16[2,1024,256]{2,1,0:T(8,128)(2,1)S(1)}, u32[]{:S(2)}, u32[]{:S(2)}) collective-permute-start(bf16[2,1024,256]{2,1,0:T(8,128)(2,1)S(1)} %shard_map.135.far_a), channel_id=1, source_target_pairs={{0,64},{64,0},{1,65},{65,1},{2,66},{66,2},{3,67},{67,3},{4,68},{68... | collective-permute-start | bytes 3145736 | tf_op jit(solution)/shard_map/ppermute | solution.py:29
  100.2 41.8 %copy-start.7 = (s32[1,32]{1,0:T(1,128)S(1)}, s32[1,32]{1,0:T(1,128)}, u32[]{:S(2)}) copy-start(s32[1,32]{1,0:T(1,128)} %param.23) | copy-start | bytes 388
  100.3 58.8 %copy-start.1 = (bf16[1,2048,512]{2,1,0:T(8,128)(2,1)S(1)}, bf16[1,2048,512]{2,1,0:T(8,128)(2,1)}, u32[]{:S(2)}) copy-start(bf16[1,2048,512]{2,1,0:T(8,128)(2,1)} %param.21) | copy-start | bytes 6291460
  100.3 58.8 %copy-start.3 = (f32[1,32,512]{2,1,0:T(8,128)S(1)}, f32[1,32,512]{2,1,0:T(8,128)}, u32[]{:S(2)}) copy-start(f32[1,32,512]{2,1,0:T(8,128)} %param.22) | copy-start | bytes 196612
  121.9 20.3 %collective-permute-start.9 = (bf16[32,2048]{1,0:T(8,128)(2,1)}, bf16[32,2048]{1,0:T(8,128)(2,1)S(1)}, u32[]{:S(2)}, u32[]{:S(2)}) collective-permute-start(bf16[32,2048]{1,0:T(8,128)(2,1)} %get-tuple-element.23), channel_id=1, source_target_pairs={{0,12},{4,0},{8,4},{12,8},{1,13},{5,1},{9,5},{13,9},{2,14},{6,2},{... | collective-permute-start | bytes 393224 | tf_op jit(solution)/shard_map/ppermute | solution.py:29
  128.6 19.7 %collective-permute-start.10 = (bf16[32,2048]{1,0:T(8,128)(2,1)S(1)}, bf16[32,2048]{1,0:T(8,128)(2,1)S(1)}, u32[]{:S(2)}, u32[]{:S(2)}) collective-permute-start(bf16[32,2048]{1,0:T(8,128)(2,1)S(1)} %get-tuple-element.24), channel_id=1, source_target_pairs={{0,4},{4,8},{8,12},{12,0},{1,5},{5,9},{9,13},{13,1},{2,6},{6,10},{... | collective-permute-start | bytes 393224 | tf_op jit(solution)/shard_map/ppermute | solution.py:29
  131.5 27.6 %collective-permute-start.11 = (bf16[32,2048]{1,0:T(8,128)(2,1)S(1)}, bf16[32,2048]{1,0:T(8,128)(2,1)S(1)}, u32[]{:S(2)}, u32[]{:S(2)}) collective-permute-start(bf16[32,2048]{1,0:T(8,128)(2,1)S(1)} %get-tuple-element.25), channel_id=1, source_target_pairs={{0,8},{4,12},{8,0},{12,4},{1,9},{5,13},{9,1},{13,5},{2,10},{6,14},... | collective-permute-start | bytes 393224 | tf_op jit(solution)/shard_map/ppermute | solution.py:29

commit v8 on v7

--- a/solution.py
+++ b/solution.py
@@ -278,7 +278,7 @@
         "svvvvv",
         (4 * tok_rows * LEN * model_width, 1 << 20),
     )(facts, hidden[0], arrived, gain_rows, router_rows, routes[0])
-    order = (1, 3, 2)
+    order = (2, 1, 3)
     visitors = [turned(block, "z4", k) for k in order]
     near_mine = lax.ppermute(shared, ("core", "z4", "zl"), onward)
     slots = 4 * capacity

time: 201 us -> 198 us (0.985)
  waiting for transfers between devices: 39.3 us -> 33.5 us
  starting transfers between devices: 65.3 us -> 69 us
    ppermute x8, waiting for transfers between devices: 38.9 us -> 33.1 us  [turned(): lax.ppermute(block, axis, [(i, (i + distance) % count) for i in range(cou...]
    ppermute x1, starting transfers between devices: 1.92 us -> 5.58 us  [local(): far_mine = lax.ppermute(relayed, ('core', 'z4', 'zl'), onward)]
  transfers between devices with their start and end apart: 12 -> 12, of which waited for: 6 -> 4; matrix products, arithmetic and copies ran while one was open for 0% -> 0% of each run, Pallas kernels for 1% -> 1%
where the time goes in v8:
time: 198 us; the launch traced here: 197 us
  blocking collectives  77.3 us (39%)
  starting transfers between devices  69 us (35%)
  waiting for transfers between devices  33.5 us (17%)
  Pallas kernels  11.8 us (6%)
  between operations  4.01 us (2%)
    ppermute x8, starting transfers between devices, turned(): lax.ppermute(block, axis, [(i, (i + distance) % count) for i in range(cou...  52.4 us
    ppermute x8, waiting for transfers between devices, turned(): lax.ppermute(block, axis, [(i, (i + distance) % count) for i in range(cou...  33.1 us
    all_to_all x1, blocking collectives, local(): lax.all_to_all(totals, far_axes, split_axis=0, concat_axis=0, tiled=True)  26.2 us
    all_to_all x1, blocking collectives, local(): rows = lax.all_to_all(packed, 'x', split_axis=0, concat_axis=0, tiled=True)  21.6 us
    all_to_all x1, blocking collectives, local(): lax.all_to_all(partial_out, 'x', split_axis=0, concat_axis=0, tiled=True)  20.2 us
    all_to_all x1, blocking collectives, local(): lax.all_to_all(totals, local_axes, split_axis=0, concat_axis=0, tiled=True)  9.28 us
    ppermute x2, starting transfers between devices, passed_along(): return lax.ppermute(block, axis, route)  6.68 us
    ppermute x1, starting transfers between devices, local(): far_mine = lax.ppermute(relayed, ('core', 'z4', 'zl'), onward)  5.58 us
  transfers between devices with their start and end apart: 12, of which 4 were waited for; matrix products, arithmetic and copies ran while one was open for 0% of the time, Pallas kernels for 1%

profile of v8, /device:TPU:1, one launch (start us, length us, event | category | flops | bytes accessed | tf_op | source)
XLA Modules:
  0.0 197.3 jit_solution(4198509915013697649)
XLA Ops:
  0.7 3.0 %shard_map.133.own = bf16[2,2,1024,256]{3,2,1,0:T(8,128)(2,1)} custom-call(bf16[2048,256]{1,0:T(8,128)(2,1)} %bitcast.40, bf16[256,2048]{1,0:T(8,128)(2,1)} %bitcast.41), custom_call_target="tpu_custom_call" | custom-call | bytes 4194304 | tf_op jit(solution)/shard_map/pallas_call | solution.py:254
  3.7 4.4 %collective-permute-start.5 = (bf16[2,2,1024,256]{3,2,1,0:T(8,128)(2,1)}, bf16[2,2,1024,256]{3,2,1,0:T(8,128)(2,1)S(1)}, u32[]{:S(2)}, u32[]{:S(2)}) collective-permute-start(bf16[2,2,1024,256]{3,2,1,0:T(8,128)(2,1)} %shard_map.133.own), channel_id=1, source_target_pairs={{0,15},{1,0},{2,1},{3,2},{4,3},{5,4},{6,5},{7,6},{8,7},{9,8},{10,9... | collective-permute-start | bytes 6291464 | tf_op jit(solution)/shard_map/ppermute | solution.py:283
  8.1 5.4 %collective-permute-start = (s32[1]{0:T(128)}, s32[1]{0:T(128)}, u32[]{:S(2)}, u32[]{:S(2)}) collective-permute-start(s32[1]{0:T(128)} %bitcast.1), channel_id=1, source_target_pairs={{0,256},{128,384},{1,257},{129,385},{2,258},{130,386},{3,259},{131... | collective-permute-start | bytes 20 | tf_op jit(solution)/shard_map/ppermute | solution.py:24
  13.5 1.3 collective-permute-start.1
  16.7 2.0 shard_map.131
  18.7 15.5 %collective-permute-start.2 = (bf16[32,2176]{1,0:T(8,128)(2,1)S(1)}, bf16[32,2176]{1,0:T(8,128)(2,1)S(1)}, u32[]{:S(2)}, u32[]{:S(2)}) collective-permute-start(bf16[32,2176]{1,0:T(8,128)(2,1)S(1)} %get-tuple-element.16.own), channel_id=1, source_target_pairs={{0,8},{4,12},{8,0},{12,4},{1,9},{5,13},{9,1},{13,5},{2,10},{6,14},... | collective-permute-start | bytes 417800 | tf_op jit(solution)/shard_map/ppermute | solution.py:29
  34.2 3.1 %collective-permute-start.3 = (bf16[32,2176]{1,0:T(8,128)(2,1)S(1)}, bf16[32,2176]{1,0:T(8,128)(2,1)S(1)}, u32[]{:S(2)}, u32[]{:S(2)}) collective-permute-start(bf16[32,2176]{1,0:T(8,128)(2,1)S(1)} %get-tuple-element.16.own), channel_id=1, source_target_pairs={{0,4},{4,8},{8,12},{12,0},{1,5},{5,9},{9,13},{13,1},{2,6},{6,10},{... | collective-permute-start | bytes 417800 | tf_op jit(solution)/shard_map/ppermute | solution.py:29
  37.3 6.1 %collective-permute-start.4 = (bf16[32,2176]{1,0:T(8,128)(2,1)S(1)}, bf16[32,2176]{1,0:T(8,128)(2,1)S(1)}, u32[]{:S(2)}, u32[]{:S(2)}) collective-permute-start(bf16[32,2176]{1,0:T(8,128)(2,1)S(1)} %get-tuple-element.16.own), channel_id=1, source_target_pairs={{0,12},{4,0},{8,4},{12,8},{1,13},{5,1},{9,5},{13,9},{2,14},{6,2},{... | collective-permute-start | bytes 417800 | tf_op jit(solution)/shard_map/ppermute | solution.py:29
  43.4 14.7 %collective-permute-done.2.b1 = bf16[32,2176]{1,0:T(8,128)(2,1)S(1)} collective-permute-done((bf16[32,2176]{1,0:T(8,128)(2,1)S(1)}, bf16[32,2176]{1,0:T(8,128)(2,1)S(1)}, u32[]{:S(2)}, u32[]{:S(2)}) %collective-permute-start.2) | collective-permute-done | bytes 139296 | tf_op jit(solution)/shard_map/ppermute | solution.py:29
  59.1 5.6 %collective-permute-start.7 = (bf16[2,1024,256]{2,1,0:T(8,128)(2,1)S(1)}, bf16[2,1024,256]{2,1,0:T(8,128)(2,1)S(1)}, u32[]{:S(2)}, u32[]{:S(2)}) collective-permute-start(bf16[2,1024,256]{2,1,0:T(8,128)(2,1)S(1)} %get-tuple-element.20), channel_id=1, source_target_pairs={{0,15},{1,0},{2,1},{3,2},{4,3},{5,4},{6,5},{7,6},{8,7},{9,8},{10,9... | collective-permute-start | bytes 3145736 | tf_op jit(solution)/shard_map/ppermute | solution.py:309
  64.6 5.7 %collective-permute-start.6 = (bf16[2,2,1024,256]{3,2,1,0:T(8,128)(2,1)S(1)}, bf16[2,2,1024,256]{3,2,1,0:T(8,128)(2,1)S(1)}, u32[]{:S(2)}, u32[]{:S(2)}) collective-permute-start(bf16[2,2,1024,256]{3,2,1,0:T(8,128)(2,1)S(1)} %get-tuple-element.19.near_a), channel_id=1, source_target_pairs={{0,64},{64,0},{1,65},{65,1},{2,66},{66,2},{3,67},{67,3},{4,68},{68... | collective-permute-start | bytes 6291464 | tf_op jit(solution)/shard_map/ppermute | solution.py:29
  70.4 21.6 %all_to_all.37 = bf16[4,80,2048]{2,1,0:T(8,128)(2,1)S(1)} all-to-all(bf16[4,80,2048]{2,1,0:T(8,128)(2,1)S(1)} %bitcast.34), channel_id=1, replica_groups=mesh['y'=4,'core'=2,'x'=4,'z4'=4,'zl'=4] {'x'}, dimensions={0} | all-to-all | bytes 2621440 | tf_op jit(solution)/shard_map/all_to_all | solution.py:311
  92.0 3.1 %collective-permute-start.8 = (bf16[2,1024,256]{2,1,0:T(8,128)(2,1)S(1)}, bf16[2,1024,256]{2,1,0:T(8,128)(2,1)S(1)}, u32[]{:S(2)}, u32[]{:S(2)}) collective-permute-start(bf16[2,1024,256]{2,1,0:T(8,128)(2,1)S(1)} %shard_map.135.far_a), channel_id=1, source_target_pairs={{0,64},{64,0},{1,65},{65,1},{2,66},{66,2},{3,67},{67,3},{4,68},{68... | collective-permute-start | bytes 3145736 | tf_op jit(solution)/shard_map/ppermute | solution.py:29
  95.1 2.3 %collective-permute-done.8.far_b = bf16[2,1024,256]{2,1,0:T(8,128)(2,1)S(1)} collective-permute-done((bf16[2,1024,256]{2,1,0:T(8,128)(2,1)S(1)}, bf16[2,1024,256]{2,1,0:T(8,128)(2,1)S(1)}, u32[]{:S(2)}, u32[]{:S(2)}) %collective-permute-start.8) | collective-permute-done | bytes 1048608 | tf_op jit(solution)/shard_map/ppermute | solution.py:29
  97.4 2.9 %shard_map.136 = bf16[320,2048]{1,0:T(8,128)(2,1)S(1)} custom-call(bf16[320,2048]{1,0:T(8,128)(2,1)S(1)} %bitcast.30, bf16[2,2,1024,256]{3,2,1,0:T(8,128)(2,1)S(1)} %copy-done, bf16[2,2,1024,256]{3,2,1,0:T(8,128)(2,1)S(1)} %get-tuple-element.19.near_a, bf16[2,2,1024,256]{3,2,1,0:T(8,128)(2,1)S(1)} %collective-permute-done.6.near_b, ...), custom_call_target="tpu_custom_call" | custom-call | flops 2684354560 | bytes 11534336 | tf_op jit(solution)/shard_map/pallas_call | solution.py:322
  100.3 20.2 %all_to_all.38 = bf16[4,80,2048]{2,1,0:T(8,128)(2,1)S(1)} all-to-all(bf16[4,80,2048]{2,1,0:T(8,128)(2,1)S(1)} %bitcast.32), channel_id=1, replica_groups=mesh['y'=4,'core'=2,'x'=4,'z4'=4,'zl'=4] {'x'}, dimensions={0} | all-to-all | bytes 2621440 | tf_op jit(solution)/shard_map/all_to_all | solution.py:335
  120.5 1.4 shard_map.137
  121.9 9.7 %collective-permute-start.9 = (bf16[32,2048]{1,0:T(8,128)(2,1)}, bf16[32,2048]{1,0:T(8,128)(2,1)S(1)}, u32[]{:S(2)}, u32[]{:S(2)}) collective-permute-start(bf16[32,2048]{1,0:T(8,128)(2,1)} %get-tuple-element.23), channel_id=1, source_target_pairs={{0,8},{4,12},{8,0},{12,4},{1,9},{5,13},{9,1},{13,5},{2,10},{6,14},... | collective-permute-start | bytes 393224 | tf_op jit(solution)/shard_map/ppermute | solution.py:29
  131.5 3.2 %collective-permute-start.10 = (bf16[32,2048]{1,0:T(8,128)(2,1)S(1)}, bf16[32,2048]{1,0:T(8,128)(2,1)S(1)}, u32[]{:S(2)}, u32[]{:S(2)}) collective-permute-start(bf16[32,2048]{1,0:T(8,128)(2,1)S(1)} %get-tuple-element.24), channel_id=1, source_target_pairs={{0,12},{4,0},{8,4},{12,8},{1,13},{5,1},{9,5},{13,9},{2,14},{6,2},{... | collective-permute-start | bytes 393224 | tf_op jit(solution)/shard_map/ppermute | solution.py:29
  134.7 6.0 %collective-permute-start.11 = (bf16[32,2048]{1,0:T(8,128)(2,1)S(1)}, bf16[32,2048]{1,0:T(8,128)(2,1)S(1)}, u32[]{:S(2)}, u32[]{:S(2)}) collective-permute-start(bf16[32,2048]{1,0:T(8,128)(2,1)S(1)} %get-tuple-element.25), channel_id=1, source_target_pairs={{0,4},{4,8},{8,12},{12,0},{1,5},{5,9},{9,13},{13,1},{2,6},{6,10},{... | collective-permute-start | bytes 393224 | tf_op jit(solution)/shard_map/ppermute | solution.py:29
  140.9 16.1 %collective-permute-done.10.p2 = bf16[32,2048]{1,0:T(8,128)(2,1)S(1)} collective-permute-done((bf16[32,2048]{1,0:T(8,128)(2,1)S(1)}, bf16[32,2048]{1,0:T(8,128)(2,1)S(1)}, u32[]{:S(2)}, u32[]{:S(2)}) %collective-permute-start.10) | collective-permute-done | bytes 131104 | tf_op jit(solution)/shard_map/ppermute | solution.py:29
  157.0 1.7 shard_map.138
  158.7 9.3 %all_to_all.39 = f32[16,1,128]{2,1,0:T(1,128)S(1)} all-to-all(f32[16,1,128]{2,1,0:T(1,128)S(1)} %bitcast.39), channel_id=1, replica_groups=mesh['y'=4,'core'=2,'x'=4,'z4'=4,'zl'=4] {'x','zl'}, dimensions={0} | all-to-all | bytes 16384 | tf_op jit(solution)/shard_map/all_to_all | solution.py:355
  168.0 26.2 %all_to_all.40 = f32[32,1,128]{2,1,0:T(1,128)S(1)} all-to-all(f32[32,1,128]{2,1,0:T(1,128)S(1)} %broadcast_in_dim.14), channel_id=1, replica_groups=mesh['y'=4,'core'=2,'x'=4,'z4'=4,'zl'=4] {'y','core','z4'}, dimensions={0} | all-to-all | bytes 32768 | tf_op jit(solution)/shard_map/all_to_all | solution.py:357
  (40 shorter events, 3.0 us)
Async XLA Ops:
  0.6 12.9 %copy-start.8 = (bf16[1,32,2048]{2,1,0:T(8,128)(2,1)S(1)}, bf16[1,32,2048]{2,1,0:T(8,128)(2,1)}, u32[]{:S(2)}) copy-start(bf16[1,32,2048]{2,1,0:T(8,128)(2,1)} %param.13) | copy-start | bytes 393220
  0.6 14.2 %copy-start.5 = (bf16[1,2048,4]{1,2,0:T(4,128)(2,1)S(1)}, bf16[1,2048,4]{1,2,0:T(4,128)(2,1)}, u32[]{:S(2)}) copy-start(bf16[1,2048,4]{1,2,0:T(4,128)(2,1)} %param.18) | copy-start | bytes 49156
  0.7 14.9 %copy-start.4 = (f32[1,3,2048]{2,0,1:T(1,128)S(1)}, f32[1,3,2048]{2,0,1:T(1,128)}, u32[]{:S(2)}) copy-start(f32[1,3,2048]{2,0,1:T(1,128)} %param.17) | copy-start | bytes 73732
  0.7 14.9 %copy-start.6 = (s32[1,32,2]{1,2,0:T(2,128)S(1)}, s32[1,32,2]{1,2,0:T(2,128)}, u32[]{:S(2)}) copy-start(s32[1,32,2]{1,2,0:T(2,128)} %param.16) | copy-start | bytes 772
  0.7 16.1 %copy-start.2 = (bf16[1,32,2048]{2,1,0:T(8,128)(2,1)S(1)}, bf16[1,32,2048]{2,1,0:T(8,128)(2,1)}, u32[]{:S(2)}) copy-start(bf16[1,32,2048]{2,1,0:T(8,128)(2,1)} %param.12) | copy-start | bytes 393220
  3.7 55.2 %collective-permute-start.5 = (bf16[2,2,1024,256]{3,2,1,0:T(8,128)(2,1)}, bf16[2,2,1024,256]{3,2,1,0:T(8,128)(2,1)S(1)}, u32[]{:S(2)}, u32[]{:S(2)}) collective-permute-start(bf16[2,2,1024,256]{3,2,1,0:T(8,128)(2,1)} %shard_map.133.own), channel_id=1, source_target_pairs={{0,15},{1,0},{2,1},{3,2},{4,3},{5,4},{6,5},{7,6},{8,7},{9,8},{10,9... | collective-permute-start | bytes 6291464 | tf_op jit(solution)/shard_map/ppermute | solution.py:283
  8.1 7.6 %collective-permute-start = (s32[1]{0:T(128)}, s32[1]{0:T(128)}, u32[]{:S(2)}, u32[]{:S(2)}) collective-permute-start(s32[1]{0:T(128)} %bitcast.1), channel_id=1, source_target_pairs={{0,256},{128,384},{1,257},{129,385},{2,258},{130,386},{3,259},{131... | collective-permute-start | bytes 20 | tf_op jit(solution)/shard_map/ppermute | solution.py:24
  13.5 3.2 %collective-permute-start.1 = (bf16[32,2048]{1,0:T(8,128)(2,1)S(1)}, bf16[32,2048]{1,0:T(8,128)(2,1)S(1)}, u32[]{:S(2)}, u32[]{:S(2)}) collective-permute-start(bf16[32,2048]{1,0:T(8,128)(2,1)S(1)} %bitcast.46), channel_id=1, source_target_pairs={{0,256},{128,384},{1,257},{129,385},{2,258},{130,386},{3,259},{131... | collective-permute-start | bytes 393224 | tf_op jit(solution)/shard_map/ppermute | solution.py:24
  18.7 39.4 %collective-permute-start.2 = (bf16[32,2176]{1,0:T(8,128)(2,1)S(1)}, bf16[32,2176]{1,0:T(8,128)(2,1)S(1)}, u32[]{:S(2)}, u32[]{:S(2)}) collective-permute-start(bf16[32,2176]{1,0:T(8,128)(2,1)S(1)} %get-tuple-element.16.own), channel_id=1, source_target_pairs={{0,8},{4,12},{8,0},{12,4},{1,9},{5,13},{9,1},{13,5},{2,10},{6,14},... | collective-permute-start | bytes 417800 | tf_op jit(solution)/shard_map/ppermute | solution.py:29
  34.2 23.9 %collective-permute-start.3 = (bf16[32,2176]{1,0:T(8,128)(2,1)S(1)}, bf16[32,2176]{1,0:T(8,128)(2,1)S(1)}, u32[]{:S(2)}, u32[]{:S(2)}) collective-permute-start(bf16[32,2176]{1,0:T(8,128)(2,1)S(1)} %get-tuple-element.16.own), channel_id=1, source_target_pairs={{0,4},{4,8},{8,12},{12,0},{1,5},{5,9},{9,13},{13,1},{2,6},{6,10},{... | collective-permute-start | bytes 417800 | tf_op jit(solution)/shard_map/ppermute | solution.py:29
  37.3 20.8 %collective-permute-start.4 = (bf16[32,2176]{1,0:T(8,128)(2,1)S(1)}, bf16[32,2176]{1,0:T(8,128)(2,1)S(1)}, u32[]{:S(2)}, u32[]{:S(2)}) collective-permute-start(bf16[32,2176]{1,0:T(8,128)(2,1)S(1)} %get-tuple-element.16.own), channel_id=1, source_target_pairs={{0,12},{4,0},{8,4},{12,8},{1,13},{5,1},{9,5},{13,9},{2,14},{6,2},{... | collective-permute-start | bytes 417800 | tf_op jit(solution)/shard_map/ppermute | solution.py:29
  59.1 32.9 %collective-permute-start.7 = (bf16[2,1024,256]{2,1,0:T(8,128)(2,1)S(1)}, bf16[2,1024,256]{2,1,0:T(8,128)(2,1)S(1)}, u32[]{:S(2)}, u32[]{:S(2)}) collective-permute-start(bf16[2,1024,256]{2,1,0:T(8,128)(2,1)S(1)} %get-tuple-element.20), channel_id=1, source_target_pairs={{0,15},{1,0},{2,1},{3,2},{4,3},{5,4},{6,5},{7,6},{8,7},{9,8},{10,9... | collective-permute-start | bytes 3145736 | tf_op jit(solution)/shard_map/ppermute | solution.py:309
  64.6 30.5 %collective-permute-start.6 = (bf16[2,2,1024,256]{3,2,1,0:T(8,128)(2,1)S(1)}, bf16[2,2,1024,256]{3,2,1,0:T(8,128)(2,1)S(1)}, u32[]{:S(2)}, u32[]{:S(2)}) collective-permute-start(bf16[2,2,1024,256]{3,2,1,0:T(8,128)(2,1)S(1)} %get-tuple-element.19.near_a), channel_id=1, source_target_pairs={{0,64},{64,0},{1,65},{65,1},{2,66},{66,2},{3,67},{67,3},{4,68},{68... | collective-permute-start | bytes 6291464 | tf_op jit(solution)/shard_map/ppermute | solution.py:29
  91.9 5.4 %copy-start = (bf16[2,2,1024,256]{3,2,1,0:T(8,128)(2,1)S(1)}, bf16[2,2,1024,256]{3,2,1,0:T(8,128)(2,1)}, u32[]{:S(2)}) copy-start(bf16[2,2,1024,256]{3,2,1,0:T(8,128)(2,1)} %shard_map.133.own) | copy-start | bytes 6291460
  92.0 5.4 %collective-permute-start.8 = (bf16[2,1024,256]{2,1,0:T(8,128)(2,1)S(1)}, bf16[2,1024,256]{2,1,0:T(8,128)(2,1)S(1)}, u32[]{:S(2)}, u32[]{:S(2)}) collective-permute-start(bf16[2,1024,256]{2,1,0:T(8,128)(2,1)S(1)} %shard_map.135.far_a), channel_id=1, source_target_pairs={{0,64},{64,0},{1,65},{65,1},{2,66},{66,2},{3,67},{67,3},{4,68},{68... | collective-permute-start | bytes 3145736 | tf_op jit(solution)/shard_map/ppermute | solution.py:29
  100.2 40.5 %copy-start.7 = (s32[1,32]{1,0:T(1,128)S(1)}, s32[1,32]{1,0:T(1,128)}, u32[]{:S(2)}) copy-start(s32[1,32]{1,0:T(1,128)} %param.23) | copy-start | bytes 388
  100.3 56.7 %copy-start.1 = (bf16[1,2048,512]{2,1,0:T(8,128)(2,1)S(1)}, bf16[1,2048,512]{2,1,0:T(8,128)(2,1)}, u32[]{:S(2)}) copy-start(bf16[1,2048,512]{2,1,0:T(8,128)(2,1)} %param.21) | copy-start | bytes 6291460
  100.3 56.7 %copy-start.3 = (f32[1,32,512]{2,1,0:T(8,128)S(1)}, f32[1,32,512]{2,1,0:T(8,128)}, u32[]{:S(2)}) copy-start(f32[1,32,512]{2,1,0:T(8,128)} %param.22) | copy-start | bytes 196612
  121.9 19.0 %collective-permute-start.9 = (bf16[32,2048]{1,0:T(8,128)(2,1)}, bf16[32,2048]{1,0:T(8,128)(2,1)S(1)}, u32[]{:S(2)}, u32[]{:S(2)}) collective-permute-start(bf16[32,2048]{1,0:T(8,128)(2,1)} %get-tuple-element.23), channel_id=1, source_target_pairs={{0,8},{4,12},{8,0},{12,4},{1,9},{5,13},{9,1},{13,5},{2,10},{6,14},... | collective-permute-start | bytes 393224 | tf_op jit(solution)/shard_map/ppermute | solution.py:29
  131.5 25.4 %collective-permute-start.10 = (bf16[32,2048]{1,0:T(8,128)(2,1)S(1)}, bf16[32,2048]{1,0:T(8,128)(2,1)S(1)}, u32[]{:S(2)}, u32[]{:S(2)}) collective-permute-start(bf16[32,2048]{1,0:T(8,128)(2,1)S(1)} %get-tuple-element.24), channel_id=1, source_target_pairs={{0,12},{4,0},{8,4},{12,8},{1,13},{5,1},{9,5},{13,9},{2,14},{6,2},{... | collective-permute-start | bytes 393224 | tf_op jit(solution)/shard_map/ppermute | solution.py:29
  134.7 22.3 %collective-permute-start.11 = (bf16[32,2048]{1,0:T(8,128)(2,1)S(1)}, bf16[32,2048]{1,0:T(8,128)(2,1)S(1)}, u32[]{:S(2)}, u32[]{:S(2)}) collective-permute-start(bf16[32,2048]{1,0:T(8,128)(2,1)S(1)} %get-tuple-element.25), channel_id=1, source_target_pairs={{0,4},{4,8},{8,12},{12,0},{1,5},{5,9},{9,13},{13,1},{2,6},{6,10},{... | collective-permute-start | bytes 393224 | tf_op jit(solution)/shard_map/ppermute | solution.py:29

commit v9 on v8

--- a/solution.py
+++ b/solution.py
@@ -70,11 +70,16 @@
     copy.wait()
 
 
-def later_body(block, after, out):
-    del block, after, out
-
-
-def mlp_body(rows, own, near_a, near_b, far_a, far_b, out, act):
+def later_body(block, one, two, three, out):
+    del block, one, two, three, out
+
+
+def mlp_body(
+    r0, r1, r2, r3, own, near_a, near_b, far_a, far_b, o0, o1, o2, o3, rows, act
+):
+    slots = r0.shape[0]
+    for k, r in enumerate((r0, r1, r2, r3)):
+        rows[k * slots : (k + 1) * slots, :] = r[...]
     half = own.shape[3] // 2
     deep = own.shape[2]
     hidden = 2 * half
@@ -94,9 +99,9 @@
     for p in range(2 * deep // hidden):
         at = slice(p * half, (p + 1) * half)
         panel = jnp.concatenate([o[1, at, :] for pair in pairs for o in pair], axis=0)
-        out[:, p * hidden : (p + 1) * hidden] = jnp.dot(
-            act[...], panel, preferred_element_type=f32
-        ).astype(bf16)
+        product = jnp.dot(act[...], panel, preferred_element_type=f32).astype(bf16)
+        for k, o in enumerate((o0, o1, o2, o3)):
+            o[:, p * hidden : (p + 1) * hidden] = product[k * slots : (k + 1) * slots]
 
 
 def normed_of(values, gain):
@@ -155,15 +160,15 @@
     block[:, width:] = jnp.where(lane < 8, upper, gates - upper).astype(bf16)
 
 
-def pack_body(slots, own, b1, b2, b3, rows, high, low):
-    width = rows.shape[1]
-    lanes = rows.shape[0]
+def pack_body(slots, facts, own, b1, b2, b3, r0, r1, r2, r3, high, low):
+    width = r0.shape[1]
+    lanes = 4 * slots
     tokens = jnp.concatenate([own[...], b1[...], b2[...], b3[...]], axis=0)
     count = tokens.shape[0]
     aux = tokens[:, width:]
     lane = lax.broadcasted_iota(jnp.int32, (128, lanes), 1)
     part = lax.broadcasted_iota(jnp.int32, (128, lanes), 0)
-    of_expert = lane // slots
+    of_expert = (lane // slots + facts[3]) % 4
     pick_high = (part == of_expert).astype(f32).astype(bf16)
     pick_low = (part == of_expert + 8).astype(f32).astype(bf16)
     gate_high = jnp.dot(aux, pick_high, preferred_element_type=f32)
@@ -176,16 +181,19 @@
     rank = jnp.dot(upto, chosen.astype(f32).astype(bf16), preferred_element_type=f32)
     slot = (lax.broadcasted_iota(jnp.int32, (count, lanes), 1) % slots + 1).astype(f32)
     here = jnp.where(chosen & (rank == slot), 1.0, 0.0)
-    rows[...] = lax.dot_general(
+    rows = lax.dot_general(
         here.astype(bf16), tokens[:, :width], (((0,), (0,)), ((), ())), preferred_element_type=f32
     ).astype(bf16)
+    for k, r in enumerate((r0, r1, r2, r3)):
+        r[...] = rows[k * slots : (k + 1) * slots]
     high[...] = (here * gate_high).astype(bf16)
     low[...] = (here * gate_low).astype(bf16)
 
 
-def combine_body(rows, high, low, own, o1, o2, o3):
-    value = jnp.dot(high[...], rows[...], preferred_element_type=f32) + jnp.dot(
-        low[...], rows[...], preferred_element_type=f32
+def combine_body(r0, r1, r2, r3, high, low, own, o1, o2, o3):
+    rows = jnp.concatenate([r0[...], r1[...], r2[...], r3[...]], axis=0)
+    value = jnp.dot(high[...], rows, preferred_element_type=f32) + jnp.dot(
+        low[...], rows, preferred_element_type=f32
     )
     n = own.shape[0]
     own[...] = value[:n]
@@ -268,7 +276,8 @@
     onward = [(i, (i - 1) % line) for i in range(line)] + [
         (line + i, line + (i + 1) % line) for i in range(line)
     ]
-    facts = jnp.stack([lengths[0, 0], arrived_length[0], decoder.astype(jnp.int32)])
+    facts = jnp.stack([lengths[0, 0], arrived_length[0], decoder.astype(jnp.int32),
+         lax.axis_index("x").astype(jnp.int32)])
     mid_states, block = kernel_call(
         before_body,
         (
@@ -283,16 +292,17 @@
     near_mine = lax.ppermute(shared, ("core", "z4", "zl"), onward)
     slots = 4 * capacity
     lanes = experts * slots
-    packed, gates_high, gates_low = kernel_call(
+    block_shape = jax.ShapeDtypeStruct((slots, model_width), bf16)
+    *packed, gates_high, gates_low = kernel_call(
         functools.partial(pack_body, slots),
-        (
-            jax.ShapeDtypeStruct((lanes, model_width), bf16),
-            jax.ShapeDtypeStruct((4 * tok_rows, lanes), bf16),
-            jax.ShapeDtypeStruct((4 * tok_rows, lanes), bf16),
-        ),
-        "vvvv",
+        (block_shape,) * 4 + (jax.ShapeDtypeStruct((4 * tok_rows, lanes), bf16),) * 2,
+        "svvvv",
         (2 * lanes * 4 * tok_rows * model_width, 2 << 20),
-    )(block, *visitors)
+    )(facts, block, *visitors)
+    across = (2, 1, 3)
+    rows = [packed[0], None, None, None]
+    for k in across:
+        rows[k] = turned(packed[k], "x", k)
     near_mine, relayed = pl.pallas_call(
         relay_body,
         out_shape=(
@@ -308,38 +318,40 @@
     )(core, near_mine, gates_high)
     far_mine = lax.ppermute(relayed, ("core", "z4", "zl"), onward)
     near_other = turned(near_mine, "core", 1)
-    rows = lax.all_to_all(packed, "x", split_axis=0, concat_axis=0, tiled=True)
     far_mine = pl.pallas_call(
         later_body,
         out_shape=jax.ShapeDtypeStruct(piece, bf16),
-        in_specs=[anywhere] * 2,
+        in_specs=[anywhere] * 4,
         out_specs=anywhere,
         input_output_aliases={0: 0},
         cost_estimate=pl.CostEstimate(flops=0, bytes_accessed=0, transcendentals=0),
         compiler_params=pltpu.CompilerParams(vmem_limit_bytes=4 << 20),
-    )(far_mine, rows)
+    )(far_mine, *rows[1:])
     far_other = turned(far_mine, "core", 1)
     partial_out = pl.pallas_call(
         mlp_body,
-        out_shape=jax.ShapeDtypeStruct((lanes, model_width), bf16),
-        in_specs=[whole] * 6,
-        out_specs=whole,
+        out_shape=(block_shape,) * 4,
+        in_specs=[whole] * 9,
+        out_specs=(whole,) * 4,
         scratch_shapes=[
+            pltpu.VMEM((lanes, model_width), bf16),
             pltpu.VMEM((lanes, 4 * model_hidden), bf16),
         ],
         cost_estimate=pl.CostEstimate(
             flops=16 * lanes * model_width * model_hidden, bytes_accessed=11 << 20, transcendentals=0
         ),
         compiler_params=pltpu.CompilerParams(vmem_limit_bytes=24 << 20),
-    )(rows, shared, near_mine, near_other, far_mine, far_other)
-    returned = lax.all_to_all(partial_out, "x", split_axis=0, concat_axis=0, tiled=True)
+    )(*rows, shared, near_mine, near_other, far_mine, far_other)
+    returned = [partial_out[0], None, None, None]
+    for k in across:
+        returned[k] = turned(partial_out[k], "x", -k)
     own_part, *parts = kernel_call(
         combine_body,
         (jax.ShapeDtypeStruct((tok_rows, model_width), f32),)
         + (jax.ShapeDtypeStruct((tok_rows, model_width), bf16),) * 3,
-        "vvv",
+        "vvvvvv",
         (4 * lanes * 4 * tok_rows * model_width, 2 << 20),
-    )(returned, gates_high, gates_low)
+    )(*returned, gates_high, gates_low)
     home = [turned(part, "z4", -k) for k, part in zip(order, parts)]
     local_axes, far_axes = ("x", "zl"), ("y", "core", "z4")
     members = [math.prod(lax.axis_size(a) for a in axes) for axes in (local_axes, far_axes)]

time: 198 us -> 204 us (1.030)
  blocking collectives: 77.3 us -> 36.1 us
  waiting for transfers between devices: 33.5 us -> 59.2 us
  starting transfers between devices: 69 us -> 89.1 us
    all_to_all x2 -> x0, blocking collectives: 41.8 us -> none  [the longest x1 21.6 us: local(): rows = lax.all_to_all(packed, 'x', split_axis=0, concat_axis=0, tiled=True)]
    ppermute x8 -> x14, waiting for transfers between devices: 33.1 us -> 58.8 us  [turned(): lax.ppermute(block, axis, [(i, (i + distance) % count) for i in range(cou...]
    ppermute x8 -> x14, starting transfers between devices: 52.4 us -> 72.5 us  [turned(): lax.ppermute(block, axis, [(i, (i + distance) % count) for i in range(cou...]
  transfers between devices with their start and end apart: 12 -> 18, of which waited for: 4 -> 10; matrix products, arithmetic and copies ran while one was open for 0% -> 0% of each run, Pallas kernels for 1% -> 2%
where the time goes in v9:
time: 204 us; the launch traced here: 203 us
  starting transfers between devices  89.1 us (44%)
  waiting for transfers between devices  59.2 us (29%)
  blocking collectives  36.1 us (18%)
  Pallas kernels  11.8 us (6%)
  between operations  4.12 us (2%)
  local copies, waits for them, and re-layouts  2.43 us (1%)
    ppermute x14, starting transfers between devices, turned(): lax.ppermute(block, axis, [(i, (i + distance) % count) for i in range(cou...  72.5 us
    ppermute x14, waiting for transfers between devices, turned(): lax.ppermute(block, axis, [(i, (i + distance) % count) for i in range(cou...  58.8 us
    all_to_all x1, blocking collectives, local(): lax.all_to_all(totals, far_axes, split_axis=0, concat_axis=0, tiled=True)  26.6 us
    all_to_all x1, blocking collectives, local(): lax.all_to_all(totals, local_axes, split_axis=0, concat_axis=0, tiled=True)  9.54 us
    ppermute x2, starting transfers between devices, passed_along(): return lax.ppermute(block, axis, route)  6.63 us
    ppermute x1, starting transfers between devices, local(): far_mine = lax.ppermute(relayed, ('core', 'z4', 'zl'), onward)  5.64 us
    ppermute x1, starting transfers between devices, local(): near_mine = lax.ppermute(shared, ('core', 'z4', 'zl'), onward)  4.37 us
  transfers between devices with their start and end apart: 18, of which 10 were waited for; matrix products, arithmetic and copies ran while one was open for 0% of the time, Pallas kernels for 2%

profile of v9, /device:TPU:1, one launch (start us, length us, event | category | flops | bytes accessed | tf_op | source)
XLA Modules:
  0.0 203.5 jit_solution(11818346351970292761)
XLA Ops:
  0.7 3.1 %shard_map.133.own = bf16[2,2,1024,256]{3,2,1,0:T(8,128)(2,1)} custom-call(bf16[2048,256]{1,0:T(8,128)(2,1)} %bitcast.32, bf16[256,2048]{1,0:T(8,128)(2,1)} %bitcast.33), custom_call_target="tpu_custom_call" | custom-call | bytes 4194304 | tf_op jit(solution)/shard_map/pallas_call | solution.py:262
  3.7 4.4 %collective-permute-start.8 = (bf16[2,2,1024,256]{3,2,1,0:T(8,128)(2,1)}, bf16[2,2,1024,256]{3,2,1,0:T(8,128)(2,1)S(1)}, u32[]{:S(2)}, u32[]{:S(2)}) collective-permute-start(bf16[2,2,1024,256]{3,2,1,0:T(8,128)(2,1)} %shard_map.133.own), channel_id=1, source_target_pairs={{0,15},{1,0},{2,1},{3,2},{4,3},{5,4},{6,5},{7,6},{8,7},{9,8},{10,9... | collective-permute-start | bytes 6291464 | tf_op jit(solution)/shard_map/ppermute | solution.py:292
  8.1 5.3 %collective-permute-start = (s32[1]{0:T(128)}, s32[1]{0:T(128)}, u32[]{:S(2)}, u32[]{:S(2)}) collective-permute-start(s32[1]{0:T(128)} %bitcast.1), channel_id=1, source_target_pairs={{0,256},{128,384},{1,257},{129,385},{2,258},{130,386},{3,259},{131... | collective-permute-start | bytes 20 | tf_op jit(solution)/shard_map/ppermute | solution.py:24
  18.6 15.5 %collective-permute-start.2 = (bf16[32,2176]{1,0:T(8,128)(2,1)S(1)}, bf16[32,2176]{1,0:T(8,128)(2,1)S(1)}, u32[]{:S(2)}, u32[]{:S(2)}) collective-permute-start(bf16[32,2176]{1,0:T(8,128)(2,1)S(1)} %get-tuple-element.23.own), channel_id=1, source_target_pairs={{0,8},{4,12},{8,0},{12,4},{1,9},{5,13},{9,1},{13,5},{2,10},{6,14},... | collective-permute-start | bytes 417800 | tf_op jit(solution)/shard_map/ppermute | solution.py:29
  34.1 3.1 %collective-permute-start.3 = (bf16[32,2176]{1,0:T(8,128)(2,1)S(1)}, bf16[32,2176]{1,0:T(8,128)(2,1)S(1)}, u32[]{:S(2)}, u32[]{:S(2)}) collective-permute-start(bf16[32,2176]{1,0:T(8,128)(2,1)S(1)} %get-tuple-element.23.own), channel_id=1, source_target_pairs={{0,4},{4,8},{8,12},{12,0},{1,5},{5,9},{9,13},{13,1},{2,6},{6,10},{... | collective-permute-start | bytes 417800 | tf_op jit(solution)/shard_map/ppermute | solution.py:29
  37.2 6.1 %collective-permute-start.4 = (bf16[32,2176]{1,0:T(8,128)(2,1)S(1)}, bf16[32,2176]{1,0:T(8,128)(2,1)S(1)}, u32[]{:S(2)}, u32[]{:S(2)}) collective-permute-start(bf16[32,2176]{1,0:T(8,128)(2,1)S(1)} %get-tuple-element.23.own), channel_id=1, source_target_pairs={{0,12},{4,0},{8,4},{12,8},{1,13},{5,1},{9,5},{13,9},{2,14},{6,2},{... | collective-permute-start | bytes 417800 | tf_op jit(solution)/shard_map/ppermute | solution.py:29
  43.3 14.8 %collective-permute-done.2.b1 = bf16[32,2176]{1,0:T(8,128)(2,1)S(1)} collective-permute-done((bf16[32,2176]{1,0:T(8,128)(2,1)S(1)}, bf16[32,2176]{1,0:T(8,128)(2,1)S(1)}, u32[]{:S(2)}, u32[]{:S(2)}) %collective-permute-start.2) | collective-permute-done | bytes 139296 | tf_op jit(solution)/shard_map/ppermute | solution.py:29
  59.7 5.6 %collective-permute-start.10 = (bf16[2,1024,256]{2,1,0:T(8,128)(2,1)S(1)}, bf16[2,1024,256]{2,1,0:T(8,128)(2,1)S(1)}, u32[]{:S(2)}, u32[]{:S(2)}) collective-permute-start(bf16[2,1024,256]{2,1,0:T(8,128)(2,1)S(1)} %get-tuple-element.30), channel_id=1, source_target_pairs={{0,15},{1,0},{2,1},{3,2},{4,3},{5,4},{6,5},{7,6},{8,7},{9,8},{10,9... | collective-permute-start | bytes 3145736 | tf_op jit(solution)/shard_map/ppermute | solution.py:319
  65.3 5.2 %collective-permute-start.9 = (bf16[2,2,1024,256]{3,2,1,0:T(8,128)(2,1)S(1)}, bf16[2,2,1024,256]{3,2,1,0:T(8,128)(2,1)S(1)}, u32[]{:S(2)}, u32[]{:S(2)}) collective-permute-start(bf16[2,2,1024,256]{3,2,1,0:T(8,128)(2,1)S(1)} %get-tuple-element.29.near_a), channel_id=1, source_target_pairs={{0,64},{64,0},{1,65},{65,1},{2,66},{66,2},{3,67},{67,3},{4,68},{68... | collective-permute-start | bytes 6291464 | tf_op jit(solution)/shard_map/ppermute | solution.py:29
  70.5 3.1 %collective-permute-start.5 = (bf16[80,2048]{1,0:T(8,128)(2,1)S(1)}, bf16[80,2048]{1,0:T(8,128)(2,1)S(1)}, u32[]{:S(2)}, u32[]{:S(2)}) collective-permute-start(bf16[80,2048]{1,0:T(8,128)(2,1)S(1)} %get-tuple-element.25), channel_id=1, source_target_pairs={{0,16},{16,32},{32,48},{48,0},{1,17},{17,33},{33,49},{49,1},{2,18}... | collective-permute-start | bytes 983048 | tf_op jit(solution)/shard_map/ppermute | solution.py:29
  73.7 4.4 %collective-permute-start.6 = (bf16[80,2048]{1,0:T(8,128)(2,1)S(1)}, bf16[80,2048]{1,0:T(8,128)(2,1)S(1)}, u32[]{:S(2)}, u32[]{:S(2)}) collective-permute-start(bf16[80,2048]{1,0:T(8,128)(2,1)S(1)} %get-tuple-element.26), channel_id=1, source_target_pairs={{0,32},{16,48},{32,0},{48,16},{1,33},{17,49},{33,1},{49,17},{2,34}... | collective-permute-start | bytes 983048 | tf_op jit(solution)/shard_map/ppermute | solution.py:29
  78.0 3.1 %collective-permute-start.7 = (bf16[80,2048]{1,0:T(8,128)(2,1)S(1)}, bf16[80,2048]{1,0:T(8,128)(2,1)S(1)}, u32[]{:S(2)}, u32[]{:S(2)}) collective-permute-start(bf16[80,2048]{1,0:T(8,128)(2,1)S(1)} %get-tuple-element.27), channel_id=1, source_target_pairs={{0,48},{16,0},{32,16},{48,32},{1,49},{17,1},{33,17},{49,33},{2,50}... | collective-permute-start | bytes 983048 | tf_op jit(solution)/shard_map/ppermute | solution.py:29
  83.0 8.0 %collective-permute-done.6.two.r2 = bf16[80,2048]{1,0:T(8,128)(2,1)S(1)} collective-permute-done((bf16[80,2048]{1,0:T(8,128)(2,1)S(1)}, bf16[80,2048]{1,0:T(8,128)(2,1)S(1)}, u32[]{:S(2)}, u32[]{:S(2)}) %collective-permute-start.6) | collective-permute-done | bytes 327712 | tf_op jit(solution)/shard_map/ppermute | solution.py:29
  92.2 3.0 %collective-permute-start.11 = (bf16[2,1024,256]{2,1,0:T(8,128)(2,1)S(1)}, bf16[2,1024,256]{2,1,0:T(8,128)(2,1)S(1)}, u32[]{:S(2)}, u32[]{:S(2)}) collective-permute-start(bf16[2,1024,256]{2,1,0:T(8,128)(2,1)S(1)} %shard_map.135.far_a), channel_id=1, source_target_pairs={{0,64},{64,0},{1,65},{65,1},{2,66},{66,2},{3,67},{67,3},{4,68},{68... | collective-permute-start | bytes 3145736 | tf_op jit(solution)/shard_map/ppermute | solution.py:29
  100.4 4.3 %collective-permute-start.12 = (bf16[80,2048]{1,0:T(8,128)(2,1)S(1)}, bf16[80,2048]{1,0:T(8,128)(2,1)S(1)}, u32[]{:S(2)}, u32[]{:S(2)}) collective-permute-start(bf16[80,2048]{1,0:T(8,128)(2,1)S(1)} %get-tuple-element.32), channel_id=1, source_target_pairs={{0,48},{16,0},{32,16},{48,32},{1,49},{17,1},{33,17},{49,33},{2,50}... | collective-permute-start | bytes 983048 | tf_op jit(solution)/shard_map/ppermute | solution.py:29
  104.6 3.4 %collective-permute-start.13 = (bf16[80,2048]{1,0:T(8,128)(2,1)S(1)}, bf16[80,2048]{1,0:T(8,128)(2,1)S(1)}, u32[]{:S(2)}, u32[]{:S(2)}) collective-permute-start(bf16[80,2048]{1,0:T(8,128)(2,1)S(1)} %get-tuple-element.33), channel_id=1, source_target_pairs={{0,32},{16,48},{32,0},{48,16},{1,33},{17,49},{33,1},{49,17},{2,34}... | collective-permute-start | bytes 983048 | tf_op jit(solution)/shard_map/ppermute | solution.py:29
  112.2 4.5 %collective-permute-done.13.r2 = bf16[80,2048]{1,0:T(8,128)(2,1)S(1)} collective-permute-done((bf16[80,2048]{1,0:T(8,128)(2,1)S(1)}, bf16[80,2048]{1,0:T(8,128)(2,1)S(1)}, u32[]{:S(2)}, u32[]{:S(2)}) %collective-permute-start.13) | collective-permute-done | bytes 327712 | tf_op jit(solution)/shard_map/ppermute | solution.py:29
  116.7 8.0 %collective-permute-done.14.r3 = bf16[80,2048]{1,0:T(8,128)(2,1)S(1)} collective-permute-done((bf16[80,2048]{1,0:T(8,128)(2,1)S(1)}, bf16[80,2048]{1,0:T(8,128)(2,1)S(1)}, u32[]{:S(2)}, u32[]{:S(2)}) %collective-permute-start.14) | collective-permute-done | bytes 327712 | tf_op jit(solution)/shard_map/ppermute | solution.py:29
  125.4 10.3 %collective-permute-start.15 = (bf16[32,2048]{1,0:T(8,128)(2,1)S(1)}, bf16[32,2048]{1,0:T(8,128)(2,1)S(1)}, u32[]{:S(2)}, u32[]{:S(2)}) collective-permute-start(bf16[32,2048]{1,0:T(8,128)(2,1)S(1)} %get-tuple-element.37), channel_id=1, source_target_pairs={{0,8},{4,12},{8,0},{12,4},{1,9},{5,13},{9,1},{13,5},{2,10},{6,14},... | collective-permute-start | bytes 393224 | tf_op jit(solution)/shard_map/ppermute | solution.py:29
  135.7 3.0 %collective-permute-start.16 = (bf16[32,2048]{1,0:T(8,128)(2,1)S(1)}, bf16[32,2048]{1,0:T(8,128)(2,1)S(1)}, u32[]{:S(2)}, u32[]{:S(2)}) collective-permute-start(bf16[32,2048]{1,0:T(8,128)(2,1)S(1)} %get-tuple-element.38), channel_id=1, source_target_pairs={{0,12},{4,0},{8,4},{12,8},{1,13},{5,1},{9,5},{13,9},{2,14},{6,2},{... | collective-permute-start | bytes 393224 | tf_op jit(solution)/shard_map/ppermute | solution.py:29
  138.7 6.2 %collective-permute-start.17 = (bf16[32,2048]{1,0:T(8,128)(2,1)S(1)}, bf16[32,2048]{1,0:T(8,128)(2,1)S(1)}, u32[]{:S(2)}, u32[]{:S(2)}) collective-permute-start(bf16[32,2048]{1,0:T(8,128)(2,1)S(1)} %get-tuple-element.39), channel_id=1, source_target_pairs={{0,4},{4,8},{8,12},{12,0},{1,5},{5,9},{9,13},{13,1},{2,6},{6,10},{... | collective-permute-start | bytes 393224 | tf_op jit(solution)/shard_map/ppermute | solution.py:29
  145.0 15.9 %collective-permute-done.16.p2 = bf16[32,2048]{1,0:T(8,128)(2,1)S(1)} collective-permute-done((bf16[32,2048]{1,0:T(8,128)(2,1)S(1)}, bf16[32,2048]{1,0:T(8,128)(2,1)S(1)}, u32[]{:S(2)}, u32[]{:S(2)}) %collective-permute-start.16) | collective-permute-done | bytes 131104 | tf_op jit(solution)/shard_map/ppermute | solution.py:29
  164.2 9.5 %all_to_all.15 = f32[16,1,128]{2,1,0:T(1,128)S(1)} all-to-all(f32[16,1,128]{2,1,0:T(1,128)S(1)} %bitcast.31), channel_id=1, replica_groups=mesh['y'=4,'core'=2,'x'=4,'z4'=4,'zl'=4] {'x','zl'}, dimensions={0} | all-to-all | bytes 16384 | tf_op jit(solution)/shard_map/all_to_all | solution.py:367
  173.8 26.6 %all_to_all.16 = f32[32,1,128]{2,1,0:T(1,128)S(1)} all-to-all(f32[32,1,128]{2,1,0:T(1,128)S(1)} %broadcast_in_dim.14), channel_id=1, replica_groups=mesh['y'=4,'core'=2,'x'=4,'z4'=4,'zl'=4] {'y','core','z4'}, dimensions={0} | all-to-all | bytes 32768 | tf_op jit(solution)/shard_map/all_to_all | solution.py:369
  (50 shorter events, 23.0 us)
Async XLA Ops:
  0.7 14.8 %copy-start.4 = (f32[1,3,2048]{2,0,1:T(1,128)S(1)}, f32[1,3,2048]{2,0,1:T(1,128)}, u32[]{:S(2)}) copy-start(f32[1,3,2048]{2,0,1:T(1,128)} %param.17) | copy-start | bytes 73732
  0.7 14.9 %copy-start.6 = (s32[1,32,2]{1,2,0:T(2,128)S(1)}, s32[1,32,2]{1,2,0:T(2,128)}, u32[]{:S(2)}) copy-start(s32[1,32,2]{1,2,0:T(2,128)} %param.16) | copy-start | bytes 772
  0.7 16.0 %copy-start.2 = (bf16[1,32,2048]{2,1,0:T(8,128)(2,1)S(1)}, bf16[1,32,2048]{2,1,0:T(8,128)(2,1)}, u32[]{:S(2)}) copy-start(bf16[1,32,2048]{2,1,0:T(8,128)(2,1)} %param.12) | copy-start | bytes 393220
  3.7 55.8 %collective-permute-start.8 = (bf16[2,2,1024,256]{3,2,1,0:T(8,128)(2,1)}, bf16[2,2,1024,256]{3,2,1,0:T(8,128)(2,1)S(1)}, u32[]{:S(2)}, u32[]{:S(2)}) collective-permute-start(bf16[2,2,1024,256]{3,2,1,0:T(8,128)(2,1)} %shard_map.133.own), channel_id=1, source_target_pairs={{0,15},{1,0},{2,1},{3,2},{4,3},{5,4},{6,5},{7,6},{8,7},{9,8},{10,9... | collective-permute-start | bytes 6291464 | tf_op jit(solution)/shard_map/ppermute | solution.py:292
  8.1 7.5 %collective-permute-start = (s32[1]{0:T(128)}, s32[1]{0:T(128)}, u32[]{:S(2)}, u32[]{:S(2)}) collective-permute-start(s32[1]{0:T(128)} %bitcast.1), channel_id=1, source_target_pairs={{0,256},{128,384},{1,257},{129,385},{2,258},{130,386},{3,259},{131... | collective-permute-start | bytes 20 | tf_op jit(solution)/shard_map/ppermute | solution.py:24
  13.5 3.2 %collective-permute-start.1 = (bf16[32,2048]{1,0:T(8,128)(2,1)S(1)}, bf16[32,2048]{1,0:T(8,128)(2,1)S(1)}, u32[]{:S(2)}, u32[]{:S(2)}) collective-permute-start(bf16[32,2048]{1,0:T(8,128)(2,1)S(1)} %bitcast.38), channel_id=1, source_target_pairs={{0,256},{128,384},{1,257},{129,385},{2,258},{130,386},{3,259},{131... | collective-permute-start | bytes 393224 | tf_op jit(solution)/shard_map/ppermute | solution.py:24
  18.6 39.5 %collective-permute-start.2 = (bf16[32,2176]{1,0:T(8,128)(2,1)S(1)}, bf16[32,2176]{1,0:T(8,128)(2,1)S(1)}, u32[]{:S(2)}, u32[]{:S(2)}) collective-permute-start(bf16[32,2176]{1,0:T(8,128)(2,1)S(1)} %get-tuple-element.23.own), channel_id=1, source_target_pairs={{0,8},{4,12},{8,0},{12,4},{1,9},{5,13},{9,1},{13,5},{2,10},{6,14},... | collective-permute-start | bytes 417800 | tf_op jit(solution)/shard_map/ppermute | solution.py:29
  34.1 24.1 %collective-permute-start.3 = (bf16[32,2176]{1,0:T(8,128)(2,1)S(1)}, bf16[32,2176]{1,0:T(8,128)(2,1)S(1)}, u32[]{:S(2)}, u32[]{:S(2)}) collective-permute-start(bf16[32,2176]{1,0:T(8,128)(2,1)S(1)} %get-tuple-element.23.own), channel_id=1, source_target_pairs={{0,4},{4,8},{8,12},{12,0},{1,5},{5,9},{9,13},{13,1},{2,6},{6,10},{... | collective-permute-start | bytes 417800 | tf_op jit(solution)/shard_map/ppermute | solution.py:29
  37.2 21.0 %collective-permute-start.4 = (bf16[32,2176]{1,0:T(8,128)(2,1)S(1)}, bf16[32,2176]{1,0:T(8,128)(2,1)S(1)}, u32[]{:S(2)}, u32[]{:S(2)}) collective-permute-start(bf16[32,2176]{1,0:T(8,128)(2,1)S(1)} %get-tuple-element.23.own), channel_id=1, source_target_pairs={{0,12},{4,0},{8,4},{12,8},{1,13},{5,1},{9,5},{13,9},{2,14},{6,2},{... | collective-permute-start | bytes 417800 | tf_op jit(solution)/shard_map/ppermute | solution.py:29
  59.6 37.9 %copy-start.1 = (bf16[2,2,1024,256]{3,2,1,0:T(8,128)(2,1)S(1)}, bf16[2,2,1024,256]{3,2,1,0:T(8,128)(2,1)}, u32[]{:S(2)}) copy-start(bf16[2,2,1024,256]{3,2,1,0:T(8,128)(2,1)} %shard_map.133.own) | copy-start | bytes 6291460
  59.7 32.5 %collective-permute-start.10 = (bf16[2,1024,256]{2,1,0:T(8,128)(2,1)S(1)}, bf16[2,1024,256]{2,1,0:T(8,128)(2,1)S(1)}, u32[]{:S(2)}, u32[]{:S(2)}) collective-permute-start(bf16[2,1024,256]{2,1,0:T(8,128)(2,1)S(1)} %get-tuple-element.30), channel_id=1, source_target_pairs={{0,15},{1,0},{2,1},{3,2},{4,3},{5,4},{6,5},{7,6},{8,7},{9,8},{10,9... | collective-permute-start | bytes 3145736 | tf_op jit(solution)/shard_map/ppermute | solution.py:319
  65.3 29.9 %collective-permute-start.9 = (bf16[2,2,1024,256]{3,2,1,0:T(8,128)(2,1)S(1)}, bf16[2,2,1024,256]{3,2,1,0:T(8,128)(2,1)S(1)}, u32[]{:S(2)}, u32[]{:S(2)}) collective-permute-start(bf16[2,2,1024,256]{3,2,1,0:T(8,128)(2,1)S(1)} %get-tuple-element.29.near_a), channel_id=1, source_target_pairs={{0,64},{64,0},{1,65},{65,1},{2,66},{66,2},{3,67},{67,3},{4,68},{68... | collective-permute-start | bytes 6291464 | tf_op jit(solution)/shard_map/ppermute | solution.py:29
  70.5 12.4 %collective-permute-start.5 = (bf16[80,2048]{1,0:T(8,128)(2,1)S(1)}, bf16[80,2048]{1,0:T(8,128)(2,1)S(1)}, u32[]{:S(2)}, u32[]{:S(2)}) collective-permute-start(bf16[80,2048]{1,0:T(8,128)(2,1)S(1)} %get-tuple-element.25), channel_id=1, source_target_pairs={{0,16},{16,32},{32,48},{48,0},{1,17},{17,33},{33,49},{49,1},{2,18}... | collective-permute-start | bytes 983048 | tf_op jit(solution)/shard_map/ppermute | solution.py:29
  73.7 17.3 %collective-permute-start.6 = (bf16[80,2048]{1,0:T(8,128)(2,1)S(1)}, bf16[80,2048]{1,0:T(8,128)(2,1)S(1)}, u32[]{:S(2)}, u32[]{:S(2)}) collective-permute-start(bf16[80,2048]{1,0:T(8,128)(2,1)S(1)} %get-tuple-element.26), channel_id=1, source_target_pairs={{0,32},{16,48},{32,0},{48,16},{1,33},{17,49},{33,1},{49,17},{2,34}... | collective-permute-start | bytes 983048 | tf_op jit(solution)/shard_map/ppermute | solution.py:29
  78.0 14.2 %collective-permute-start.7 = (bf16[80,2048]{1,0:T(8,128)(2,1)S(1)}, bf16[80,2048]{1,0:T(8,128)(2,1)S(1)}, u32[]{:S(2)}, u32[]{:S(2)}) collective-permute-start(bf16[80,2048]{1,0:T(8,128)(2,1)S(1)} %get-tuple-element.27), channel_id=1, source_target_pairs={{0,48},{16,0},{32,16},{48,32},{1,49},{17,1},{33,17},{49,33},{2,50}... | collective-permute-start | bytes 983048 | tf_op jit(solution)/shard_map/ppermute | solution.py:29
  92.2 5.3 %collective-permute-start.11 = (bf16[2,1024,256]{2,1,0:T(8,128)(2,1)S(1)}, bf16[2,1024,256]{2,1,0:T(8,128)(2,1)S(1)}, u32[]{:S(2)}, u32[]{:S(2)}) collective-permute-start(bf16[2,1024,256]{2,1,0:T(8,128)(2,1)S(1)} %shard_map.135.far_a), channel_id=1, source_target_pairs={{0,64},{64,0},{1,65},{65,1},{2,66},{66,2},{3,67},{67,3},{4,68},{68... | collective-permute-start | bytes 3145736 | tf_op jit(solution)/shard_map/ppermute | solution.py:29
  97.5 47.4 %copy-start.7 = (s32[1,32]{1,0:T(1,128)S(1)}, s32[1,32]{1,0:T(1,128)}, u32[]{:S(2)}) copy-start(s32[1,32]{1,0:T(1,128)} %param.23) | copy-start | bytes 388
  97.5 63.4 %copy-start.3 = (f32[1,32,512]{2,1,0:T(8,128)S(1)}, f32[1,32,512]{2,1,0:T(8,128)}, u32[]{:S(2)}) copy-start(f32[1,32,512]{2,1,0:T(8,128)} %param.22) | copy-start | bytes 196612
  100.4 11.8 %collective-permute-start.12 = (bf16[80,2048]{1,0:T(8,128)(2,1)S(1)}, bf16[80,2048]{1,0:T(8,128)(2,1)S(1)}, u32[]{:S(2)}, u32[]{:S(2)}) collective-permute-start(bf16[80,2048]{1,0:T(8,128)(2,1)S(1)} %get-tuple-element.32), channel_id=1, source_target_pairs={{0,48},{16,0},{32,16},{48,32},{1,49},{17,1},{33,17},{49,33},{2,50}... | collective-permute-start | bytes 983048 | tf_op jit(solution)/shard_map/ppermute | solution.py:29
  104.6 12.0 %collective-permute-start.13 = (bf16[80,2048]{1,0:T(8,128)(2,1)S(1)}, bf16[80,2048]{1,0:T(8,128)(2,1)S(1)}, u32[]{:S(2)}, u32[]{:S(2)}) collective-permute-start(bf16[80,2048]{1,0:T(8,128)(2,1)S(1)} %get-tuple-element.33), channel_id=1, source_target_pairs={{0,32},{16,48},{32,0},{48,16},{1,33},{17,49},{33,1},{49,17},{2,34}... | collective-permute-start | bytes 983048 | tf_op jit(solution)/shard_map/ppermute | solution.py:29
  108.1 16.6 %collective-permute-start.14 = (bf16[80,2048]{1,0:T(8,128)(2,1)S(1)}, bf16[80,2048]{1,0:T(8,128)(2,1)S(1)}, u32[]{:S(2)}, u32[]{:S(2)}) collective-permute-start(bf16[80,2048]{1,0:T(8,128)(2,1)S(1)} %get-tuple-element.34), channel_id=1, source_target_pairs={{0,16},{16,32},{32,48},{48,0},{1,17},{17,33},{33,49},{49,1},{2,18}... | collective-permute-start | bytes 983048 | tf_op jit(solution)/shard_map/ppermute | solution.py:29
  125.4 19.6 %collective-permute-start.15 = (bf16[32,2048]{1,0:T(8,128)(2,1)S(1)}, bf16[32,2048]{1,0:T(8,128)(2,1)S(1)}, u32[]{:S(2)}, u32[]{:S(2)}) collective-permute-start(bf16[32,2048]{1,0:T(8,128)(2,1)S(1)} %get-tuple-element.37), channel_id=1, source_target_pairs={{0,8},{4,12},{8,0},{12,4},{1,9},{5,13},{9,1},{13,5},{2,10},{6,14},... | collective-permute-start | bytes 393224 | tf_op jit(solution)/shard_map/ppermute | solution.py:29
  135.7 25.2 %collective-permute-start.16 = (bf16[32,2048]{1,0:T(8,128)(2,1)S(1)}, bf16[32,2048]{1,0:T(8,128)(2,1)S(1)}, u32[]{:S(2)}, u32[]{:S(2)}) collective-permute-start(bf16[32,2048]{1,0:T(8,128)(2,1)S(1)} %get-tuple-element.38), channel_id=1, source_target_pairs={{0,12},{4,0},{8,4},{12,8},{1,13},{5,1},{9,5},{13,9},{2,14},{6,2},{... | collective-permute-start | bytes 393224 | tf_op jit(solution)/shard_map/ppermute | solution.py:29
  138.7 22.2 %collective-permute-start.17 = (bf16[32,2048]{1,0:T(8,128)(2,1)S(1)}, bf16[32,2048]{1,0:T(8,128)(2,1)S(1)}, u32[]{:S(2)}, u32[]{:S(2)}) collective-permute-start(bf16[32,2048]{1,0:T(8,128)(2,1)S(1)} %get-tuple-element.39), channel_id=1, source_target_pairs={{0,4},{4,8},{8,12},{12,0},{1,5},{5,9},{9,13},{13,1},{2,6},{6,10},{... | collective-permute-start | bytes 393224 | tf_op jit(solution)/shard_map/ppermute | solution.py:29
  (3 other events, 28.6 us)

commit v10 on v8

--- a/solution.py
+++ b/solution.py
@@ -68,10 +68,6 @@
     copy = pltpu.make_async_copy(near.at[core[0]], out, sem)
     copy.start()
     copy.wait()
-
-
-def later_body(block, after, out):
-    del block, after, out
 
 
 def mlp_body(rows, own, near_a, near_b, far_a, far_b, out, act):
@@ -307,18 +303,10 @@
         compiler_params=pltpu.CompilerParams(vmem_limit_bytes=8 << 20),
     )(core, near_mine, gates_high)
     far_mine = lax.ppermute(relayed, ("core", "z4", "zl"), onward)
+    crossing = [(i, (j + line) % (2 * line)) for i, j in onward]
+    far_other = lax.ppermute(relayed, ("core", "z4", "zl"), crossing)
     near_other = turned(near_mine, "core", 1)
     rows = lax.all_to_all(packed, "x", split_axis=0, concat_axis=0, tiled=True)
-    far_mine = pl.pallas_call(
-        later_body,
-        out_shape=jax.ShapeDtypeStruct(piece, bf16),
-        in_specs=[anywhere] * 2,
-        out_specs=anywhere,
-        input_output_aliases={0: 0},
-        cost_estimate=pl.CostEstimate(flops=0, bytes_accessed=0, transcendentals=0),
-        compiler_params=pltpu.CompilerParams(vmem_limit_bytes=4 << 20),
-    )(far_mine, rows)
-    far_other = turned(far_mine, "core", 1)
     partial_out = pl.pallas_call(
         mlp_body,
         out_shape=jax.ShapeDtypeStruct((lanes, model_width), bf16),

time: 198 us -> 197 us (level)
  waiting for transfers between devices: 33.5 us -> 24.5 us
  blocking collectives: 77.3 us -> 85.1 us
    ppermute x8 -> x7, waiting for transfers between devices: 33.1 us -> 21.5 us  [turned(): lax.ppermute(block, axis, [(i, (i + distance) % count) for i in range(cou...]
    all_to_all x1, blocking collectives: 9.28 us -> 18.9 us  [local(): lax.all_to_all(totals, local_axes, split_axis=0, concat_axis=0, tiled=True)]
    ppermute x0 -> x1, waiting for transfers between devices: none -> 2.68 us  [local(): far_other = lax.ppermute(relayed, ('core', 'z4', 'zl'), crossing)]
    ppermute x1, starting transfers between devices: 5.58 us -> 3.26 us  [local(): far_mine = lax.ppermute(relayed, ('core', 'z4', 'zl'), onward)]
    ppermute x0 -> x1, starting transfers between devices: none -> 2.2 us  [local(): far_other = lax.ppermute(relayed, ('core', 'z4', 'zl'), crossing)]
    all_to_all x1, blocking collectives: 21.6 us -> 19.4 us  [local(): rows = lax.all_to_all(packed, 'x', split_axis=0, concat_axis=0, tiled=True)]
    ppermute x8 -> x7, starting transfers between devices: 52.4 us -> 53.2 us  [turned(): lax.ppermute(block, axis, [(i, (i + distance) % count) for i in range(cou...]
  transfers between devices with their start and end apart: 12 -> 12, of which waited for: 4 -> 5; matrix products, arithmetic and copies ran while one was open for 0% -> 0% of each run, Pallas kernels for 1% -> 1%
where the time goes in v10:
time: 197 us
  blocking collectives  85.1 us (43%)
  starting transfers between devices  69.8 us (35%)
  waiting for transfers between devices  24.5 us (12%)
  Pallas kernels  11.8 us (6%)
  between operations  4.01 us (2%)
    ppermute x7, starting transfers between devices, turned(): lax.ppermute(block, axis, [(i, (i + distance) % count) for i in range(cou...  53.2 us
    all_to_all x1, blocking collectives, local(): lax.all_to_all(totals, far_axes, split_axis=0, concat_axis=0, tiled=True)  26.8 us
    ppermute x7, waiting for transfers between devices, turned(): lax.ppermute(block, axis, [(i, (i + distance) % count) for i in range(cou...  21.5 us
    all_to_all x1, blocking collectives, local(): lax.all_to_all(partial_out, 'x', split_axis=0, concat_axis=0, tiled=True)  20 us
    all_to_all x1, blocking collectives, local(): rows = lax.all_to_all(packed, 'x', split_axis=0, concat_axis=0, tiled=True)  19.4 us
    all_to_all x1, blocking collectives, local(): lax.all_to_all(totals, local_axes, split_axis=0, concat_axis=0, tiled=True)  18.9 us
    ppermute x2, starting transfers between devices, passed_along(): return lax.ppermute(block, axis, route)  6.68 us
    ppermute x1, starting transfers between devices, local(): near_mine = lax.ppermute(shared, ('core', 'z4', 'zl'), onward)  4.37 us
  transfers between devices with their start and end apart: 12, of which 5 were waited for; matrix products, arithmetic and copies ran while one was open for 0% of the time, Pallas kernels for 1%

profile of v10, /device:TPU:1, one launch (start us, length us, event | category | flops | bytes accessed | tf_op | source)
XLA Modules:
  0.0 196.8 jit_solution(13063517665891158333)
XLA Ops:
  0.7 3.0 %shard_map.133.own = bf16[2,2,1024,256]{3,2,1,0:T(8,128)(2,1)} custom-call(bf16[2048,256]{1,0:T(8,128)(2,1)} %bitcast.39, bf16[256,2048]{1,0:T(8,128)(2,1)} %bitcast.40), custom_call_target="tpu_custom_call" | custom-call | bytes 4194304 | tf_op jit(solution)/shard_map/pallas_call | solution.py:250
  3.7 4.4 %collective-permute-start.5 = (bf16[2,2,1024,256]{3,2,1,0:T(8,128)(2,1)}, bf16[2,2,1024,256]{3,2,1,0:T(8,128)(2,1)S(1)}, u32[]{:S(2)}, u32[]{:S(2)}) collective-permute-start(bf16[2,2,1024,256]{3,2,1,0:T(8,128)(2,1)} %shard_map.133.own), channel_id=1, source_target_pairs={{0,15},{1,0},{2,1},{3,2},{4,3},{5,4},{6,5},{7,6},{8,7},{9,8},{10,9... | collective-permute-start | bytes 6291464 | tf_op jit(solution)/shard_map/ppermute | solution.py:279
  8.1 5.4 %collective-permute-start = (s32[1]{0:T(128)}, s32[1]{0:T(128)}, u32[]{:S(2)}, u32[]{:S(2)}) collective-permute-start(s32[1]{0:T(128)} %bitcast.1), channel_id=1, source_target_pairs={{0,256},{128,384},{1,257},{129,385},{2,258},{130,386},{3,259},{131... | collective-permute-start | bytes 20 | tf_op jit(solution)/shard_map/ppermute | solution.py:24
  16.7 2.0 shard_map.131
  18.7 15.5 %collective-permute-start.2 = (bf16[32,2176]{1,0:T(8,128)(2,1)S(1)}, bf16[32,2176]{1,0:T(8,128)(2,1)S(1)}, u32[]{:S(2)}, u32[]{:S(2)}) collective-permute-start(bf16[32,2176]{1,0:T(8,128)(2,1)S(1)} %get-tuple-element.16.own), channel_id=1, source_target_pairs={{0,8},{4,12},{8,0},{12,4},{1,9},{5,13},{9,1},{13,5},{2,10},{6,14},... | collective-permute-start | bytes 417800 | tf_op jit(solution)/shard_map/ppermute | solution.py:29
  34.2 3.1 %collective-permute-start.3 = (bf16[32,2176]{1,0:T(8,128)(2,1)S(1)}, bf16[32,2176]{1,0:T(8,128)(2,1)S(1)}, u32[]{:S(2)}, u32[]{:S(2)}) collective-permute-start(bf16[32,2176]{1,0:T(8,128)(2,1)S(1)} %get-tuple-element.16.own), channel_id=1, source_target_pairs={{0,4},{4,8},{8,12},{12,0},{1,5},{5,9},{9,13},{13,1},{2,6},{6,10},{... | collective-permute-start | bytes 417800 | tf_op jit(solution)/shard_map/ppermute | solution.py:29
  37.3 6.1 %collective-permute-start.4 = (bf16[32,2176]{1,0:T(8,128)(2,1)S(1)}, bf16[32,2176]{1,0:T(8,128)(2,1)S(1)}, u32[]{:S(2)}, u32[]{:S(2)}) collective-permute-start(bf16[32,2176]{1,0:T(8,128)(2,1)S(1)} %get-tuple-element.16.own), channel_id=1, source_target_pairs={{0,12},{4,0},{8,4},{12,8},{1,13},{5,1},{9,5},{13,9},{2,14},{6,2},{... | collective-permute-start | bytes 417800 | tf_op jit(solution)/shard_map/ppermute | solution.py:29
  43.4 14.7 %collective-permute-done.2.b1 = bf16[32,2176]{1,0:T(8,128)(2,1)S(1)} collective-permute-done((bf16[32,2176]{1,0:T(8,128)(2,1)S(1)}, bf16[32,2176]{1,0:T(8,128)(2,1)S(1)}, u32[]{:S(2)}, u32[]{:S(2)}) %collective-permute-start.2) | collective-permute-done | bytes 139296 | tf_op jit(solution)/shard_map/ppermute | solution.py:29
  59.1 8.2 %collective-permute-start.6 = (bf16[2,2,1024,256]{3,2,1,0:T(8,128)(2,1)S(1)}, bf16[2,2,1024,256]{3,2,1,0:T(8,128)(2,1)S(1)}, u32[]{:S(2)}, u32[]{:S(2)}) collective-permute-start(bf16[2,2,1024,256]{3,2,1,0:T(8,128)(2,1)S(1)} %get-tuple-element.19.near_a), channel_id=1, source_target_pairs={{0,64},{64,0},{1,65},{65,1},{2,66},{66,2},{3,67},{67,3},{4,68},{68... | collective-permute-start | bytes 6291464 | tf_op jit(solution)/shard_map/ppermute | solution.py:29
  67.3 3.3 %collective-permute-start.7 = (bf16[2,1024,256]{2,1,0:T(8,128)(2,1)S(1)}, bf16[2,1024,256]{2,1,0:T(8,128)(2,1)S(1)}, u32[]{:S(2)}, u32[]{:S(2)}) collective-permute-start(bf16[2,1024,256]{2,1,0:T(8,128)(2,1)S(1)} %get-tuple-element.20), channel_id=1, source_target_pairs={{0,15},{1,0},{2,1},{3,2},{4,3},{5,4},{6,5},{7,6},{8,7},{9,8},{10,9... | collective-permute-start | bytes 3145736 | tf_op jit(solution)/shard_map/ppermute | solution.py:305
  70.6 2.2 %collective-permute-start.8 = (bf16[2,1024,256]{2,1,0:T(8,128)(2,1)S(1)}, bf16[2,1024,256]{2,1,0:T(8,128)(2,1)S(1)}, u32[]{:S(2)}, u32[]{:S(2)}) collective-permute-start(bf16[2,1024,256]{2,1,0:T(8,128)(2,1)S(1)} %get-tuple-element.20), channel_id=1, source_target_pairs={{0,79},{1,64},{2,65},{3,66},{4,67},{5,68},{6,69},{7,70},{8,71},{9,... | collective-permute-start | bytes 3145736 | tf_op jit(solution)/shard_map/ppermute | solution.py:307
  72.8 19.4 %all_to_all.37 = bf16[4,80,2048]{2,1,0:T(8,128)(2,1)S(1)} all-to-all(bf16[4,80,2048]{2,1,0:T(8,128)(2,1)S(1)} %bitcast.33), channel_id=1, replica_groups=mesh['y'=4,'core'=2,'x'=4,'z4'=4,'zl'=4] {'x'}, dimensions={0} | all-to-all | bytes 2621440 | tf_op jit(solution)/shard_map/all_to_all | solution.py:309
  92.2 2.7 %collective-permute-done.8.far_b = bf16[2,1024,256]{2,1,0:T(8,128)(2,1)S(1)} collective-permute-done((bf16[2,1024,256]{2,1,0:T(8,128)(2,1)S(1)}, bf16[2,1024,256]{2,1,0:T(8,128)(2,1)S(1)}, u32[]{:S(2)}, u32[]{:S(2)}) %collective-permute-start.8) | collective-permute-done | bytes 1048608 | tf_op jit(solution)/shard_map/ppermute | solution.py:307
  94.8 2.9 %shard_map.135 = bf16[320,2048]{1,0:T(8,128)(2,1)S(1)} custom-call(bf16[320,2048]{1,0:T(8,128)(2,1)S(1)} %bitcast.30, bf16[2,2,1024,256]{3,2,1,0:T(8,128)(2,1)S(1)} %copy-done, bf16[2,2,1024,256]{3,2,1,0:T(8,128)(2,1)S(1)} %get-tuple-element.19.near_a, bf16[2,2,1024,256]{3,2,1,0:T(8,128)(2,1)S(1)} %collective-permute-done.6.near_b, ...), custom_call_target="tpu_custom_call" | custom-call | flops 2684354560 | bytes 11534336 | tf_op jit(solution)/shard_map/pallas_call | solution.py:310
  97.7 20.0 %all_to_all.38 = bf16[4,80,2048]{2,1,0:T(8,128)(2,1)S(1)} all-to-all(bf16[4,80,2048]{2,1,0:T(8,128)(2,1)S(1)} %bitcast.31), channel_id=1, replica_groups=mesh['y'=4,'core'=2,'x'=4,'z4'=4,'zl'=4] {'x'}, dimensions={0} | all-to-all | bytes 2621440 | tf_op jit(solution)/shard_map/all_to_all | solution.py:323
  117.7 1.3 shard_map.136
  119.1 11.2 %collective-permute-start.9 = (bf16[32,2048]{1,0:T(8,128)(2,1)}, bf16[32,2048]{1,0:T(8,128)(2,1)S(1)}, u32[]{:S(2)}, u32[]{:S(2)}) collective-permute-start(bf16[32,2048]{1,0:T(8,128)(2,1)} %get-tuple-element.23), channel_id=1, source_target_pairs={{0,8},{4,12},{8,0},{12,4},{1,9},{5,13},{9,1},{13,5},{2,10},{6,14},... | collective-permute-start | bytes 393224 | tf_op jit(solution)/shard_map/ppermute | solution.py:29
  130.3 1.9 collective-permute-start.10
  132.2 7.3 %collective-permute-start.11 = (bf16[32,2048]{1,0:T(8,128)(2,1)S(1)}, bf16[32,2048]{1,0:T(8,128)(2,1)S(1)}, u32[]{:S(2)}, u32[]{:S(2)}) collective-permute-start(bf16[32,2048]{1,0:T(8,128)(2,1)S(1)} %get-tuple-element.25), channel_id=1, source_target_pairs={{0,4},{4,8},{8,12},{12,0},{1,5},{5,9},{9,13},{13,1},{2,6},{6,10},{... | collective-permute-start | bytes 393224 | tf_op jit(solution)/shard_map/ppermute | solution.py:29
  139.6 2.2 %collective-permute-done.10.p2 = bf16[32,2048]{1,0:T(8,128)(2,1)S(1)} collective-permute-done((bf16[32,2048]{1,0:T(8,128)(2,1)S(1)}, bf16[32,2048]{1,0:T(8,128)(2,1)S(1)}, u32[]{:S(2)}, u32[]{:S(2)}) %collective-permute-start.10) | collective-permute-done | bytes 131104 | tf_op jit(solution)/shard_map/ppermute | solution.py:29
  141.8 4.6 %collective-permute-done.11.p3 = bf16[32,2048]{1,0:T(8,128)(2,1)S(1)} collective-permute-done((bf16[32,2048]{1,0:T(8,128)(2,1)S(1)}, bf16[32,2048]{1,0:T(8,128)(2,1)S(1)}, u32[]{:S(2)}, u32[]{:S(2)}) %collective-permute-start.11) | collective-permute-done | bytes 131104 | tf_op jit(solution)/shard_map/ppermute | solution.py:29
  146.3 1.7 shard_map.137
  148.0 18.9 %all_to_all.39 = f32[16,1,128]{2,1,0:T(1,128)S(1)} all-to-all(f32[16,1,128]{2,1,0:T(1,128)S(1)} %bitcast.38), channel_id=1, replica_groups=mesh['y'=4,'core'=2,'x'=4,'z4'=4,'zl'=4] {'x','zl'}, dimensions={0} | all-to-all | bytes 16384 | tf_op jit(solution)/shard_map/all_to_all | solution.py:343
  167.0 26.8 %all_to_all.40 = f32[32,1,128]{2,1,0:T(1,128)S(1)} all-to-all(f32[32,1,128]{2,1,0:T(1,128)S(1)} %broadcast_in_dim.14), channel_id=1, replica_groups=mesh['y'=4,'core'=2,'x'=4,'z4'=4,'zl'=4] {'y','core','z4'}, dimensions={0} | all-to-all | bytes 32768 | tf_op jit(solution)/shard_map/all_to_all | solution.py:345
  (39 shorter events, 4.2 us)
Async XLA Ops:
  0.6 12.9 %copy-start.8 = (bf16[1,32,2048]{2,1,0:T(8,128)(2,1)S(1)}, bf16[1,32,2048]{2,1,0:T(8,128)(2,1)}, u32[]{:S(2)}) copy-start(bf16[1,32,2048]{2,1,0:T(8,128)(2,1)} %param.13) | copy-start | bytes 393220
  0.6 14.2 %copy-start.5 = (bf16[1,2048,4]{1,2,0:T(4,128)(2,1)S(1)}, bf16[1,2048,4]{1,2,0:T(4,128)(2,1)}, u32[]{:S(2)}) copy-start(bf16[1,2048,4]{1,2,0:T(4,128)(2,1)} %param.18) | copy-start | bytes 49156
  0.7 14.9 %copy-start.4 = (f32[1,3,2048]{2,0,1:T(1,128)S(1)}, f32[1,3,2048]{2,0,1:T(1,128)}, u32[]{:S(2)}) copy-start(f32[1,3,2048]{2,0,1:T(1,128)} %param.17) | copy-start | bytes 73732
  0.7 14.9 %copy-start.6 = (s32[1,32,2]{1,2,0:T(2,128)S(1)}, s32[1,32,2]{1,2,0:T(2,128)}, u32[]{:S(2)}) copy-start(s32[1,32,2]{1,2,0:T(2,128)} %param.16) | copy-start | bytes 772
  0.7 16.1 %copy-start.2 = (bf16[1,32,2048]{2,1,0:T(8,128)(2,1)S(1)}, bf16[1,32,2048]{2,1,0:T(8,128)(2,1)}, u32[]{:S(2)}) copy-start(bf16[1,32,2048]{2,1,0:T(8,128)(2,1)} %param.12) | copy-start | bytes 393220
  3.7 55.2 %collective-permute-start.5 = (bf16[2,2,1024,256]{3,2,1,0:T(8,128)(2,1)}, bf16[2,2,1024,256]{3,2,1,0:T(8,128)(2,1)S(1)}, u32[]{:S(2)}, u32[]{:S(2)}) collective-permute-start(bf16[2,2,1024,256]{3,2,1,0:T(8,128)(2,1)} %shard_map.133.own), channel_id=1, source_target_pairs={{0,15},{1,0},{2,1},{3,2},{4,3},{5,4},{6,5},{7,6},{8,7},{9,8},{10,9... | collective-permute-start | bytes 6291464 | tf_op jit(solution)/shard_map/ppermute | solution.py:279
  8.1 7.6 %collective-permute-start = (s32[1]{0:T(128)}, s32[1]{0:T(128)}, u32[]{:S(2)}, u32[]{:S(2)}) collective-permute-start(s32[1]{0:T(128)} %bitcast.1), channel_id=1, source_target_pairs={{0,256},{128,384},{1,257},{129,385},{2,258},{130,386},{3,259},{131... | collective-permute-start | bytes 20 | tf_op jit(solution)/shard_map/ppermute | solution.py:24
  13.5 3.2 %collective-permute-start.1 = (bf16[32,2048]{1,0:T(8,128)(2,1)S(1)}, bf16[32,2048]{1,0:T(8,128)(2,1)S(1)}, u32[]{:S(2)}, u32[]{:S(2)}) collective-permute-start(bf16[32,2048]{1,0:T(8,128)(2,1)S(1)} %bitcast.45), channel_id=1, source_target_pairs={{0,256},{128,384},{1,257},{129,385},{2,258},{130,386},{3,259},{131... | collective-permute-start | bytes 393224 | tf_op jit(solution)/shard_map/ppermute | solution.py:24
  18.7 39.4 %collective-permute-start.2 = (bf16[32,2176]{1,0:T(8,128)(2,1)S(1)}, bf16[32,2176]{1,0:T(8,128)(2,1)S(1)}, u32[]{:S(2)}, u32[]{:S(2)}) collective-permute-start(bf16[32,2176]{1,0:T(8,128)(2,1)S(1)} %get-tuple-element.16.own), channel_id=1, source_target_pairs={{0,8},{4,12},{8,0},{12,4},{1,9},{5,13},{9,1},{13,5},{2,10},{6,14},... | collective-permute-start | bytes 417800 | tf_op jit(solution)/shard_map/ppermute | solution.py:29
  34.2 23.9 %collective-permute-start.3 = (bf16[32,2176]{1,0:T(8,128)(2,1)S(1)}, bf16[32,2176]{1,0:T(8,128)(2,1)S(1)}, u32[]{:S(2)}, u32[]{:S(2)}) collective-permute-start(bf16[32,2176]{1,0:T(8,128)(2,1)S(1)} %get-tuple-element.16.own), channel_id=1, source_target_pairs={{0,4},{4,8},{8,12},{12,0},{1,5},{5,9},{9,13},{13,1},{2,6},{6,10},{... | collective-permute-start | bytes 417800 | tf_op jit(solution)/shard_map/ppermute | solution.py:29
  37.3 20.8 %collective-permute-start.4 = (bf16[32,2176]{1,0:T(8,128)(2,1)S(1)}, bf16[32,2176]{1,0:T(8,128)(2,1)S(1)}, u32[]{:S(2)}, u32[]{:S(2)}) collective-permute-start(bf16[32,2176]{1,0:T(8,128)(2,1)S(1)} %get-tuple-element.16.own), channel_id=1, source_target_pairs={{0,12},{4,0},{8,4},{12,8},{1,13},{5,1},{9,5},{13,9},{2,14},{6,2},{... | collective-permute-start | bytes 417800 | tf_op jit(solution)/shard_map/ppermute | solution.py:29
  59.0 35.9 %copy-start = (bf16[2,2,1024,256]{3,2,1,0:T(8,128)(2,1)S(1)}, bf16[2,2,1024,256]{3,2,1,0:T(8,128)(2,1)}, u32[]{:S(2)}) copy-start(bf16[2,2,1024,256]{3,2,1,0:T(8,128)(2,1)} %shard_map.133.own) | copy-start | bytes 6291460
  59.1 35.8 %collective-permute-start.6 = (bf16[2,2,1024,256]{3,2,1,0:T(8,128)(2,1)S(1)}, bf16[2,2,1024,256]{3,2,1,0:T(8,128)(2,1)S(1)}, u32[]{:S(2)}, u32[]{:S(2)}) collective-permute-start(bf16[2,2,1024,256]{3,2,1,0:T(8,128)(2,1)S(1)} %get-tuple-element.19.near_a), channel_id=1, source_target_pairs={{0,64},{64,0},{1,65},{65,1},{2,66},{66,2},{3,67},{67,3},{4,68},{68... | collective-permute-start | bytes 6291464 | tf_op jit(solution)/shard_map/ppermute | solution.py:29
  67.3 24.9 %collective-permute-start.7 = (bf16[2,1024,256]{2,1,0:T(8,128)(2,1)S(1)}, bf16[2,1024,256]{2,1,0:T(8,128)(2,1)S(1)}, u32[]{:S(2)}, u32[]{:S(2)}) collective-permute-start(bf16[2,1024,256]{2,1,0:T(8,128)(2,1)S(1)} %get-tuple-element.20), channel_id=1, source_target_pairs={{0,15},{1,0},{2,1},{3,2},{4,3},{5,4},{6,5},{7,6},{8,7},{9,8},{10,9... | collective-permute-start | bytes 3145736 | tf_op jit(solution)/shard_map/ppermute | solution.py:305
  70.6 24.3 %collective-permute-start.8 = (bf16[2,1024,256]{2,1,0:T(8,128)(2,1)S(1)}, bf16[2,1024,256]{2,1,0:T(8,128)(2,1)S(1)}, u32[]{:S(2)}, u32[]{:S(2)}) collective-permute-start(bf16[2,1024,256]{2,1,0:T(8,128)(2,1)S(1)} %get-tuple-element.20), channel_id=1, source_target_pairs={{0,79},{1,64},{2,65},{3,66},{4,67},{5,68},{6,69},{7,70},{8,71},{9,... | collective-permute-start | bytes 3145736 | tf_op jit(solution)/shard_map/ppermute | solution.py:307
  97.7 41.8 %copy-start.7 = (s32[1,32]{1,0:T(1,128)S(1)}, s32[1,32]{1,0:T(1,128)}, u32[]{:S(2)}) copy-start(s32[1,32]{1,0:T(1,128)} %param.23) | copy-start | bytes 388
  97.7 48.6 %copy-start.1 = (bf16[1,2048,512]{2,1,0:T(8,128)(2,1)S(1)}, bf16[1,2048,512]{2,1,0:T(8,128)(2,1)}, u32[]{:S(2)}) copy-start(bf16[1,2048,512]{2,1,0:T(8,128)(2,1)} %param.21) | copy-start | bytes 6291460
  97.7 48.6 %copy-start.3 = (f32[1,32,512]{2,1,0:T(8,128)S(1)}, f32[1,32,512]{2,1,0:T(8,128)}, u32[]{:S(2)}) copy-start(f32[1,32,512]{2,1,0:T(8,128)} %param.22) | copy-start | bytes 196612
  119.1 20.5 %collective-permute-start.9 = (bf16[32,2048]{1,0:T(8,128)(2,1)}, bf16[32,2048]{1,0:T(8,128)(2,1)S(1)}, u32[]{:S(2)}, u32[]{:S(2)}) collective-permute-start(bf16[32,2048]{1,0:T(8,128)(2,1)} %get-tuple-element.23), channel_id=1, source_target_pairs={{0,8},{4,12},{8,0},{12,4},{1,9},{5,13},{9,1},{13,5},{2,10},{6,14},... | collective-permute-start | bytes 393224 | tf_op jit(solution)/shard_map/ppermute | solution.py:29
  130.3 11.5 %collective-permute-start.10 = (bf16[32,2048]{1,0:T(8,128)(2,1)S(1)}, bf16[32,2048]{1,0:T(8,128)(2,1)S(1)}, u32[]{:S(2)}, u32[]{:S(2)}) collective-permute-start(bf16[32,2048]{1,0:T(8,128)(2,1)S(1)} %get-tuple-element.24), channel_id=1, source_target_pairs={{0,12},{4,0},{8,4},{12,8},{1,13},{5,1},{9,5},{13,9},{2,14},{6,2},{... | collective-permute-start | bytes 393224 | tf_op jit(solution)/shard_map/ppermute | solution.py:29
  132.2 14.1 %collective-permute-start.11 = (bf16[32,2048]{1,0:T(8,128)(2,1)S(1)}, bf16[32,2048]{1,0:T(8,128)(2,1)S(1)}, u32[]{:S(2)}, u32[]{:S(2)}) collective-permute-start(bf16[32,2048]{1,0:T(8,128)(2,1)S(1)} %get-tuple-element.25), channel_id=1, source_target_pairs={{0,4},{4,8},{8,12},{12,0},{1,5},{5,9},{9,13},{13,1},{2,6},{6,10},{... | collective-permute-start | bytes 393224 | tf_op jit(solution)/shard_map/ppermute | solution.py:29

commit v11 on v10

--- a/solution.py
+++ b/solution.py
@@ -329,7 +329,7 @@
         (4 * lanes * 4 * tok_rows * model_width, 2 << 20),
     )(returned, gates_high, gates_low)
     home = [turned(part, "z4", -k) for k, part in zip(order, parts)]
-    local_axes, far_axes = ("x", "zl"), ("y", "core", "z4")
+    local_axes, far_axes = ("core", "x", "zl"), ("y", "z4")
     members = [math.prod(lax.axis_size(a) for a in axes) for axes in (local_axes, far_axes)]
     layer_out, totals = kernel_call(
         after_body,

time: 197 us -> 196 us (level)
    all_to_all x1, blocking collectives: 26.8 us -> 24 us  [local(): lax.all_to_all(totals, far_axes, split_axis=0, concat_axis=0, tiled=True)]
where the time goes in v11:
time: 196 us; the launch traced here: 195 us
  blocking collectives  83.6 us (43%)
  starting transfers between devices  69.8 us (36%)
  waiting for transfers between devices  24.5 us (12%)
  Pallas kernels  11.8 us (6%)
  between operations  4.01 us (2%)
    ppermute x7, starting transfers between devices, turned(): lax.ppermute(block, axis, [(i, (i + distance) % count) for i in range(cou...  53.2 us
    all_to_all x1, blocking collectives, local(): lax.all_to_all(totals, far_axes, split_axis=0, concat_axis=0, tiled=True)  24 us
    ppermute x7, waiting for transfers between devices, turned(): lax.ppermute(block, axis, [(i, (i + distance) % count) for i in range(cou...  21.5 us
    all_to_all x1, blocking collectives, local(): lax.all_to_all(totals, local_axes, split_axis=0, concat_axis=0, tiled=True)  20.3 us
    all_to_all x1, blocking collectives, local(): lax.all_to_all(partial_out, 'x', split_axis=0, concat_axis=0, tiled=True)  20 us
    all_to_all x1, blocking collectives, local(): rows = lax.all_to_all(packed, 'x', split_axis=0, concat_axis=0, tiled=True)  19.4 us
    ppermute x2, starting transfers between devices, passed_along(): return lax.ppermute(block, axis, route)  6.68 us
    ppermute x1, starting transfers between devices, local(): near_mine = lax.ppermute(shared, ('core', 'z4', 'zl'), onward)  4.37 us
  transfers between devices with their start and end apart: 12, of which 5 were waited for; matrix products, arithmetic and copies ran while one was open for 0% of the time, Pallas kernels for 1%

profile of v11, /device:TPU:1, one launch (start us, length us, event | category | flops | bytes accessed | tf_op | source)
XLA Modules:
  0.0 195.4 jit_solution(4028979597024247217)
XLA Ops:
  0.7 3.0 %shard_map.133.own = bf16[2,2,1024,256]{3,2,1,0:T(8,128)(2,1)} custom-call(bf16[2048,256]{1,0:T(8,128)(2,1)} %bitcast.39, bf16[256,2048]{1,0:T(8,128)(2,1)} %bitcast.40), custom_call_target="tpu_custom_call" | custom-call | bytes 4194304 | tf_op jit(solution)/shard_map/pallas_call | solution.py:250
  3.7 4.4 %collective-permute-start.5 = (bf16[2,2,1024,256]{3,2,1,0:T(8,128)(2,1)}, bf16[2,2,1024,256]{3,2,1,0:T(8,128)(2,1)S(1)}, u32[]{:S(2)}, u32[]{:S(2)}) collective-permute-start(bf16[2,2,1024,256]{3,2,1,0:T(8,128)(2,1)} %shard_map.133.own), channel_id=1, source_target_pairs={{0,15},{1,0},{2,1},{3,2},{4,3},{5,4},{6,5},{7,6},{8,7},{9,8},{10,9... | collective-permute-start | bytes 6291464 | tf_op jit(solution)/shard_map/ppermute | solution.py:279
  8.1 5.4 %collective-permute-start = (s32[1]{0:T(128)}, s32[1]{0:T(128)}, u32[]{:S(2)}, u32[]{:S(2)}) collective-permute-start(s32[1]{0:T(128)} %bitcast.1), channel_id=1, source_target_pairs={{0,256},{128,384},{1,257},{129,385},{2,258},{130,386},{3,259},{131... | collective-permute-start | bytes 20 | tf_op jit(solution)/shard_map/ppermute | solution.py:24
  16.7 2.0 shard_map.131
  18.7 15.5 %collective-permute-start.2 = (bf16[32,2176]{1,0:T(8,128)(2,1)S(1)}, bf16[32,2176]{1,0:T(8,128)(2,1)S(1)}, u32[]{:S(2)}, u32[]{:S(2)}) collective-permute-start(bf16[32,2176]{1,0:T(8,128)(2,1)S(1)} %get-tuple-element.16.own), channel_id=1, source_target_pairs={{0,8},{4,12},{8,0},{12,4},{1,9},{5,13},{9,1},{13,5},{2,10},{6,14},... | collective-permute-start | bytes 417800 | tf_op jit(solution)/shard_map/ppermute | solution.py:29
  34.2 3.1 %collective-permute-start.3 = (bf16[32,2176]{1,0:T(8,128)(2,1)S(1)}, bf16[32,2176]{1,0:T(8,128)(2,1)S(1)}, u32[]{:S(2)}, u32[]{:S(2)}) collective-permute-start(bf16[32,2176]{1,0:T(8,128)(2,1)S(1)} %get-tuple-element.16.own), channel_id=1, source_target_pairs={{0,4},{4,8},{8,12},{12,0},{1,5},{5,9},{9,13},{13,1},{2,6},{6,10},{... | collective-permute-start | bytes 417800 | tf_op jit(solution)/shard_map/ppermute | solution.py:29
  37.3 6.1 %collective-permute-start.4 = (bf16[32,2176]{1,0:T(8,128)(2,1)S(1)}, bf16[32,2176]{1,0:T(8,128)(2,1)S(1)}, u32[]{:S(2)}, u32[]{:S(2)}) collective-permute-start(bf16[32,2176]{1,0:T(8,128)(2,1)S(1)} %get-tuple-element.16.own), channel_id=1, source_target_pairs={{0,12},{4,0},{8,4},{12,8},{1,13},{5,1},{9,5},{13,9},{2,14},{6,2},{... | collective-permute-start | bytes 417800 | tf_op jit(solution)/shard_map/ppermute | solution.py:29
  43.4 14.7 %collective-permute-done.2.b1 = bf16[32,2176]{1,0:T(8,128)(2,1)S(1)} collective-permute-done((bf16[32,2176]{1,0:T(8,128)(2,1)S(1)}, bf16[32,2176]{1,0:T(8,128)(2,1)S(1)}, u32[]{:S(2)}, u32[]{:S(2)}) %collective-permute-start.2) | collective-permute-done | bytes 139296 | tf_op jit(solution)/shard_map/ppermute | solution.py:29
  59.1 8.2 %collective-permute-start.6 = (bf16[2,2,1024,256]{3,2,1,0:T(8,128)(2,1)S(1)}, bf16[2,2,1024,256]{3,2,1,0:T(8,128)(2,1)S(1)}, u32[]{:S(2)}, u32[]{:S(2)}) collective-permute-start(bf16[2,2,1024,256]{3,2,1,0:T(8,128)(2,1)S(1)} %get-tuple-element.19.near_a), channel_id=1, source_target_pairs={{0,64},{64,0},{1,65},{65,1},{2,66},{66,2},{3,67},{67,3},{4,68},{68... | collective-permute-start | bytes 6291464 | tf_op jit(solution)/shard_map/ppermute | solution.py:29
  67.3 3.3 %collective-permute-start.7 = (bf16[2,1024,256]{2,1,0:T(8,128)(2,1)S(1)}, bf16[2,1024,256]{2,1,0:T(8,128)(2,1)S(1)}, u32[]{:S(2)}, u32[]{:S(2)}) collective-permute-start(bf16[2,1024,256]{2,1,0:T(8,128)(2,1)S(1)} %get-tuple-element.20), channel_id=1, source_target_pairs={{0,15},{1,0},{2,1},{3,2},{4,3},{5,4},{6,5},{7,6},{8,7},{9,8},{10,9... | collective-permute-start | bytes 3145736 | tf_op jit(solution)/shard_map/ppermute | solution.py:305
  70.6 2.2 %collective-permute-start.8 = (bf16[2,1024,256]{2,1,0:T(8,128)(2,1)S(1)}, bf16[2,1024,256]{2,1,0:T(8,128)(2,1)S(1)}, u32[]{:S(2)}, u32[]{:S(2)}) collective-permute-start(bf16[2,1024,256]{2,1,0:T(8,128)(2,1)S(1)} %get-tuple-element.20), channel_id=1, source_target_pairs={{0,79},{1,64},{2,65},{3,66},{4,67},{5,68},{6,69},{7,70},{8,71},{9,... | collective-permute-start | bytes 3145736 | tf_op jit(solution)/shard_map/ppermute | solution.py:307
  72.8 19.4 %all_to_all.37 = bf16[4,80,2048]{2,1,0:T(8,128)(2,1)S(1)} all-to-all(bf16[4,80,2048]{2,1,0:T(8,128)(2,1)S(1)} %bitcast.33), channel_id=1, replica_groups=mesh['y'=4,'core'=2,'x'=4,'z4'=4,'zl'=4] {'x'}, dimensions={0} | all-to-all | bytes 2621440 | tf_op jit(solution)/shard_map/all_to_all | solution.py:309
  92.2 2.7 %collective-permute-done.8.far_b = bf16[2,1024,256]{2,1,0:T(8,128)(2,1)S(1)} collective-permute-done((bf16[2,1024,256]{2,1,0:T(8,128)(2,1)S(1)}, bf16[2,1024,256]{2,1,0:T(8,128)(2,1)S(1)}, u32[]{:S(2)}, u32[]{:S(2)}) %collective-permute-start.8) | collective-permute-done | bytes 1048608 | tf_op jit(solution)/shard_map/ppermute | solution.py:307
  94.8 2.9 %shard_map.135 = bf16[320,2048]{1,0:T(8,128)(2,1)S(1)} custom-call(bf16[320,2048]{1,0:T(8,128)(2,1)S(1)} %bitcast.30, bf16[2,2,1024,256]{3,2,1,0:T(8,128)(2,1)S(1)} %copy-done, bf16[2,2,1024,256]{3,2,1,0:T(8,128)(2,1)S(1)} %get-tuple-element.19.near_a, bf16[2,2,1024,256]{3,2,1,0:T(8,128)(2,1)S(1)} %collective-permute-done.6.near_b, ...), custom_call_target="tpu_custom_call" | custom-call | flops 2684354560 | bytes 11534336 | tf_op jit(solution)/shard_map/pallas_call | solution.py:310
  97.7 20.0 %all_to_all.38 = bf16[4,80,2048]{2,1,0:T(8,128)(2,1)S(1)} all-to-all(bf16[4,80,2048]{2,1,0:T(8,128)(2,1)S(1)} %bitcast.31), channel_id=1, replica_groups=mesh['y'=4,'core'=2,'x'=4,'z4'=4,'zl'=4] {'x'}, dimensions={0} | all-to-all | bytes 2621440 | tf_op jit(solution)/shard_map/all_to_all | solution.py:323
  117.7 1.3 shard_map.136
  119.1 11.2 %collective-permute-start.9 = (bf16[32,2048]{1,0:T(8,128)(2,1)}, bf16[32,2048]{1,0:T(8,128)(2,1)S(1)}, u32[]{:S(2)}, u32[]{:S(2)}) collective-permute-start(bf16[32,2048]{1,0:T(8,128)(2,1)} %get-tuple-element.23), channel_id=1, source_target_pairs={{0,8},{4,12},{8,0},{12,4},{1,9},{5,13},{9,1},{13,5},{2,10},{6,14},... | collective-permute-start | bytes 393224 | tf_op jit(solution)/shard_map/ppermute | solution.py:29
  130.3 1.9 collective-permute-start.10
  132.2 7.3 %collective-permute-start.11 = (bf16[32,2048]{1,0:T(8,128)(2,1)S(1)}, bf16[32,2048]{1,0:T(8,128)(2,1)S(1)}, u32[]{:S(2)}, u32[]{:S(2)}) collective-permute-start(bf16[32,2048]{1,0:T(8,128)(2,1)S(1)} %get-tuple-element.25), channel_id=1, source_target_pairs={{0,4},{4,8},{8,12},{12,0},{1,5},{5,9},{9,13},{13,1},{2,6},{6,10},{... | collective-permute-start | bytes 393224 | tf_op jit(solution)/shard_map/ppermute | solution.py:29
  139.6 2.2 %collective-permute-done.10.p2 = bf16[32,2048]{1,0:T(8,128)(2,1)S(1)} collective-permute-done((bf16[32,2048]{1,0:T(8,128)(2,1)S(1)}, bf16[32,2048]{1,0:T(8,128)(2,1)S(1)}, u32[]{:S(2)}, u32[]{:S(2)}) %collective-permute-start.10) | collective-permute-done | bytes 131104 | tf_op jit(solution)/shard_map/ppermute | solution.py:29
  141.8 4.6 %collective-permute-done.11.p3 = bf16[32,2048]{1,0:T(8,128)(2,1)S(1)} collective-permute-done((bf16[32,2048]{1,0:T(8,128)(2,1)S(1)}, bf16[32,2048]{1,0:T(8,128)(2,1)S(1)}, u32[]{:S(2)}, u32[]{:S(2)}) %collective-permute-start.11) | collective-permute-done | bytes 131104 | tf_op jit(solution)/shard_map/ppermute | solution.py:29
  146.3 1.7 shard_map.137
  148.0 20.3 %all_to_all.39 = f32[32,1,128]{2,1,0:T(1,128)S(1)} all-to-all(f32[32,1,128]{2,1,0:T(1,128)S(1)} %bitcast.38), channel_id=1, replica_groups=mesh['y'=4,'core'=2,'x'=4,'z4'=4,'zl'=4] {'core','x','zl'}, dimensions={0} | all-to-all | bytes 32768 | tf_op jit(solution)/shard_map/all_to_all | solution.py:343
  168.4 24.0 %all_to_all.40 = f32[16,1,128]{2,1,0:T(1,128)S(1)} all-to-all(f32[16,1,128]{2,1,0:T(1,128)S(1)} %broadcast_in_dim.14), channel_id=1, replica_groups=mesh['y'=4,'core'=2,'x'=4,'z4'=4,'zl'=4] {'y','z4'}, dimensions={0} | all-to-all | bytes 16384 | tf_op jit(solution)/shard_map/all_to_all | solution.py:345
  (39 shorter events, 4.2 us)
Async XLA Ops:
  0.6 12.9 %copy-start.8 = (bf16[1,32,2048]{2,1,0:T(8,128)(2,1)S(1)}, bf16[1,32,2048]{2,1,0:T(8,128)(2,1)}, u32[]{:S(2)}) copy-start(bf16[1,32,2048]{2,1,0:T(8,128)(2,1)} %param.13) | copy-start | bytes 393220
  0.6 14.2 %copy-start.5 = (bf16[1,2048,4]{1,2,0:T(4,128)(2,1)S(1)}, bf16[1,2048,4]{1,2,0:T(4,128)(2,1)}, u32[]{:S(2)}) copy-start(bf16[1,2048,4]{1,2,0:T(4,128)(2,1)} %param.18) | copy-start | bytes 49156
  0.7 14.9 %copy-start.4 = (f32[1,3,2048]{2,0,1:T(1,128)S(1)}, f32[1,3,2048]{2,0,1:T(1,128)}, u32[]{:S(2)}) copy-start(f32[1,3,2048]{2,0,1:T(1,128)} %param.17) | copy-start | bytes 73732
  0.7 14.9 %copy-start.6 = (s32[1,32,2]{1,2,0:T(2,128)S(1)}, s32[1,32,2]{1,2,0:T(2,128)}, u32[]{:S(2)}) copy-start(s32[1,32,2]{1,2,0:T(2,128)} %param.16) | copy-start | bytes 772
  0.7 16.1 %copy-start.2 = (bf16[1,32,2048]{2,1,0:T(8,128)(2,1)S(1)}, bf16[1,32,2048]{2,1,0:T(8,128)(2,1)}, u32[]{:S(2)}) copy-start(bf16[1,32,2048]{2,1,0:T(8,128)(2,1)} %param.12) | copy-start | bytes 393220
  3.7 55.2 %collective-permute-start.5 = (bf16[2,2,1024,256]{3,2,1,0:T(8,128)(2,1)}, bf16[2,2,1024,256]{3,2,1,0:T(8,128)(2,1)S(1)}, u32[]{:S(2)}, u32[]{:S(2)}) collective-permute-start(bf16[2,2,1024,256]{3,2,1,0:T(8,128)(2,1)} %shard_map.133.own), channel_id=1, source_target_pairs={{0,15},{1,0},{2,1},{3,2},{4,3},{5,4},{6,5},{7,6},{8,7},{9,8},{10,9... | collective-permute-start | bytes 6291464 | tf_op jit(solution)/shard_map/ppermute | solution.py:279
  8.1 7.6 %collective-permute-start = (s32[1]{0:T(128)}, s32[1]{0:T(128)}, u32[]{:S(2)}, u32[]{:S(2)}) collective-permute-start(s32[1]{0:T(128)} %bitcast.1), channel_id=1, source_target_pairs={{0,256},{128,384},{1,257},{129,385},{2,258},{130,386},{3,259},{131... | collective-permute-start | bytes 20 | tf_op jit(solution)/shard_map/ppermute | solution.py:24
  13.5 3.2 %collective-permute-start.1 = (bf16[32,2048]{1,0:T(8,128)(2,1)S(1)}, bf16[32,2048]{1,0:T(8,128)(2,1)S(1)}, u32[]{:S(2)}, u32[]{:S(2)}) collective-permute-start(bf16[32,2048]{1,0:T(8,128)(2,1)S(1)} %bitcast.45), channel_id=1, source_target_pairs={{0,256},{128,384},{1,257},{129,385},{2,258},{130,386},{3,259},{131... | collective-permute-start | bytes 393224 | tf_op jit(solution)/shard_map/ppermute | solution.py:24
  18.7 39.4 %collective-permute-start.2 = (bf16[32,2176]{1,0:T(8,128)(2,1)S(1)}, bf16[32,2176]{1,0:T(8,128)(2,1)S(1)}, u32[]{:S(2)}, u32[]{:S(2)}) collective-permute-start(bf16[32,2176]{1,0:T(8,128)(2,1)S(1)} %get-tuple-element.16.own), channel_id=1, source_target_pairs={{0,8},{4,12},{8,0},{12,4},{1,9},{5,13},{9,1},{13,5},{2,10},{6,14},... | collective-permute-start | bytes 417800 | tf_op jit(solution)/shard_map/ppermute | solution.py:29
  34.2 23.9 %collective-permute-start.3 = (bf16[32,2176]{1,0:T(8,128)(2,1)S(1)}, bf16[32,2176]{1,0:T(8,128)(2,1)S(1)}, u32[]{:S(2)}, u32[]{:S(2)}) collective-permute-start(bf16[32,2176]{1,0:T(8,128)(2,1)S(1)} %get-tuple-element.16.own), channel_id=1, source_target_pairs={{0,4},{4,8},{8,12},{12,0},{1,5},{5,9},{9,13},{13,1},{2,6},{6,10},{... | collective-permute-start | bytes 417800 | tf_op jit(solution)/shard_map/ppermute | solution.py:29
  37.3 20.8 %collective-permute-start.4 = (bf16[32,2176]{1,0:T(8,128)(2,1)S(1)}, bf16[32,2176]{1,0:T(8,128)(2,1)S(1)}, u32[]{:S(2)}, u32[]{:S(2)}) collective-permute-start(bf16[32,2176]{1,0:T(8,128)(2,1)S(1)} %get-tuple-element.16.own), channel_id=1, source_target_pairs={{0,12},{4,0},{8,4},{12,8},{1,13},{5,1},{9,5},{13,9},{2,14},{6,2},{... | collective-permute-start | bytes 417800 | tf_op jit(solution)/shard_map/ppermute | solution.py:29
  59.0 35.9 %copy-start = (bf16[2,2,1024,256]{3,2,1,0:T(8,128)(2,1)S(1)}, bf16[2,2,1024,256]{3,2,1,0:T(8,128)(2,1)}, u32[]{:S(2)}) copy-start(bf16[2,2,1024,256]{3,2,1,0:T(8,128)(2,1)} %shard_map.133.own) | copy-start | bytes 6291460
  59.1 35.8 %collective-permute-start.6 = (bf16[2,2,1024,256]{3,2,1,0:T(8,128)(2,1)S(1)}, bf16[2,2,1024,256]{3,2,1,0:T(8,128)(2,1)S(1)}, u32[]{:S(2)}, u32[]{:S(2)}) collective-permute-start(bf16[2,2,1024,256]{3,2,1,0:T(8,128)(2,1)S(1)} %get-tuple-element.19.near_a), channel_id=1, source_target_pairs={{0,64},{64,0},{1,65},{65,1},{2,66},{66,2},{3,67},{67,3},{4,68},{68... | collective-permute-start | bytes 6291464 | tf_op jit(solution)/shard_map/ppermute | solution.py:29
  67.3 24.9 %collective-permute-start.7 = (bf16[2,1024,256]{2,1,0:T(8,128)(2,1)S(1)}, bf16[2,1024,256]{2,1,0:T(8,128)(2,1)S(1)}, u32[]{:S(2)}, u32[]{:S(2)}) collective-permute-start(bf16[2,1024,256]{2,1,0:T(8,128)(2,1)S(1)} %get-tuple-element.20), channel_id=1, source_target_pairs={{0,15},{1,0},{2,1},{3,2},{4,3},{5,4},{6,5},{7,6},{8,7},{9,8},{10,9... | collective-permute-start | bytes 3145736 | tf_op jit(solution)/shard_map/ppermute | solution.py:305
  70.6 24.3 %collective-permute-start.8 = (bf16[2,1024,256]{2,1,0:T(8,128)(2,1)S(1)}, bf16[2,1024,256]{2,1,0:T(8,128)(2,1)S(1)}, u32[]{:S(2)}, u32[]{:S(2)}) collective-permute-start(bf16[2,1024,256]{2,1,0:T(8,128)(2,1)S(1)} %get-tuple-element.20), channel_id=1, source_target_pairs={{0,79},{1,64},{2,65},{3,66},{4,67},{5,68},{6,69},{7,70},{8,71},{9,... | collective-permute-start | bytes 3145736 | tf_op jit(solution)/shard_map/ppermute | solution.py:307
  97.7 41.8 %copy-start.7 = (s32[1,32]{1,0:T(1,128)S(1)}, s32[1,32]{1,0:T(1,128)}, u32[]{:S(2)}) copy-start(s32[1,32]{1,0:T(1,128)} %param.23) | copy-start | bytes 388
  97.7 48.6 %copy-start.1 = (bf16[1,2048,512]{2,1,0:T(8,128)(2,1)S(1)}, bf16[1,2048,512]{2,1,0:T(8,128)(2,1)}, u32[]{:S(2)}) copy-start(bf16[1,2048,512]{2,1,0:T(8,128)(2,1)} %param.21) | copy-start | bytes 6291460
  97.7 48.6 %copy-start.3 = (f32[1,32,512]{2,1,0:T(8,128)S(1)}, f32[1,32,512]{2,1,0:T(8,128)}, u32[]{:S(2)}) copy-start(f32[1,32,512]{2,1,0:T(8,128)} %param.22) | copy-start | bytes 196612
  119.1 20.5 %collective-permute-start.9 = (bf16[32,2048]{1,0:T(8,128)(2,1)}, bf16[32,2048]{1,0:T(8,128)(2,1)S(1)}, u32[]{:S(2)}, u32[]{:S(2)}) collective-permute-start(bf16[32,2048]{1,0:T(8,128)(2,1)} %get-tuple-element.23), channel_id=1, source_target_pairs={{0,8},{4,12},{8,0},{12,4},{1,9},{5,13},{9,1},{13,5},{2,10},{6,14},... | collective-permute-start | bytes 393224 | tf_op jit(solution)/shard_map/ppermute | solution.py:29
  130.3 11.5 %collective-permute-start.10 = (bf16[32,2048]{1,0:T(8,128)(2,1)S(1)}, bf16[32,2048]{1,0:T(8,128)(2,1)S(1)}, u32[]{:S(2)}, u32[]{:S(2)}) collective-permute-start(bf16[32,2048]{1,0:T(8,128)(2,1)S(1)} %get-tuple-element.24), channel_id=1, source_target_pairs={{0,12},{4,0},{8,4},{12,8},{1,13},{5,1},{9,5},{13,9},{2,14},{6,2},{... | collective-permute-start | bytes 393224 | tf_op jit(solution)/shard_map/ppermute | solution.py:29
  132.2 14.1 %collective-permute-start.11 = (bf16[32,2048]{1,0:T(8,128)(2,1)S(1)}, bf16[32,2048]{1,0:T(8,128)(2,1)S(1)}, u32[]{:S(2)}, u32[]{:S(2)}) collective-permute-start(bf16[32,2048]{1,0:T(8,128)(2,1)S(1)} %get-tuple-element.25), channel_id=1, source_target_pairs={{0,4},{4,8},{8,12},{12,0},{1,5},{5,9},{9,13},{13,1},{2,6},{6,10},{... | collective-permute-start | bytes 393224 | tf_op jit(solution)/shard_map/ppermute | solution.py:29
